TPU v7x, 32 devices: a whole 2x2x4 slice. The times are simulated.
32 devices in a mesh: ta: 4 (over z), ha: 4 (over x, core), wa: 2 (over y).
Axes of the slice: x: 2, y: 2, z: 4, core: 2. Of those that a mesh axis runs over, the one named last changes fastest.
Arguments:
- features: bfloat16 [16, 64, 32, 256], P('ta', 'ha', 'wa'), may hold values from -6 to 6
- norm_gain: float32 [256], replicated, may hold values from 0.5 to 1.5
- conv_weight: bfloat16 [3, 3, 3, 256, 256], replicated, may hold values from -0.078125 to 0.078125
- cotangent: bfloat16 [16, 64, 32, 256], P('ta', 'ha', 'wa'), may hold values from -6 to 6
Outputs:
- decoded: bfloat16 [16, 64, 32, 256], P('ta', 'ha', 'wa')
- grad_features: bfloat16 [16, 64, 32, 256], P('ta', 'ha', 'wa')
- grad_weight: float32 [3, 3, 3, 256, 256], P(None, None, None, None, ('ha', 'wa'))
All inputs are finite; a program needn't handle non-finite values.
Results may differ from a plain program's by a relative error of at most 0.0032.
Values may be sent and summed in bfloat16 or wider, within the bound.
No kernel may reach another device: no remote copies, remote signals or barrier semaphores. Data moves between devices by JAX's collectives and lax.ppermute only.
A program may use at most 128 MiB of HBM per device.

v0:
```python
import jax
import jax.numpy as jnp
from jax import lax
from jax.sharding import PartitionSpec as P

EPSILON = 1e-06


def from_behind(array, axis, by):
    length = lax.axis_size(axis)
    pairs = [(i, i + by) for i in range(length) if 0 <= i + by < length]
    return lax.ppermute(array, axis, pairs)


def with_halo(cells, sides, width):
    for axis, dim in sides:
        count = lax.axis_size(axis)
        ends = count - 1
        head = lax.slice_in_dim(cells, 0, width, axis=dim)
        tail = lax.slice_in_dim(cells, cells.shape[dim] - width, cells.shape[dim], axis=dim)
        cells = jnp.concatenate(
            [
                lax.ppermute(tail, axis, [(i, (i + 1) % count) for i in range(ends)]),
                cells,
                lax.ppermute(head, axis, [((i + 1) % count, i) for i in range(ends)]),
            ],
            axis=dim,
        )
    return cells


def activate(features, norm_gain):
    values = features.astype(jnp.float32)
    inverse = lax.rsqrt(jnp.mean(values * values, axis=-1, keepdims=True) + EPSILON)
    unit_rms = values * inverse
    normed = unit_rms * norm_gain
    activated = (normed * jax.nn.sigmoid(normed)).astype(jnp.bfloat16)
    return (values, inverse, unit_rms, normed, activated)


def norm_backward(grad_act, normed, unit_rms, inverse, norm_gain):
    logistic = jax.nn.sigmoid(normed)
    grad_normed = grad_act * logistic * (1.0 + normed * (1.0 - logistic))
    grad_unit = grad_normed * norm_gain
    return inverse * (grad_unit - unit_rms * jnp.mean(grad_unit * unit_rms, axis=-1, keepdims=True))


def body(features, norm_gain, conv_weight, cotangent):
    frames, height, width, channels = features.shape
    values, inverse, unit_rms, normed, activated = activate(features, norm_gain)
    earlier = from_behind(activated[frames - 2 :], "ta", 1)
    padded = with_halo(jnp.concatenate([earlier, activated], 0), (("ha", 1), ("wa", 2)), 1)
    later = from_behind(cotangent[:2], "ta", -1)
    grad_padded = with_halo(jnp.concatenate([cotangent, later], 0), (("ha", 1), ("wa", 2)), 1)
    flat_grad = cotangent.reshape(-1, channels)
    mixed = jnp.zeros((frames * height * width, channels), jnp.float32)
    grad_act = jnp.zeros((frames * height * width, channels), jnp.float32)
    windows = []
    for t_off in range(3):
        for h_off in range(3):
            for w_off in range(3):
                window = padded[
                    t_off : t_off + frames, h_off : h_off + height, w_off : w_off + width
                ].reshape(-1, channels)
                windows.append(window)
                mixed = mixed + jnp.dot(
                    window, conv_weight[t_off, h_off, w_off], preferred_element_type=jnp.float32
                )
                back = grad_padded[
                    2 - t_off : 2 - t_off + frames,
                    2 - h_off : 2 - h_off + height,
                    2 - w_off : 2 - w_off + width,
                ].reshape(-1, channels)
                grad_act = grad_act + lax.dot_general(
                    back,
                    conv_weight[t_off, h_off, w_off],
                    (((1,), (1,)), ((), ())),
                    preferred_element_type=jnp.float32,
                )
    owners = lax.axis_size("ha") * lax.axis_size("wa")
    owned = channels // owners
    weight_taps = jnp.stack(
        [
            lax.dot_general(
                window, flat_grad, (((0,), (0,)), ((), ())), preferred_element_type=jnp.float32
            )
            for window in windows
        ]
    )
    shared = lax.psum_scatter(weight_taps, ("ha", "wa"), scatter_dimension=2, tiled=True)
    summed = lax.psum(shared, "ta")
    voxels_all = (
        frames * height * width * lax.axis_size("ta") * lax.axis_size("ha") * lax.axis_size("wa")
    )
    grad_weight = summed.reshape(3, 3, 3, channels, owned) * float(voxels_all) ** (-0.5)
    decoded = (values + mixed.reshape(features.shape)).astype(jnp.bfloat16)
    grad_norm = norm_backward(
        grad_act.reshape(features.shape), normed, unit_rms, inverse, norm_gain
    )
    grad_features = (cotangent.astype(jnp.float32) + grad_norm).astype(jnp.bfloat16)
    return (decoded, grad_features, grad_weight)


def solution(mesh):
    placed = (P("ta", "ha", "wa", None), P(), P(), P("ta", "ha", "wa", None))
    return jax.shard_map(
        body,
        mesh=mesh,
        in_specs=placed,
        out_specs=(
            P("ta", "ha", "wa", None),
            P("ta", "ha", "wa", None),
            P(None, None, None, None, ("ha", "wa")),
        ),
        check_vma=False,
    )
```

profile of v0, /device:TPU:0, one launch (start us, length us, event | category | flops | bytes accessed | tf_op | source)
XLA Modules:
  0.0 247.9 jit_solution(2919217578016059299)
XLA Ops:
  8.2 1.3 collective-permute-start.5
  11.8 7.6 %collective-permute-done.5 = bf16[2,16,16,256]{3,2,1,0:T(8,128)(2,1)S(1)} collective-permute-done((bf16[2,16,16,256]{3,2,1,0:T(8,128)(2,1)S(1)}, bf16[2,16,16,256]{3,2,1,0:T(8,128)(2,1)S(1)}, u32[]{:S(2)}, u32[]{:S(2)}) %collective-permute-start.5) | collective-permute-done | bytes 262176 | tf_op jit(solution)/shard_map/ppermute | solution.py:12
  19.4 1.3 collective-permute-start.6
  20.8 1.3 collective-permute-start.7
  22.1 3.7 %collective-permute-done.7 = bf16[6,1,16,256]{3,2,1,0:T(8,128)(2,1)S(1)} collective-permute-done((bf16[6,1,16,256]{3,2,1,0:T(8,128)(2,1)S(1)}, bf16[6,1,16,256]{3,2,1,0:T(8,128)(2,1)S(1)}, u32[]{:S(2)}, u32[]{:S(2)}) %collective-permute-start.7) | collective-permute-done | bytes 49184 | tf_op jit(solution)/shard_map/ppermute | solution.py:25
  25.9 1.3 collective-permute-start.8
  27.2 4.6 %collective-permute-start.9 = (bf16[6,18,1,256]{3,2,1,0:T(2,128)(2,1)S(1)}, bf16[6,18,1,256]{3,2,1,0:T(2,128)(2,1)S(1)}, u32[]{:S(2)}, u32[]{:S(2)}) collective-permute-start(bf16[6,18,1,256]{3,2,1,0:T(2,128)(2,1)S(1)} %get-tuple-element.48), channel_id=1, source_target_pairs={{0,1},{2,3},{4,5},{6,7},{8,9},{10,11},{12,13},{14,15},{16,17},{18,... | collective-permute-start | bytes 165896 | tf_op jit(solution)/shard_map/ppermute | solution.py:23
  32.7 1.4 collective-permute-done.9
  35.0 3.3 %fusion.191 = (bf16[4,16,16,256]{3,2,1,0:T(8,128)(2,1)S(1)}, bf16[4,16,16,256]{3,2,1,0:T(8,128)(2,1)S(1)}, bf16[4,16,16,256]{3,2,1,0:T(8,128)(2,1)S(1)}, bf16[4,...) fusion(bf16[6,18,17,256]{3,2,1,0:T(8,128)(2,1)S(1)} %get-tuple-, ...), kind=kLoop, calls=%fused_computation.304 | loop fusion | bytes 18874368 | tf_op jit(solution)/shard_map/slice | solution.py:69
  48.5 1.6 fusion.48
  50.1 3.5 %collective-permute-start = (bf16[2,16,16,256]{3,2,1,0:T(8,128)(2,1)S(1)}, bf16[2,16,16,256]{3,2,1,0:T(8,128)(2,1)S(1)}, u32[]{:S(2)}, u32[]{:S(2)}) collective-permute-start(bf16[2,16,16,256]{3,2,1,0:T(8,128)(2,1)S(1)} %slice.431), channel_id=1, source_target_pairs={{0,8},{8,16},{16,24},{1,9},{9,17},{17,25},{2,10},{10,18},{18,26},{... | collective-permute-start | bytes 786440 | tf_op jit(solution)/shard_map/ppermute | solution.py:12
  53.6 6.0 %collective-permute-done = bf16[2,16,16,256]{3,2,1,0:T(8,128)(2,1)S(1)} collective-permute-done((bf16[2,16,16,256]{3,2,1,0:T(8,128)(2,1)S(1)}, bf16[2,16,16,256]{3,2,1,0:T(8,128)(2,1)S(1)}, u32[]{:S(2)}, u32[]{:S(2)}) %collective-permute-start) | collective-permute-done | bytes 262176 | tf_op jit(solution)/shard_map/ppermute | solution.py:12
  59.6 1.3 collective-permute-start.2
  60.9 3.3 %collective-permute-start.1 = (bf16[6,1,16,256]{3,2,1,0:T(8,128)(2,1)S(1)}, bf16[6,1,16,256]{3,2,1,0:T(8,128)(2,1)S(1)}, u32[]{:S(2)}, u32[]{:S(2)}) collective-permute-start(bf16[6,1,16,256]{3,2,1,0:T(8,128)(2,1)S(1)} %get-tuple-element.77), channel_id=1, source_target_pairs={{0,2},{2,4},{4,6},{1,3},{3,5},{5,7},{8,10},{10,12},{12,14},{9,11},... | collective-permute-start | bytes 147464 | tf_op jit(solution)/shard_map/ppermute | solution.py:23
  65.3 1.3 collective-permute-start.4
  66.6 4.7 %collective-permute-start.3 = (bf16[6,18,1,256]{3,2,1,0:T(2,128)(2,1)S(1)}, bf16[6,18,1,256]{3,2,1,0:T(2,128)(2,1)S(1)}, u32[]{:S(2)}, u32[]{:S(2)}) collective-permute-start(bf16[6,18,1,256]{3,2,1,0:T(2,128)(2,1)S(1)} %get-tuple-element.52), channel_id=1, source_target_pairs={{0,1},{2,3},{4,5},{6,7},{8,9},{10,11},{12,13},{14,15},{16,17},{18,... | collective-permute-start | bytes 165896 | tf_op jit(solution)/shard_map/ppermute | solution.py:23
  72.0 1.8 collective-permute-done.3
  103.1 10.3 %copy.10 = f32[27,256,256]{1,0,2:T(8,128)} copy(f32[27,256,256]{2,1,0:T(8,128)} %fusion.12) | data formatting | bytes 14155776 | tf_op jit(solution)/shard_map/stack | solution.py:82
  114.1 1.6 copy-done.1
  125.9 63.1 %reduce-scatter.2.cloned.1.call-done = f32[27,256,32]{1,0,2:T(8,128)} async-done(((f32[27,256,256]{1,0,2:T(8,128)}), f32[27,256,32]{1,0,2:T(8,128)}) %reduce-scatter.2.cloned.1.call-update) | async-done | bytes 884752 | tf_op jit(solution)/shard_map/reduce_scatter | solution.py:90
  189.0 2.7 %copy.11 = f32[27,256,32]{1,2,0:T(8,128)} copy(f32[27,256,32]{1,0,2:T(8,128)} %reduce-scatter.2.cloned.1.call-done) | data formatting | bytes 1769472 | tf_op jit(solution)/shard_map/reduce_scatter | solution.py:90
  191.7 1.3 convolution_add_fusion.24
  196.4 42.4 %all-reduce.2.cloned.1.call-done = f32[27,256,32]{1,2,0:T(8,128)} async-done(((f32[27,256,32]{1,2,0:T(8,128)}), f32[27,256,32]{1,2,0:T(8,128)}) %all-reduce.2.cloned.1.call-update) | async-done | bytes 884752 | tf_op jit(solution)/shard_map/psum | solution.py:91
  238.9 2.2 broadcast_multiply_fusion
  (126 shorter events, 60.5 us)
Async XLA Ops:
  7.2 181.9 %reduce-scatter.2.cloned.1.call-start = ((), (), s32[]{:S(2)}) async-start(), calls=%async_computation.1 | async-start | bytes 9437184 | tf_op jit(solution)/shard_map/reduce_scatter | solution.py:90
  8.2 11.2 %collective-permute-start.5 = (bf16[2,16,16,256]{3,2,1,0:T(8,128)(2,1)S(1)}, bf16[2,16,16,256]{3,2,1,0:T(8,128)(2,1)S(1)}, u32[]{:S(2)}, u32[]{:S(2)}) collective-permute-start(bf16[2,16,16,256]{3,2,1,0:T(8,128)(2,1)S(1)} %slice.400), channel_id=1, source_target_pairs={{8,0},{16,8},{24,16},{9,1},{17,9},{25,17},{10,2},{18,10},{26,18},{... | collective-permute-start | bytes 786440 | tf_op jit(solution)/shard_map/ppermute | solution.py:12
  19.4 2.6 %collective-permute-start.6 = (bf16[6,1,16,256]{3,2,1,0:T(8,128)(2,1)S(1)}, bf16[6,1,16,256]{3,2,1,0:T(8,128)(2,1)S(1)}, u32[]{:S(2)}, u32[]{:S(2)}) collective-permute-start(bf16[6,1,16,256]{3,2,1,0:T(8,128)(2,1)S(1)} %get-tuple-element.70), channel_id=1, source_target_pairs={{0,2},{2,4},{4,6},{1,3},{3,5},{5,7},{8,10},{10,12},{12,14},{9,11},... | collective-permute-start | bytes 147464 | tf_op jit(solution)/shard_map/ppermute | solution.py:23
  20.8 5.0 %collective-permute-start.7 = (bf16[6,1,16,256]{3,2,1,0:T(8,128)(2,1)S(1)}, bf16[6,1,16,256]{3,2,1,0:T(8,128)(2,1)S(1)}, u32[]{:S(2)}, u32[]{:S(2)}) collective-permute-start(bf16[6,1,16,256]{3,2,1,0:T(8,128)(2,1)S(1)} %get-tuple-element.71), channel_id=1, source_target_pairs={{2,0},{4,2},{6,4},{3,1},{5,3},{7,5},{10,8},{12,10},{14,12},{11,9},... | collective-permute-start | bytes 147464 | tf_op jit(solution)/shard_map/ppermute | solution.py:25
  22.1 10.3 %copy-start = (bf16[3,3,3,256,256]{4,3,2,1,0:T(8,128)(2,1)S(1)}, bf16[3,3,3,256,256]{4,3,2,1,0:T(8,128)(2,1)}, u32[]{:S(2)}) copy-start(bf16[3,3,3,256,256]{4,3,2,1,0:T(8,128)(2,1)} %param.6) | copy-start | bytes 10616836
  25.9 6.8 %collective-permute-start.8 = (bf16[6,18,1,256]{3,2,1,0:T(2,128)(2,1)S(1)}, bf16[6,18,1,256]{3,2,1,0:T(2,128)(2,1)S(1)}, u32[]{:S(2)}, u32[]{:S(2)}) collective-permute-start(bf16[6,18,1,256]{3,2,1,0:T(2,128)(2,1)S(1)} %get-tuple-element.47), channel_id=1, source_target_pairs={{1,0},{3,2},{5,4},{7,6},{9,8},{11,10},{13,12},{15,14},{17,16},{19,... | collective-permute-start | bytes 165896 | tf_op jit(solution)/shard_map/ppermute | solution.py:25
  27.2 6.9 %collective-permute-start.9 = (bf16[6,18,1,256]{3,2,1,0:T(2,128)(2,1)S(1)}, bf16[6,18,1,256]{3,2,1,0:T(2,128)(2,1)S(1)}, u32[]{:S(2)}, u32[]{:S(2)}) collective-permute-start(bf16[6,18,1,256]{3,2,1,0:T(2,128)(2,1)S(1)} %get-tuple-element.48), channel_id=1, source_target_pairs={{0,1},{2,3},{4,5},{6,7},{8,9},{10,11},{12,13},{14,15},{16,17},{18,... | collective-permute-start | bytes 165896 | tf_op jit(solution)/shard_map/ppermute | solution.py:23
  45.0 1.0 copy-start.4
  46.7 1.0 copy-start.2
  46.7 1.0 copy-start.7
  50.1 9.5 %collective-permute-start = (bf16[2,16,16,256]{3,2,1,0:T(8,128)(2,1)S(1)}, bf16[2,16,16,256]{3,2,1,0:T(8,128)(2,1)S(1)}, u32[]{:S(2)}, u32[]{:S(2)}) collective-permute-start(bf16[2,16,16,256]{3,2,1,0:T(8,128)(2,1)S(1)} %slice.431), channel_id=1, source_target_pairs={{0,8},{8,16},{16,24},{1,9},{9,17},{17,25},{2,10},{10,18},{18,26},{... | collective-permute-start | bytes 786440 | tf_op jit(solution)/shard_map/ppermute | solution.py:12
  59.6 4.6 %collective-permute-start.2 = (bf16[6,1,16,256]{3,2,1,0:T(8,128)(2,1)S(1)}, bf16[6,1,16,256]{3,2,1,0:T(8,128)(2,1)S(1)}, u32[]{:S(2)}, u32[]{:S(2)}) collective-permute-start(bf16[6,1,16,256]{3,2,1,0:T(8,128)(2,1)S(1)} %get-tuple-element.76), channel_id=1, source_target_pairs={{2,0},{4,2},{6,4},{3,1},{5,3},{7,5},{10,8},{12,10},{14,12},{11,9},... | collective-permute-start | bytes 147464 | tf_op jit(solution)/shard_map/ppermute | solution.py:25
  60.9 4.2 %collective-permute-start.1 = (bf16[6,1,16,256]{3,2,1,0:T(8,128)(2,1)S(1)}, bf16[6,1,16,256]{3,2,1,0:T(8,128)(2,1)S(1)}, u32[]{:S(2)}, u32[]{:S(2)}) collective-permute-start(bf16[6,1,16,256]{3,2,1,0:T(8,128)(2,1)S(1)} %get-tuple-element.77), channel_id=1, source_target_pairs={{0,2},{2,4},{4,6},{1,3},{3,5},{5,7},{8,10},{10,12},{12,14},{9,11},... | collective-permute-start | bytes 147464 | tf_op jit(solution)/shard_map/ppermute | solution.py:23
  65.3 6.7 %collective-permute-start.4 = (bf16[6,18,1,256]{3,2,1,0:T(2,128)(2,1)S(1)}, bf16[6,18,1,256]{3,2,1,0:T(2,128)(2,1)S(1)}, u32[]{:S(2)}, u32[]{:S(2)}) collective-permute-start(bf16[6,18,1,256]{3,2,1,0:T(2,128)(2,1)S(1)} %get-tuple-element.51), channel_id=1, source_target_pairs={{1,0},{3,2},{5,4},{7,6},{9,8},{11,10},{13,12},{15,14},{17,16},{19,... | collective-permute-start | bytes 165896 | tf_op jit(solution)/shard_map/ppermute | solution.py:25
  66.6 7.2 %collective-permute-start.3 = (bf16[6,18,1,256]{3,2,1,0:T(2,128)(2,1)S(1)}, bf16[6,18,1,256]{3,2,1,0:T(2,128)(2,1)S(1)}, u32[]{:S(2)}, u32[]{:S(2)}) collective-permute-start(bf16[6,18,1,256]{3,2,1,0:T(2,128)(2,1)S(1)} %get-tuple-element.52), channel_id=1, source_target_pairs={{0,1},{2,3},{4,5},{6,7},{8,9},{10,11},{12,13},{14,15},{16,17},{18,... | collective-permute-start | bytes 165896 | tf_op jit(solution)/shard_map/ppermute | solution.py:23
  113.4 125.5 %all-reduce.2.cloned.1.call-start = ((), (), s32[]{:S(2)}) async-start(), calls=%async_computation.2 | async-start | bytes 1769472 | tf_op jit(solution)/shard_map/psum | solution.py:91
  113.7 2.0 copy-start.1
  125.3 66.4 %copy-start.5 = (bf16[4,16,16,256]{3,2,1,0:T(8,128)(2,1)S(1)}, bf16[4,16,16,256]{3,2,1,0:T(8,128)(2,1)}, u32[]{:S(2)}) copy-start(bf16[4,16,16,256]{3,2,1,0:T(8,128)(2,1)} %get-tuple-element.36) | copy-start | bytes 1572868
  125.6 67.4 %copy-start.6 = (bf16[4,16,16,256]{3,2,1,0:T(8,128)(2,1)S(1)}, bf16[4,16,16,256]{3,2,1,0:T(8,128)(2,1)}, u32[]{:S(2)}) copy-start(bf16[4,16,16,256]{3,2,1,0:T(8,128)(2,1)} %get-tuple-element.59) | copy-start | bytes 1572868
  191.7 3.7 %copy-start.3 = (bf16[4,16,16,256]{3,2,1,0:T(8,128)(2,1)S(1)}, bf16[4,16,16,256]{3,2,1,0:T(8,128)(2,1)}, u32[]{:S(2)}) copy-start(bf16[4,16,16,256]{3,2,1,0:T(8,128)(2,1)} %param.4) | copy-start | bytes 1572868
Sparse Core Ops, SparseCore 0:
  113.5 75.4 reduce-scatter.1
  192.1 46.6 all-reduce.1
where the time goes:
time: 249 us; the launch traced here: 248 us
  waiting for transfers between devices  128 us (51%)
  matrix products  48.2 us (19%)
  starting transfers between devices  24.1 us (10%)
  local copies, waits for them, and re-layouts  23.7 us (10%)
  between operations  14.7 us (6%)
  other arithmetic  9.68 us (4%)
    reduce_scatter x1, waiting for transfers between devices, body(): lax.psum_scatter(weight_taps, ('ha', 'wa'), scatter_dimension=2, tiled=True)  63.1 us
    psum x1, waiting for transfers between devices, body(): summed = lax.psum(shared, 'ta')  42.4 us
    dot_general x27, matrix products, body(): lax.dot_general(window, flat_grad, (((0,), (0,)), ((), ())), preferred_el...  28.4 us
    ppermute x4, starting transfers between devices, with_halo(): lax.ppermute(tail, axis, [(i, (i + 1) % count) for i in range(ends)])  13.9 us
    ppermute x2, waiting for transfers between devices, from_behind(): return lax.ppermute(array, axis, pairs)  13.6 us
    dot_general x27, matrix products, body(): jnp.dot(window, conv_weight[t_off, h_off, w_off], preferred_element_type=...  10.8 us
    another operation x1, local copies, waits for them, and re-layouts, body(): jnp.stack([lax.dot_general(window, flat_grad, (((0,), (0,)), ((), ())), p...  10.3 us
    dot_general x27, matrix products, body(): lax.dot_general(back, conv_weight[t_off, h_off, w_off], (((1,), (1,)), ((...  9.04 us
  transfers between devices with their start and end apart: 12, of which 9 were waited for; matrix products, arithmetic and copies ran while one was open for 7% of the time, Pallas kernels for 0%

commit v1 on v0

v1 whole, which is shorter than its diff:
```python
import functools

import jax
import jax.numpy as jnp
from jax import lax
from jax.experimental import pallas as pl
from jax.experimental.pallas import tpu as pltpu
from jax.sharding import PartitionSpec as P

EPSILON = 1e-06
AXES = ("ta", "ha", "wa")
BF16 = jnp.bfloat16
F32 = jnp.float32
VMEM_LIMIT = 48 * 1024 * 1024


def dot(a, b):
    return jnp.dot(a, b, preferred_element_type=F32)


def dot_t(a, b):
    return lax.dot_general(a, b, (((1,), (1,)), ((), ())), preferred_element_type=F32)


def call(kernel, out_shape, flops, moved, scratch=()):
    return pl.pallas_call(
        kernel,
        out_shape=out_shape,
        scratch_shapes=list(scratch),
        compiler_params=pltpu.CompilerParams(vmem_limit_bytes=VMEM_LIMIT),
        cost_estimate=pl.CostEstimate(flops=flops, bytes_accessed=moved, transcendentals=0),
    )


def shift_line(array, axis, by):
    length = lax.axis_size(axis)
    pairs = [(i, i + by) for i in range(length) if 0 <= i + by < length]
    return lax.ppermute(array, axis, pairs)


def swap_core(array):
    length = lax.axis_size("ha")
    return lax.ppermute(array, "ha", [(i, i ^ 1) for i in range(length)])


def to_chip(array, du, dw):
    chips, width = lax.axis_size("ha") // 2, lax.axis_size("wa")
    pairs = []
    for u in range(chips):
        for core in range(2):
            for w in range(width):
                source = (2 * u + core) * width + w
                target = (2 * ((u + du) % chips) + core) * width + (w + dw) % width
                pairs.append((source, target))
    return lax.ppermute(array, ("ha", "wa"), pairs)


def ring(array, axis, by):
    length = lax.axis_size(axis)
    return lax.ppermute(array, axis, [(i, (i + by) % length) for i in range(length)])


def plane_halo(cells):
    for axis, dim in (("wa", 2), ("ha", 1)):
        size = cells.shape[dim]
        head = lax.slice_in_dim(cells, 0, 1, axis=dim)
        tail = lax.slice_in_dim(cells, size - 1, size, axis=dim)
        cells = jnp.concatenate(
            [shift_line(tail, axis, 1), cells, shift_line(head, axis, -1)], axis=dim
        )
    return cells


def activate_kernel(x_ref, gain_ref, act_ref, act_t_ref):
    values = x_ref[...].astype(F32)
    inverse = lax.rsqrt(jnp.mean(values * values, axis=-1, keepdims=True) + EPSILON)
    normed = values * inverse * gain_ref[...]
    activated = (normed * jax.nn.sigmoid(normed)).astype(BF16)
    act_ref[...] = activated
    act_t_ref[...] = activated.T


def spread_columns(source, width, target):
    frames, high, _, channels = source.shape
    for k in range(3):
        target[k] = source[:, :, k : k + width, :].reshape(frames * high * width, channels)


def taps_kernel(height, width, act_a, act_b, cot_a, cot_b, out, spread_a, spread_b):
    frames = cot_a.shape[0]
    spread_columns(cot_a, width, spread_a)
    spread_columns(cot_b, width, spread_b)
    acts = jnp.concatenate([act_a[...], act_b[...]], axis=1)
    part = out.shape[1]

    def shifted(tap):
        j, k = divmod(tap, 3)
        pieces = []
        for spread in (spread_a, spread_b):
            for t in range(frames):
                start = (t * (height + 2) + 2 - j) * width
                pieces.append(spread[2 - k, start : start + height * width, :])
        return jnp.concatenate(pieces, axis=0)

    for first in range(0, 9, 2):
        taps = range(first, min(first + 2, 9))
        terms = dot(acts, jnp.concatenate([shifted(tap) for tap in taps], axis=1)).T
        for place, tap in enumerate(taps):
            out[tap] = terms[place * part : (place + 1) * part].astype(BF16)


def conv_sum(height, width, frames, spread, weight, backward):
    total = None
    for i in range(3):
        for j in range(3):
            at_t, at_h = (2 - i, 2 - j) if backward else (i, j)
            columns = []
            for k in range(3):
                at_w = 2 - k if backward else k
                pieces = []
                for t in range(frames):
                    start = ((t + at_t) * (height + 2) + at_h) * width
                    pieces.append(spread[at_w, start : start + height * width, :])
                columns.append(jnp.concatenate(pieces, axis=0))
            left = jnp.concatenate(columns, axis=1)
            if backward:
                term = dot_t(left, jnp.concatenate([weight[i, j, k] for k in range(3)], axis=1))
            else:
                term = dot(left, jnp.concatenate([weight[i, j, k] for k in range(3)], axis=0))
            total = term if total is None else total + term
    return total


def forward_kernel(height, width, x_ref, padded, weight, out, spread):
    frames = padded.shape[0] - 2
    spread_columns(padded, width, spread)
    mixed = conv_sum(height, width, frames, spread, weight, False)
    out[...] = (x_ref[...].astype(F32) + mixed).astype(BF16)


def backward_kernel(height, width, x_ref, gain_ref, cot_ref, padded, weight, out, spread):
    frames = padded.shape[0] - 2
    spread_columns(padded, width, spread)
    grad_act = conv_sum(height, width, frames, spread, weight, True)
    values = x_ref[...].astype(F32)
    inverse = lax.rsqrt(jnp.mean(values * values, axis=-1, keepdims=True) + EPSILON)
    unit_rms = values * inverse
    gain = gain_ref[...]
    normed = unit_rms * gain
    logistic = jax.nn.sigmoid(normed)
    grad_unit = grad_act * logistic * (1.0 + normed * (1.0 - logistic)) * gain
    grad_norm = inverse * (
        grad_unit - unit_rms * jnp.mean(grad_unit * unit_rms, axis=-1, keepdims=True)
    )
    out[...] = (cot_ref[...].astype(F32) + grad_norm).astype(BF16)


def body(features, norm_gain, conv_weight, cotangent):
    frames, height, width, channels = features.shape
    cells = frames * height * width
    depth, rows_of, cols_of = (lax.axis_size(axis) for axis in AXES)
    chips = rows_of // 2
    owners = rows_of * cols_of
    owned = channels // owners
    half = channels // 2
    me_t, me_h, me_w = (lax.axis_index(axis) for axis in AXES)
    core, chip = me_h % 2, me_h // 2
    flat_x = features.reshape(cells, channels)
    flat_cot = cotangent.reshape(cells, channels)
    gain = norm_gain.reshape(1, channels)
    product = 2 * cells * channels * channels

    act, act_t = call(
        activate_kernel,
        (
            jax.ShapeDtypeStruct((cells, channels), BF16),
            jax.ShapeDtypeStruct((channels, cells), BF16),
        ),
        10 * cells * channels,
        6 * cells * channels,
    )(flat_x, gain)
    act_t_other = swap_core(act_t)

    cot_plane = plane_halo(cotangent)
    cot_later = shift_line(cot_plane[:2], "ta", -1)
    grad_padded = jnp.concatenate([cot_plane, cot_later], axis=0)
    by_core = grad_padded.reshape(grad_padded.shape[:3] + (chips, 2, cols_of * owned))

    def half_of(which):
        first = by_core[..., 0, :].reshape(grad_padded.shape[:3] + (half,))
        second = by_core[..., 1, :].reshape(grad_padded.shape[:3] + (half,))
        return jnp.where(which == 0, first, second)

    mine = half_of(core)
    others = swap_core(half_of(1 - core))

    spread = pltpu.VMEM((3, frames * (height + 2) * width, half), BF16)
    taps = [
        call(
            functools.partial(taps_kernel, height, width),
            jax.ShapeDtypeStruct((9, half, channels), BF16),
            9 * product,
            4 * cells * channels,
            (spread, spread),
        )(act_t, act_t_other, mine[2 - i : 2 - i + frames], others[2 - i : 2 - i + frames])
        for i in range(3)
    ]
    parts = jnp.stack(taps).reshape(27, chips * cols_of, owned, channels)

    def slice_for(du, dw):
        place = ((chip + du) % chips) * cols_of + (me_w + dw) % cols_of
        return lax.dynamic_index_in_dim(parts, place, axis=1, keepdims=False)

    total = slice_for(0, 0).astype(F32)
    for du in range(chips):
        for dw in range(cols_of):
            if du or dw:
                total = total + to_chip(slice_for(du, dw), du, dw).astype(F32)

    total = total.reshape(depth, -1, channels)
    rounded = total.astype(BF16)

    def part_of(array, place):
        return lax.dynamic_index_in_dim(array, place, axis=0, keepdims=False)

    piece = part_of(total, me_t)
    for by in range(1, depth):
        piece = piece + ring(part_of(rounded, (me_t + by) % depth), "ta", by).astype(F32)
    voxels_all = cells * depth * rows_of * cols_of
    piece = (piece * float(voxels_all) ** (-0.5)).astype(BF16)
    pieces = [piece] + [ring(piece, "ta", by) for by in range(1, depth)]
    stacked = jnp.stack(pieces[::-1])
    stacked = jnp.roll(stacked, me_t + 1, axis=0)
    grad_weight = jnp.swapaxes(stacked.reshape(27, owned, channels), 1, 2).astype(F32)
    grad_weight = grad_weight.reshape(3, 3, 3, channels, owned)

    act_plane = plane_halo(act.reshape(features.shape))
    act_earlier = shift_line(act_plane[frames - 2 :], "ta", 1)
    padded = jnp.concatenate([act_earlier, act_plane], axis=0)

    flat = jax.ShapeDtypeStruct((cells, channels), BF16)
    spread = pltpu.VMEM((3, (frames + 2) * (height + 2) * width, channels), BF16)
    moved = conv_weight.size * 2 + 8 * cells * channels
    decoded = call(
        functools.partial(forward_kernel, height, width), flat, 27 * product, moved, (spread,)
    )(flat_x, padded, conv_weight)
    grad_features = call(
        functools.partial(backward_kernel, height, width), flat, 27 * product, moved, (spread,)
    )(flat_x, gain, flat_cot, grad_padded, conv_weight)
    return (
        decoded.reshape(features.shape),
        grad_features.reshape(features.shape),
        grad_weight,
    )


def solution(mesh):
    placed = (P("ta", "ha", "wa", None), P(), P(), P("ta", "ha", "wa", None))
    return jax.shard_map(
        body,
        mesh=mesh,
        in_specs=placed,
        out_specs=(
            P("ta", "ha", "wa", None),
            P("ta", "ha", "wa", None),
            P(None, None, None, None, ("ha", "wa")),
        ),
        check_vma=False,
    )
```

time: 249 us -> 147 us (0.59)
  waiting for transfers between devices: 128 us -> 47.1 us
  matrix products: 48.2 us -> 0 us
  Pallas kernels: 0 us -> 20 us
  between operations: 14.7 us -> 1 us
  starting transfers between devices: 24.1 us -> 35.2 us
  local copies, waits for them, and re-layouts: 23.7 us -> 30.5 us
  other arithmetic: 9.68 us -> 12.3 us
    reduce_scatter x1 -> x0, waiting for transfers between devices: 63.1 us -> none  [body(): lax.psum_scatter(weight_taps, ('ha', 'wa'), scatter_dimension=2, tiled=True)]
    dot_general x81 -> x0, matrix products: 48.2 us -> none  [the longest x27 28.4 us: body(): lax.dot_general(window, flat_grad, (((0,), (0,)), ((), ())), preferred_el...]
    psum x1 -> x0, waiting for transfers between devices: 42.4 us -> none  [body(): summed = lax.psum(shared, 'ta')]
    ppermute x10 -> x21, waiting for transfers between devices: 21.9 us -> 47.1 us  [the longest x3 18.6 us: to_chip(): return lax.ppermute(array, ('ha', 'wa'), pairs)]
    pallas_call x0 -> x6, Pallas kernels: none -> 20 us  [the longest x3 9.07 us: body(): call(functools.partial(taps_kernel, height, width), jax.ShapeDtypeStruct(...]
    slice x8 -> x11, local copies, waits for them, and re-layouts: 7.41 us -> 20.5 us  [the longest x7 12.6 us: body(): mine[2 - i:2 - i + frames]]
    ppermute x10 -> x21, starting transfers between devices: 23.8 us -> 35.2 us  [the longest x10 20.4 us: shift_line(): return lax.ppermute(array, axis, pairs)]
    another operation x1 -> x0, local copies, waits for them, and re-layouts: 10.3 us -> none  [body(): jnp.stack([lax.dot_general(window, flat_grad, (((0,), (0,)), ((), ())), p...]
  transfers between devices with their start and end apart: 12 -> 21, of which waited for: 9 -> 10; matrix products, arithmetic and copies ran while one was open for 7% -> 24% of each run, Pallas kernels for 0% -> 14%
where the time goes in v1:
time: 147 us; the launch traced here: 146 us
  waiting for transfers between devices  47.1 us (32%)
  starting transfers between devices  35.2 us (24%)
  local copies, waits for them, and re-layouts  30.5 us (21%)
  Pallas kernels  20 us (14%)
  other arithmetic  12.3 us (8%)
    ppermute x10, starting transfers between devices, shift_line(): return lax.ppermute(array, axis, pairs)  20.4 us
    ppermute x3, waiting for transfers between devices, to_chip(): return lax.ppermute(array, ('ha', 'wa'), pairs)  18.6 us
    ppermute x10, waiting for transfers between devices, shift_line(): return lax.ppermute(array, axis, pairs)  16.7 us
    slice x7, local copies, waits for them, and re-layouts, body(): mine[2 - i:2 - i + frames]  12.6 us
    ppermute x6, waiting for transfers between devices, ring(): lax.ppermute(array, axis, [(i, (i + by) % length) for i in range(length)])  11.9 us
    pallas_call x3, Pallas kernels, body(): call(functools.partial(taps_kernel, height, width), jax.ShapeDtypeStruct(...  9.07 us
    ppermute x6, starting transfers between devices, ring(): lax.ppermute(array, axis, [(i, (i + by) % length) for i in range(length)])  8.3 us
    select_n x2, local copies, waits for them, and re-layouts, half_of(): return jnp.where(which == 0, first, second)  5.22 us
  transfers between devices with their start and end apart: 21, of which 10 were waited for; matrix products, arithmetic and copies ran while one was open for 24% of the time, Pallas kernels for 14%

profile of v1, /device:TPU:0, one launch (start us, length us, event | category | flops | bytes accessed | tf_op | source)
XLA Modules:
  0.0 146.0 jit_solution(12926611588569672725)
XLA Ops:
  1.9 4.9 %collective-permute-start.5 = (bf16[4,16,1,256]{3,2,1,0:T(2,128)(2,1)S(1)}, bf16[4,16,1,256]{3,2,1,0:T(2,128)(2,1)S(1)}, u32[]{:S(2)}, u32[]{:S(2)}) collective-permute-start(bf16[4,16,1,256]{3,2,1,0:T(2,128)(2,1)S(1)} %get-tuple-element.24), channel_id=1, source_target_pairs={{0,1},{2,3},{4,5},{6,7},{8,9},{10,11},{12,13},{14,15},{16,17},{18,... | collective-permute-start | bytes 98312 | tf_op jit(solution)/shard_map/ppermute | solution.py:38
  8.7 4.3 %collective-permute-done.6 = bf16[4,16,1,256]{3,2,1,0:T(2,128)(2,1)S(1)} collective-permute-done((bf16[4,16,1,256]{3,2,1,0:T(2,128)(2,1)S(1)}, bf16[4,16,1,256]{3,2,1,0:T(2,128)(2,1)S(1)}, u32[]{:S(2)}, u32[]{:S(2)}) %collective-permute-start.6) | collective-permute-done | bytes 32800 | tf_op jit(solution)/shard_map/ppermute | solution.py:38
  16.4 3.5 %collective-permute-done.8 = bf16[4,1,18,256]{3,2,1,0:T(8,128)(2,1)S(1)} collective-permute-done((bf16[4,1,18,256]{3,2,1,0:T(8,128)(2,1)S(1)}, bf16[4,1,18,256]{3,2,1,0:T(8,128)(2,1)S(1)}, u32[]{:S(2)}, u32[]{:S(2)}) %collective-permute-start.8) | collective-permute-done | bytes 36896 | tf_op jit(solution)/shard_map/ppermute | solution.py:38
  26.6 7.6 %collective-permute-done.9 = bf16[2,18,18,256]{3,2,1,0:T(8,128)(2,1)} collective-permute-done((bf16[2,18,18,256]{3,2,1,0:T(8,128)(2,1)S(1)}, bf16[2,18,18,256]{3,2,1,0:T(8,128)(2,1)}, u32[]{:S(2)}, u32[]{:S(2)}) %collective-permute-start.9) | collective-permute-done | bytes 331808 | tf_op jit(solution)/shard_map/ppermute | solution.py:38
  35.8 2.4 %reshape.57 = bf16[6,18,18,2,2,64]{5,4,3,2,1,0:T(2,128)(2,1)} reshape(bf16[6,18,18,256]{3,2,1,0:T(8,128)(2,1)S(1)} %pad_maximum_fusion.1.padded) | data formatting | bytes 1990656 | tf_op jit(solution)/shard_map/reshape | solution.py:187
  38.1 5.1 %fusion.6 = (bf16[6,18,18,2,1,64]{5,4,3,2,1,0:T(2,128)(2,1)S(1)}, bf16[6,18,18,2,1,64]{5,4,3,2,1,0:T(2,128)(2,1)S(1)}) fusion(bf16[6,18,18,2,2,64]{5,4,3,2,1,0:T(2,128)(2,1)} %reshape.57), kind=kLoop, calls=%fused_computation.42 | loop fusion | bytes 1990656 | tf_op jit(solution)/shard_map/slice | solution.py:190
  43.3 3.1 %broadcast_select_fusion = (bf16[6,18,18,2,1,64]{5,3,0,2,1,4:T(2,128)(2,1)}, bf16[6,18,18,2,1,64]{5,3,0,2,1,4:T(2,128)(2,1)}) fusion(pred[]{:T(512)S(6)} %eq.23, bf16[6,18,18,2,1,64]{5,4,3,2,1,0:T(2,128)(2,1)S(1)} %get-tuple-element.10, bf16[6,18,18,2,1,64]{5,4,3,2,1,0:T(2,128)(2,1)S(1)} %get-tuple-element.9, pred[]{:T(512)S(6)} %eq.22), kind=kLoop, calls=%fused_computation | loop fusion | flops 497664 | bytes 1990658 | tf_op jit(solution)/shard_map/jit(_where)/select_n | solution.py:192
  46.3 3.1 %reshape.68 = bf16[6,18,18,128]{3,0,2,1:T(8,128)(2,1)} reshape(bf16[6,18,18,2,1,64]{5,3,0,2,1,4:T(2,128)(2,1)} %get-tuple-element.7) | data formatting | bytes 995328 | tf_op jit(solution)/shard_map/jit(_where)/select_n | solution.py:192
  59.4 4.2 %collective-permute-start.4 = (bf16[2,18,18,256]{3,2,1,0:T(8,128)(2,1)}, bf16[2,18,18,256]{3,2,1,0:T(8,128)(2,1)}, u32[]{:S(2)}, u32[]{:S(2)}) collective-permute-start(bf16[2,18,18,256]{3,2,1,0:T(8,128)(2,1)} %pad_maximum_fusion.6), channel_id=1, source_target_pairs={{0,8},{8,16},{16,24},{1,9},{9,17},{17,25},{2,10},{10,18},{18,26},{... | collective-permute-start | bytes 995336 | tf_op jit(solution)/shard_map/ppermute | solution.py:38
  63.6 2.2 %fusion.7 = (bf16[4,18,18,2,1,64]{5,3,0,2,1,4:T(2,128)(2,1)}, bf16[4,18,18,2,1,64]{5,3,0,2,1,4:T(2,128)(2,1)}, bf16[4,18,18,2,1,64]{5,3,0,2,1,4:T(2,128)(2,1)}) fusion(bf16[6,18,18,2,1,64]{5,3,0,2,1,4:T(2,128)(2,1)S(1)} %copy-done.5), kind=kLoop, calls=%fused_computation.43 | loop fusion | bytes 1990656 | tf_op jit(solution)/shard_map/slice | solution.py:205
  65.8 2.2 %slice.78 = bf16[4,18,18,128]{3,0,2,1:T(4,128)(2,1)} reshape(bf16[4,18,18,2,1,64]{5,3,0,2,1,4:T(2,128)(2,1)} %get-tuple-element.14) | data formatting | bytes 663552 | tf_op jit(solution)/shard_map/slice | solution.py:205
  69.0 2.2 %slice.81 = bf16[4,18,18,128]{3,0,2,1:T(4,128)(2,1)} reshape(bf16[4,18,18,2,1,64]{5,3,0,2,1,4:T(2,128)(2,1)} %get-tuple-element.16) | data formatting | bytes 663552 | tf_op jit(solution)/shard_map/slice | solution.py:205
  77.7 3.1 %shard_map.70 = bf16[9,128,256]{2,1,0:T(8,128)(2,1)S(1)} custom-call(bf16[256,1024]{1,0:T(8,128)(2,1)} %get-tuple-element.6.act_a, bf16[256,1024]{1,0:T(8,128)(2,1)} %collective-permute-done.10.act_b, bf16[4,18,18,128]{3,2,1,0:T(8,128)(2,1)S(1)} %copy.12.cot_a, bf16[4,18,18,128]{3,2,1,0:T(8,128)(2,1)S(1)} %get-tuple-element.17.cot_b), custom_call_target="tpu_custom_call" | custom-call | flops 1207959552 | bytes 1048576 | tf_op jit(solution)/shard_map/pallas_call | solution.py:199
  80.8 3.0 %shard_map.71 = bf16[9,128,256]{2,1,0:T(8,128)(2,1)S(1)} custom-call(bf16[256,1024]{1,0:T(8,128)(2,1)} %get-tuple-element.6.act_a, bf16[256,1024]{1,0:T(8,128)(2,1)} %collective-permute-done.10.act_b, bf16[4,18,18,128]{3,2,1,0:T(8,128)(2,1)S(1)} %copy-done.2, bf16[4,18,18,128]{3,2,1,0:T(8,128)(2,1)S(1)} %get-tuple-element.19.cot_b), custom_call_target="tpu_custom_call" | custom-call | flops 1207959552 | bytes 1048576 | tf_op jit(solution)/shard_map/pallas_call | solution.py:199
  83.8 3.0 %shard_map.72 = bf16[9,128,256]{2,1,0:T(8,128)(2,1)S(1)} custom-call(bf16[256,1024]{1,0:T(8,128)(2,1)} %get-tuple-element.6.act_a, bf16[256,1024]{1,0:T(8,128)(2,1)} %collective-permute-done.10.act_b, bf16[4,18,18,128]{3,2,1,0:T(8,128)(2,1)S(1)} %copy.14.cot_a, bf16[4,18,18,128]{3,2,1,0:T(8,128)(2,1)S(1)} %get-tuple-element.18.cot_b), custom_call_target="tpu_custom_call" | custom-call | flops 1207959552 | bytes 1048576 | tf_op jit(solution)/shard_map/pallas_call | solution.py:199
  89.3 2.2 %collective-permute-start.13 = (bf16[27,32,256]{2,1,0:T(8,128)(2,1)}, bf16[27,32,256]{2,1,0:T(8,128)(2,1)}, u32[]{:S(2)}, u32[]{:S(2)}) collective-permute-start(bf16[27,32,256]{2,1,0:T(8,128)(2,1)} %get-tuple-element.13), channel_id=1, source_target_pairs={{0,4},{1,5},{2,6},{3,7},{4,0},{5,1},{6,2},{7,3},{8,12},{9,13},{10,... | collective-permute-start | bytes 1327112 | tf_op jit(solution)/shard_map/ppermute | solution.py:55
  94.6 7.0 %collective-permute-done.12 = bf16[27,32,256]{2,1,0:T(8,128)(2,1)} collective-permute-done((bf16[27,32,256]{2,1,0:T(8,128)(2,1)}, bf16[27,32,256]{2,1,0:T(8,128)(2,1)}, u32[]{:S(2)}, u32[]{:S(2)}) %collective-permute-start.12) | collective-permute-done | bytes 442400 | tf_op jit(solution)/shard_map/ppermute | solution.py:55
  102.3 10.9 %collective-permute-done.14 = bf16[27,32,256]{2,1,0:T(8,128)(2,1)} collective-permute-done((bf16[27,32,256]{2,1,0:T(8,128)(2,1)S(1)}, bf16[27,32,256]{2,1,0:T(8,128)(2,1)}, u32[]{:S(2)}, u32[]{:S(2)}) %collective-permute-start.14) | collective-permute-done | bytes 442400 | tf_op jit(solution)/shard_map/ppermute | solution.py:55
  116.0 2.8 %collective-permute-start.17 = (bf16[216,256]{1,0:T(8,128)(2,1)S(1)}, bf16[216,256]{1,0:T(8,128)(2,1)S(1)}, u32[]{:S(2)}, u32[]{:S(2)}) collective-permute-start(bf16[216,256]{1,0:T(8,128)(2,1)S(1)} %get-tuple-element.29), channel_id=1, source_target_pairs={{0,24},{8,0},{16,8},{24,16},{1,25},{9,1},{17,9},{25,17},{2,26},{10... | collective-permute-start | bytes 331784 | tf_op jit(solution)/shard_map/ppermute | solution.py:60
  118.8 4.6 %shard_map.68 = bf16[1024,256]{1,0:T(8,128)(2,1)} custom-call(bf16[1024,256]{1,0:T(8,128)(2,1)S(1)} %bitcast.70, bf16[6,18,18,256]{3,2,1,0:T(8,128)(2,1)S(1)} %maximum_maximum_fusion.padded, bf16[3,3,3,256,256]{4,3,2,1,0:T(8,128)(2,1)S(1)} %copy-done.4), custom_call_target="tpu_custom_call" | custom-call | flops 3623878656 | bytes 5636096 | tf_op jit(solution)/shard_map/pallas_call | solution.py:244
  123.5 3.6 %collective-permute-done.16 = bf16[216,256]{1,0:T(8,128)(2,1)S(1)} collective-permute-done((bf16[216,256]{1,0:T(8,128)(2,1)S(1)}, bf16[216,256]{1,0:T(8,128)(2,1)S(1)}, u32[]{:S(2)}, u32[]{:S(2)}) %collective-permute-start.16) | collective-permute-done | bytes 110624 | tf_op jit(solution)/shard_map/ppermute | solution.py:60
  127.1 2.8 %collective-permute-start.18 = (bf16[216,256]{1,0:T(8,128)(2,1)S(1)}, bf16[216,256]{1,0:T(8,128)(2,1)S(1)}, u32[]{:S(2)}, u32[]{:S(2)}) collective-permute-start(bf16[216,256]{1,0:T(8,128)(2,1)S(1)} %fusion.5), channel_id=1, source_target_pairs={{0,24},{8,0},{16,8},{24,16},{1,25},{9,1},{17,9},{25,17},{2,26},{10... | collective-permute-start | bytes 331784 | tf_op jit(solution)/shard_map/ppermute | solution.py:60
  129.9 5.0 %shard_map.69 = bf16[1024,256]{1,0:T(8,128)(2,1)} custom-call(bf16[1024,256]{1,0:T(8,128)(2,1)S(1)} %bitcast.71, f32[1,256]{1,0:T(1,128)S(1)} %bitcast.73, bf16[1024,256]{1,0:T(8,128)(2,1)S(1)} %bitcast.61, bf16[6,18,18,256]{3,2,1,0:T(8,128)(2,1)S(1)} %pad_maximum_fusion.1.padded, bf16[3,3,3,256,256]{4,3,2,1,0:T(8,128)(2,1)S(1)} %copy-done.4), custom_call_target="tpu_custom_call" | custom-call | flops 3623878656 | bytes 5636096 | tf_op jit(solution)/shard_map/pallas_call | solution.py:247
  136.6 8.3 %collective-permute-done.19 = bf16[216,256]{1,0:T(8,128)(2,1)S(1)} collective-permute-done((bf16[216,256]{1,0:T(8,128)(2,1)S(1)}, bf16[216,256]{1,0:T(8,128)(2,1)S(1)}, u32[]{:S(2)}, u32[]{:S(2)}) %collective-permute-start.19) | collective-permute-done | bytes 110624 | tf_op jit(solution)/shard_map/ppermute | solution.py:60
  (77 shorter events, 44.1 us)
Async XLA Ops:
  0.6 33.6 %copy-start = (bf16[4,16,16,256]{3,2,1,0:T(8,128)(2,1)S(1)}, bf16[4,16,16,256]{3,2,1,0:T(8,128)(2,1)}, u32[]{:S(2)}) copy-start(bf16[4,16,16,256]{3,2,1,0:T(8,128)(2,1)} %param.7) | copy-start | bytes 1572868
  0.6 21.8 %copy-start.1 = (bf16[4,16,16,256]{3,2,1,0:T(8,128)(2,1)S(1)}, bf16[4,16,16,256]{3,2,1,0:T(8,128)(2,1)}, u32[]{:S(2)}) copy-start(bf16[4,16,16,256]{3,2,1,0:T(8,128)(2,1)} %param.4) | copy-start | bytes 1572868
  1.9 6.8 %collective-permute-start.5 = (bf16[4,16,1,256]{3,2,1,0:T(2,128)(2,1)S(1)}, bf16[4,16,1,256]{3,2,1,0:T(2,128)(2,1)S(1)}, u32[]{:S(2)}, u32[]{:S(2)}) collective-permute-start(bf16[4,16,1,256]{3,2,1,0:T(2,128)(2,1)S(1)} %get-tuple-element.24), channel_id=1, source_target_pairs={{0,1},{2,3},{4,5},{6,7},{8,9},{10,11},{12,13},{14,15},{16,17},{18,... | collective-permute-start | bytes 98312 | tf_op jit(solution)/shard_map/ppermute | solution.py:38
  6.8 6.2 %collective-permute-start.6 = (bf16[4,16,1,256]{3,2,1,0:T(2,128)(2,1)S(1)}, bf16[4,16,1,256]{3,2,1,0:T(2,128)(2,1)S(1)}, u32[]{:S(2)}, u32[]{:S(2)}) collective-permute-start(bf16[4,16,1,256]{3,2,1,0:T(2,128)(2,1)S(1)} %get-tuple-element.25), channel_id=1, source_target_pairs={{1,0},{3,2},{5,4},{7,6},{9,8},{11,10},{13,12},{15,14},{17,16},{19,... | collective-permute-start | bytes 98312 | tf_op jit(solution)/shard_map/ppermute | solution.py:38
  13.7 2.6 %collective-permute-start.7 = (bf16[4,1,18,256]{3,2,1,0:T(8,128)(2,1)S(1)}, bf16[4,1,18,256]{3,2,1,0:T(8,128)(2,1)S(1)}, u32[]{:S(2)}, u32[]{:S(2)}) collective-permute-start(bf16[4,1,18,256]{3,2,1,0:T(8,128)(2,1)S(1)} %get-tuple-element.20), channel_id=1, source_target_pairs={{0,2},{2,4},{4,6},{1,3},{3,5},{5,7},{8,10},{10,12},{12,14},{9,11},... | collective-permute-start | bytes 110600 | tf_op jit(solution)/shard_map/ppermute | solution.py:38
  15.0 4.8 %collective-permute-start.8 = (bf16[4,1,18,256]{3,2,1,0:T(8,128)(2,1)S(1)}, bf16[4,1,18,256]{3,2,1,0:T(8,128)(2,1)S(1)}, u32[]{:S(2)}, u32[]{:S(2)}) collective-permute-start(bf16[4,1,18,256]{3,2,1,0:T(8,128)(2,1)S(1)} %get-tuple-element.21), channel_id=1, source_target_pairs={{2,0},{4,2},{6,4},{3,1},{5,3},{7,5},{10,8},{12,10},{14,12},{11,9},... | collective-permute-start | bytes 110600 | tf_op jit(solution)/shard_map/ppermute | solution.py:38
  21.1 13.2 %collective-permute-start.9 = (bf16[2,18,18,256]{3,2,1,0:T(8,128)(2,1)S(1)}, bf16[2,18,18,256]{3,2,1,0:T(8,128)(2,1)}, u32[]{:S(2)}, u32[]{:S(2)}) collective-permute-start(bf16[2,18,18,256]{3,2,1,0:T(8,128)(2,1)S(1)} %pad_maximum_fusion.2), channel_id=1, source_target_pairs={{8,0},{16,8},{24,16},{9,1},{17,9},{25,17},{10,2},{18,10},{26,18},{... | collective-permute-start | bytes 995336 | tf_op jit(solution)/shard_map/ppermute | solution.py:38
  23.7 29.5 %collective-permute-start = (bf16[4,16,1,256]{3,2,1,0:T(2,128)(2,1)S(1)}, bf16[4,16,1,256]{3,2,1,0:T(2,128)(2,1)S(1)}, u32[]{:S(2)}, u32[]{:S(2)}) collective-permute-start(bf16[4,16,1,256]{3,2,1,0:T(2,128)(2,1)S(1)} %get-tuple-element.26), channel_id=1, source_target_pairs={{0,1},{2,3},{4,5},{6,7},{8,9},{10,11},{12,13},{14,15},{16,17},{18,... | collective-permute-start | bytes 98312 | tf_op jit(solution)/shard_map/ppermute | solution.py:38
  25.3 28.0 %collective-permute-start.1 = (bf16[4,16,1,256]{3,2,1,0:T(2,128)(2,1)S(1)}, bf16[4,16,1,256]{3,2,1,0:T(2,128)(2,1)S(1)}, u32[]{:S(2)}, u32[]{:S(2)}) collective-permute-start(bf16[4,16,1,256]{3,2,1,0:T(2,128)(2,1)S(1)} %get-tuple-element.27), channel_id=1, source_target_pairs={{1,0},{3,2},{5,4},{7,6},{9,8},{11,10},{13,12},{15,14},{17,16},{19,... | collective-permute-start | bytes 98312 | tf_op jit(solution)/shard_map/ppermute | solution.py:38
  51.6 24.6 %collective-permute-start.11 = (bf16[6,18,18,128]{3,2,1,0:T(8,128)(2,1)}, bf16[6,18,18,128]{3,2,1,0:T(8,128)(2,1)}, u32[]{:S(2)}, u32[]{:S(2)}) collective-permute-start(bf16[6,18,18,128]{3,2,1,0:T(8,128)(2,1)} %copy.15), channel_id=1, source_target_pairs={{0,2},{2,0},{4,6},{6,4},{1,3},{3,1},{5,7},{7,5},{8,10},{10,8},{12,... | collective-permute-start | bytes 1493000 | tf_op jit(solution)/shard_map/ppermute | solution.py:43
  53.3 4.4 %collective-permute-start.2 = (bf16[4,1,18,256]{3,2,1,0:T(8,128)(2,1)S(1)}, bf16[4,1,18,256]{3,2,1,0:T(8,128)(2,1)S(1)}, u32[]{:S(2)}, u32[]{:S(2)}) collective-permute-start(bf16[4,1,18,256]{3,2,1,0:T(8,128)(2,1)S(1)} %get-tuple-element.22), channel_id=1, source_target_pairs={{0,2},{2,4},{4,6},{1,3},{3,5},{5,7},{8,10},{10,12},{12,14},{9,11},... | collective-permute-start | bytes 110600 | tf_op jit(solution)/shard_map/ppermute | solution.py:38
  55.2 3.1 %collective-permute-start.3 = (bf16[4,1,18,256]{3,2,1,0:T(8,128)(2,1)S(1)}, bf16[4,1,18,256]{3,2,1,0:T(8,128)(2,1)S(1)}, u32[]{:S(2)}, u32[]{:S(2)}) collective-permute-start(bf16[4,1,18,256]{3,2,1,0:T(8,128)(2,1)S(1)} %get-tuple-element.23), channel_id=1, source_target_pairs={{2,0},{4,2},{6,4},{3,1},{5,3},{7,5},{10,8},{12,10},{14,12},{11,9},... | collective-permute-start | bytes 110600 | tf_op jit(solution)/shard_map/ppermute | solution.py:38
  56.5 21.2 %collective-permute-start.10 = (bf16[256,1024]{1,0:T(8,128)(2,1)}, bf16[256,1024]{1,0:T(8,128)(2,1)}, u32[]{:S(2)}, u32[]{:S(2)}) collective-permute-start(bf16[256,1024]{1,0:T(8,128)(2,1)} %get-tuple-element.6.act_a), channel_id=1, source_target_pairs={{0,2},{2,0},{4,6},{6,4},{1,3},{3,1},{5,7},{7,5},{8,10},{10,8},{12,... | collective-permute-start | bytes 1572872 | tf_op jit(solution)/shard_map/ppermute | solution.py:43
  59.4 33.5 %collective-permute-start.4 = (bf16[2,18,18,256]{3,2,1,0:T(8,128)(2,1)}, bf16[2,18,18,256]{3,2,1,0:T(8,128)(2,1)}, u32[]{:S(2)}, u32[]{:S(2)}) collective-permute-start(bf16[2,18,18,256]{3,2,1,0:T(8,128)(2,1)} %pad_maximum_fusion.6), channel_id=1, source_target_pairs={{0,8},{8,16},{16,24},{1,9},{9,17},{17,25},{2,10},{10,18},{18,26},{... | collective-permute-start | bytes 995336 | tf_op jit(solution)/shard_map/ppermute | solution.py:38
  89.3 12.3 %collective-permute-start.12 = (bf16[27,32,256]{2,1,0:T(8,128)(2,1)}, bf16[27,32,256]{2,1,0:T(8,128)(2,1)}, u32[]{:S(2)}, u32[]{:S(2)}) collective-permute-start(bf16[27,32,256]{2,1,0:T(8,128)(2,1)} %get-tuple-element.11), channel_id=1, source_target_pairs={{0,1},{1,0},{2,3},{3,2},{4,5},{5,4},{6,7},{7,6},{8,9},{9,8},{10,11... | collective-permute-start | bytes 1327112 | tf_op jit(solution)/shard_map/ppermute | solution.py:55
  89.3 13.0 %collective-permute-start.13 = (bf16[27,32,256]{2,1,0:T(8,128)(2,1)}, bf16[27,32,256]{2,1,0:T(8,128)(2,1)}, u32[]{:S(2)}, u32[]{:S(2)}) collective-permute-start(bf16[27,32,256]{2,1,0:T(8,128)(2,1)} %get-tuple-element.13), channel_id=1, source_target_pairs={{0,4},{1,5},{2,6},{3,7},{4,0},{5,1},{6,2},{7,3},{8,12},{9,13},{10,... | collective-permute-start | bytes 1327112 | tf_op jit(solution)/shard_map/ppermute | solution.py:55
  91.4 21.7 %collective-permute-start.14 = (bf16[27,32,256]{2,1,0:T(8,128)(2,1)S(1)}, bf16[27,32,256]{2,1,0:T(8,128)(2,1)}, u32[]{:S(2)}, u32[]{:S(2)}) collective-permute-start(bf16[27,32,256]{2,1,0:T(8,128)(2,1)S(1)} %get-tuple-element.12), channel_id=1, source_target_pairs={{0,5},{1,4},{2,7},{3,6},{4,1},{5,0},{6,3},{7,2},{8,13},{9,12},{10,... | collective-permute-start | bytes 1327112 | tf_op jit(solution)/shard_map/ppermute | solution.py:55
  94.6 24.3 %copy-start.4 = (bf16[3,3,3,256,256]{4,3,2,1,0:T(8,128)(2,1)S(1)}, bf16[3,3,3,256,256]{4,3,2,1,0:T(8,128)(2,1)}, u32[]{:S(2)}) copy-start(bf16[3,3,3,256,256]{4,3,2,1,0:T(8,128)(2,1)} %weight.3) | copy-start | bytes 10616836
  114.9 8.5 %collective-permute-start.15 = (bf16[216,256]{1,0:T(8,128)(2,1)S(1)}, bf16[216,256]{1,0:T(8,128)(2,1)S(1)}, u32[]{:S(2)}, u32[]{:S(2)}) collective-permute-start(bf16[216,256]{1,0:T(8,128)(2,1)S(1)} %get-tuple-element.28), channel_id=1, source_target_pairs={{0,8},{8,16},{16,24},{24,0},{1,9},{9,17},{17,25},{25,1},{2,10},{10... | collective-permute-start | bytes 331784 | tf_op jit(solution)/shard_map/ppermute | solution.py:60
  116.0 11.0 %collective-permute-start.16 = (bf16[216,256]{1,0:T(8,128)(2,1)S(1)}, bf16[216,256]{1,0:T(8,128)(2,1)S(1)}, u32[]{:S(2)}, u32[]{:S(2)}) collective-permute-start(bf16[216,256]{1,0:T(8,128)(2,1)S(1)} %get-tuple-element.30), channel_id=1, source_target_pairs={{0,16},{8,24},{16,0},{24,8},{1,17},{9,25},{17,1},{25,9},{2,18},{10... | collective-permute-start | bytes 331784 | tf_op jit(solution)/shard_map/ppermute | solution.py:60
  116.0 11.0 %collective-permute-start.17 = (bf16[216,256]{1,0:T(8,128)(2,1)S(1)}, bf16[216,256]{1,0:T(8,128)(2,1)S(1)}, u32[]{:S(2)}, u32[]{:S(2)}) collective-permute-start(bf16[216,256]{1,0:T(8,128)(2,1)S(1)} %get-tuple-element.29), channel_id=1, source_target_pairs={{0,24},{8,0},{16,8},{24,16},{1,25},{9,1},{17,9},{25,17},{2,26},{10... | collective-permute-start | bytes 331784 | tf_op jit(solution)/shard_map/ppermute | solution.py:60
  127.1 9.5 %collective-permute-start.18 = (bf16[216,256]{1,0:T(8,128)(2,1)S(1)}, bf16[216,256]{1,0:T(8,128)(2,1)S(1)}, u32[]{:S(2)}, u32[]{:S(2)}) collective-permute-start(bf16[216,256]{1,0:T(8,128)(2,1)S(1)} %fusion.5), channel_id=1, source_target_pairs={{0,24},{8,0},{16,8},{24,16},{1,25},{9,1},{17,9},{25,17},{2,26},{10... | collective-permute-start | bytes 331784 | tf_op jit(solution)/shard_map/ppermute | solution.py:60
  134.9 9.9 %collective-permute-start.19 = (bf16[216,256]{1,0:T(8,128)(2,1)S(1)}, bf16[216,256]{1,0:T(8,128)(2,1)S(1)}, u32[]{:S(2)}, u32[]{:S(2)}) collective-permute-start(bf16[216,256]{1,0:T(8,128)(2,1)S(1)} %fusion.5), channel_id=1, source_target_pairs={{0,16},{8,24},{16,0},{24,8},{1,17},{9,25},{17,1},{25,9},{2,18},{10... | collective-permute-start | bytes 331784 | tf_op jit(solution)/shard_map/ppermute | solution.py:60
  136.6 8.3 %collective-permute-start.20 = (bf16[216,256]{1,0:T(8,128)(2,1)S(1)}, bf16[216,256]{1,0:T(8,128)(2,1)S(1)}, u32[]{:S(2)}, u32[]{:S(2)}) collective-permute-start(bf16[216,256]{1,0:T(8,128)(2,1)S(1)} %fusion.5), channel_id=1, source_target_pairs={{0,8},{8,16},{16,24},{24,0},{1,9},{9,17},{17,25},{25,1},{2,10},{10... | collective-permute-start | bytes 331784 | tf_op jit(solution)/shard_map/ppermute | solution.py:60
  (5 other events, 39.4 us)

commit v2 on v1

v2 whole, which is shorter than its diff:
```python
import functools

import jax
import jax.numpy as jnp
from jax import lax
from jax.experimental import pallas as pl
from jax.experimental.pallas import tpu as pltpu
from jax.sharding import PartitionSpec as P

EPSILON = 1e-06
AXES = ("ta", "ha", "wa")
BF16 = jnp.bfloat16
F32 = jnp.float32
VMEM_LIMIT = 48 * 1024 * 1024


def dot(a, b):
    return jnp.dot(a, b, preferred_element_type=F32)


def dot_t(a, b):
    return lax.dot_general(a, b, (((1,), (1,)), ((), ())), preferred_element_type=F32)


def call(kernel, out_shape, flops, moved, scratch=(), scalars=0, arrays=0):
    specs = [pl.BlockSpec(memory_space=pltpu.SMEM)] * scalars
    specs += [pl.BlockSpec(memory_space=pltpu.VMEM)] * arrays
    return pl.pallas_call(
        kernel,
        out_shape=out_shape,
        in_specs=specs,
        scratch_shapes=list(scratch),
        compiler_params=pltpu.CompilerParams(vmem_limit_bytes=VMEM_LIMIT),
        cost_estimate=pl.CostEstimate(flops=flops, bytes_accessed=moved, transcendentals=0),
    )


def shift_line(array, axis, by):
    length = lax.axis_size(axis)
    pairs = [(i, i + by) for i in range(length) if 0 <= i + by < length]
    return lax.ppermute(array, axis, pairs)


def swap_core(array):
    length = lax.axis_size("ha")
    return lax.ppermute(array, "ha", [(i, i ^ 1) for i in range(length)])


def to_chip(array, du, dw):
    chips, width = lax.axis_size("ha") // 2, lax.axis_size("wa")
    pairs = []
    for u in range(chips):
        for core in range(2):
            for w in range(width):
                source = (2 * u + core) * width + w
                target = (2 * ((u + du) % chips) + core) * width + (w + dw) % width
                pairs.append((source, target))
    return lax.ppermute(array, ("ha", "wa"), pairs)


def ring(array, axis, by):
    length = lax.axis_size(axis)
    return lax.ppermute(array, axis, [(i, (i + by) % length) for i in range(length)])


CORNERS = 16


def prepare_kernel(x_ref, cot_ref, gain_ref, act_ref, act_t_ref, up_ref, down_ref, lefts, rights):
    frames, height, width, channels = x_ref.shape
    values = x_ref[...].reshape(-1, channels).astype(F32)
    inverse = lax.rsqrt(jnp.mean(values * values, axis=-1, keepdims=True) + EPSILON)
    normed = values * inverse * gain_ref[...]
    activated = (normed * jax.nn.sigmoid(normed)).astype(BF16)
    act_ref[...] = activated.reshape(x_ref.shape)
    act_t_ref[...] = activated.T
    for place, source in enumerate((cot_ref, act_ref)):
        up_ref[place] = source[:, 0]
        down_ref[place] = source[:, height - 1]
        cells = source[...].astype(F32)
        lefts[place] = cells[:, :, 0, :].astype(BF16)
        rights[place] = cells[:, :, width - 1, :].astype(BF16)


def columns_kernel(lefts, rights, above, below, to_left, to_right):
    _, frames, _, channels = lefts.shape
    width = above.shape[2]
    nothing = jnp.zeros((2, frames, CORNERS - 2, channels), F32)
    for source, target, at in ((lefts, to_left, 0), (rights, to_right, width - 1)):
        over = above[...].astype(F32)[:, :, at : at + 1, :]
        under = below[...].astype(F32)[:, :, at : at + 1, :]
        parts = [source[...].astype(F32), over, under, nothing]
        target[...] = jnp.concatenate(parts, axis=2).astype(BF16)


def halves(core, values, chips):
    block = values.shape[-1] // (2 * chips)
    values = values.astype(F32)
    first, second = (
        jnp.concatenate(
            [
                values[..., (2 * u + which) * block : (2 * u + which + 1) * block]
                for u in range(chips)
            ],
            axis=-1,
        )
        for which in range(2)
    )
    own = jnp.where(core == 0, first, second)
    other = jnp.where(core == 0, second, first)
    return own.astype(BF16), other.astype(BF16)


def bundle_kernel(chips, core_ref, cot, above, below, left, right, cot_edges, act_edges, mine, send):
    core = core_ref[0]
    inner = cot.shape[1]
    for place, target in enumerate((cot_edges, act_edges)):
        target[...] = jnp.concatenate(
            [ref[place] for ref in (above, below, left, right)], axis=1
        )
    mine[:, :inner], send[:, :inner] = halves(core, cot[...], chips)
    mine[:, inner:], send[:, inner:] = halves(core, cot_edges[...], chips)


def later_kernel(chips, core_ref, cot, cot_edges, mine, send):
    core = core_ref[0]
    inner = cot.shape[1]
    mine[:, :inner], send[:, :inner] = halves(core, cot[...], chips)
    mine[:, inner:], send[:, inner:] = halves(core, cot_edges[...], chips)


def spread_frame(center, edges, height, width, target, at):
    channels = center.shape[-1]
    tall = height + CORNERS
    above, below = edges[:width], edges[width : 2 * width]
    rows = jnp.concatenate([above, center, below], axis=0)
    target[1, at : at + (height + 2) * width, :] = rows
    rows = rows.astype(F32).reshape(height + 2, width, channels)
    place = lax.broadcasted_iota(jnp.int32, rows.shape, 1)
    for k, start, edge, by in ((0, 2 * width, 0, 1), (2, 2 * width + tall, width - 1, width - 1)):
        column = edges[start : start + tall].astype(F32)
        column = jnp.concatenate(
            [column[height : height + 1], column[:height], column[height + 1 : height + 2]], axis=0
        )
        moved = jnp.where(place == edge, column[:, None, :], pltpu.roll(rows, by, 1))
        target[k, at : at + (height + 2) * width, :] = moved.astype(BF16).reshape(-1, channels)


def taps_kernel(height, width, offset, frames, *refs):
    places, act_a, act_b, *rest = refs
    count = places.shape[0]
    terms_ref, spread_a, spread_b = rest[-3:]
    outs = rest[-3 - count : -3]
    bundles = rest[: -3 - count]
    inner = height * width
    spreads = (spread_a, spread_b)
    step = (height + 2) * width
    for side, spread in enumerate(spreads):
        for t in range(frames):
            at = t + 2 - offset
            ref = bundles[side] if at < frames else bundles[2 + side]
            frame = ref[at % frames]
            spread_frame(frame[:inner], frame[inner:], height, width, spread, t * step)
    acts = jnp.concatenate([act_a[...], act_b[...]], axis=1)
    part = terms_ref.shape[1]

    def shifted(tap):
        j, k = divmod(tap, 3)
        pieces = []
        for spread in spreads:
            for t in range(frames):
                start = t * step + (2 - j) * width
                pieces.append(spread[2 - k, start : start + inner, :])
        return jnp.concatenate(pieces, axis=0)

    for first in range(0, 9, 2):
        taps = range(first, min(first + 2, 9))
        terms = dot(acts, jnp.concatenate([shifted(tap) for tap in taps], axis=1)).T
        for place, tap in enumerate(taps):
            terms_ref[tap] = terms[place * part : (place + 1) * part]
    owned = part // count
    for place, out in enumerate(outs):
        start = pl.multiple_of(places[place] * owned, owned)
        out[...] = terms_ref[:, pl.ds(start, owned), :].astype(out.dtype)


def conv_sum(height, width, frames, spread, weight, backward):
    total = None
    for i in range(3):
        for j in range(3):
            at_t, at_h = (2 - i, 2 - j) if backward else (i, j)
            columns = []
            for k in range(3):
                at_w = 2 - k if backward else k
                pieces = []
                for t in range(frames):
                    start = ((t + at_t) * (height + 2) + at_h) * width
                    pieces.append(spread[at_w, start : start + height * width, :])
                columns.append(jnp.concatenate(pieces, axis=0))
            left = jnp.concatenate(columns, axis=1)
            if backward:
                term = dot_t(left, jnp.concatenate([weight[i, j, k] for k in range(3)], axis=1))
            else:
                term = dot(left, jnp.concatenate([weight[i, j, k] for k in range(3)], axis=0))
            total = term if total is None else total + term
    return total


def spread_all(height, width, parts, spread):
    at = 0
    for center, edges in parts:
        for t in range(center.shape[0]):
            spread_frame(center[t], edges[t], height, width, spread, at)
            at += (height + 2) * width


def forward_kernel(height, width, x_ref, act, edges, earlier, earlier_edges, weight, out, spread):
    frames = act.shape[0]
    spread_all(height, width, ((earlier, earlier_edges), (act, edges)), spread)
    mixed = conv_sum(height, width, frames, spread, weight, False)
    out[...] = (x_ref[...].astype(F32) + mixed).astype(BF16)


def backward_kernel(
    height, width, x_ref, gain_ref, cot, edges, later, later_edges, weight, out, spread
):
    frames = cot.shape[0]
    spread_all(height, width, ((cot, edges), (later, later_edges)), spread)
    grad_act = conv_sum(height, width, frames, spread, weight, True)
    values = x_ref[...].astype(F32)
    inverse = lax.rsqrt(jnp.mean(values * values, axis=-1, keepdims=True) + EPSILON)
    unit_rms = values * inverse
    gain = gain_ref[...]
    normed = unit_rms * gain
    logistic = jax.nn.sigmoid(normed)
    grad_unit = grad_act * logistic * (1.0 + normed * (1.0 - logistic)) * gain
    grad_norm = inverse * (
        grad_unit - unit_rms * jnp.mean(grad_unit * unit_rms, axis=-1, keepdims=True)
    )
    out[...] = (cot[...].reshape(out.shape).astype(F32) + grad_norm).astype(BF16)


def shape_of(*dims, dtype=BF16):
    return jax.ShapeDtypeStruct(dims, dtype)


def body(features, norm_gain, conv_weight, cotangent):
    frames, height, width, channels = features.shape
    inner = height * width
    cells = frames * inner
    depth, rows_of, cols_of = (lax.axis_size(axis) for axis in AXES)
    chips = rows_of // 2
    owned = channels // (rows_of * cols_of)
    half = channels // 2
    me_t, me_h, me_w = (lax.axis_index(axis) for axis in AXES)
    core, chip = (me_h % 2).astype(jnp.int32).reshape(1), me_h // 2
    flat_x = features.reshape(cells, channels)
    framed_cot = cotangent.reshape(frames, inner, channels)
    gain = norm_gain.reshape(1, channels)
    product = 2 * cells * channels * channels
    size = 2 * cells * channels
    tall = height + CORNERS
    around = 2 * width + 2 * tall

    act, act_t, up, down, lefts, rights = call(
        prepare_kernel,
        (
            shape_of(*features.shape),
            shape_of(channels, cells),
            shape_of(2, frames, width, channels),
            shape_of(2, frames, width, channels),
            shape_of(2, frames, height, channels),
            shape_of(2, frames, height, channels),
        ),
        10 * cells * channels,
        4 * size,
        arrays=3,
    )(features, cotangent, gain)
    framed_act = act.reshape(frames, inner, channels)
    above = shift_line(down, "ha", 1)
    below = shift_line(up, "ha", -1)
    later = shift_line(framed_cot[:2], "ta", -1)
    act_t_other = swap_core(act_t)
    to_left, to_right = call(
        columns_kernel, (shape_of(2, frames, tall, channels),) * 2, 0, size // 2, arrays=4
    )(lefts, rights, above, below)
    left = shift_line(to_right, "wa", 1)
    right = shift_line(to_left, "wa", -1)
    cot_edges, act_edges, mine, send = call(
        functools.partial(bundle_kernel, chips),
        (shape_of(frames, around, channels),) * 2 + (shape_of(frames, inner + around, half),) * 2,
        0,
        3 * size,
        scalars=1,
        arrays=5,
    )(core, framed_cot, above, below, left, right)
    others = swap_core(send)
    later_edges = shift_line(cot_edges[:2], "ta", -1)
    mine_later, send_later = call(
        functools.partial(later_kernel, chips),
        (shape_of(2, inner + around, half),) * 2,
        0,
        2 * size,
        scalars=1,
        arrays=2,
    )(core, later, later_edges)
    others_later = swap_core(send_later)
    earlier = shift_line(framed_act[frames - 2 :], "ta", 1)
    earlier_edges = shift_line(act_edges[frames - 2 :], "ta", 1)

    count = chips * cols_of
    moves = [(du, dw) for du in range(chips) for dw in range(cols_of)]
    places = jnp.stack(
        [((chip + du) % chips) * cols_of + (me_w + dw) % cols_of for du, dw in moves]
    ).astype(jnp.int32)
    spread = pltpu.VMEM((3, frames * (height + 2) * width, half), BF16)
    scratch = (pltpu.VMEM((9, half, channels), F32), spread, spread)
    scale = float(cells * depth * rows_of * cols_of) ** (-0.5)

    def part_of(array, place):
        return lax.dynamic_index_in_dim(array, place, axis=0, keepdims=False)

    gradients = [None] * 3
    for offset in (2, 1, 0):
        bundles = (mine, others) + ((mine_later, others_later) if offset < 2 else ())
        pieces = call(
            functools.partial(taps_kernel, height, width, offset, frames),
            tuple(
                shape_of(9, owned, channels, dtype=F32 if place == 0 else BF16)
                for place in range(count)
            ),
            9 * product,
            4 * size,
            scratch,
            scalars=1,
            arrays=2 + len(bundles),
        )(places, act_t, act_t_other, *bundles)
        total = pieces[0]
        for piece, (du, dw) in zip(pieces[1:], moves[1:]):
            total = total + to_chip(piece, du, dw).astype(F32)
        total = total.reshape(depth, -1, channels)
        rounded = total.astype(BF16)
        piece = part_of(total, me_t)
        for by in range(1, depth):
            piece = piece + ring(part_of(rounded, (me_t + by) % depth), "ta", by).astype(F32)
        piece = (piece * scale).astype(BF16)
        gathered = [ring(piece, "ta", by) for by in range(depth - 1, 0, -1)] + [piece]
        gathered = jnp.roll(jnp.stack(gathered), me_t + 1, axis=0)
        gradients[offset] = gathered.reshape(9, owned, channels)
    grad_weight = jnp.swapaxes(jnp.concatenate(gradients), 1, 2).astype(F32)
    grad_weight = grad_weight.reshape(3, 3, 3, channels, owned)

    spread = pltpu.VMEM((3, (frames + 2) * (height + 2) * width, channels), BF16)
    moved = conv_weight.size * 2 + 4 * size
    decoded = call(
        functools.partial(forward_kernel, height, width),
        shape_of(cells, channels),
        27 * product,
        moved,
        (spread,),
        arrays=6,
    )(flat_x, framed_act, act_edges, earlier, earlier_edges, conv_weight)
    grad_features = call(
        functools.partial(backward_kernel, height, width),
        shape_of(cells, channels),
        27 * product,
        moved,
        (spread,),
        arrays=7,
    )(flat_x, gain, framed_cot, cot_edges, later, later_edges, conv_weight)
    return (
        decoded.reshape(features.shape),
        grad_features.reshape(features.shape),
        grad_weight,
    )


def solution(mesh):
    placed = (P("ta", "ha", "wa", None), P(), P(), P("ta", "ha", "wa", None))
    return jax.shard_map(
        body,
        mesh=mesh,
        in_specs=placed,
        out_specs=(
            P("ta", "ha", "wa", None),
            P("ta", "ha", "wa", None),
            P(None, None, None, None, ("ha", "wa")),
        ),
        check_vma=False,
    )
```

time: 147 us -> 100 us (0.68)
  waiting for transfers between devices: 47.1 us -> 11.7 us
  starting transfers between devices: 35.2 us -> 59.5 us
  local copies, waits for them, and re-layouts: 30.5 us -> 7.33 us
  other arithmetic: 12.3 us -> 1.93 us
    slice x11 -> x4, local copies, waits for them, and re-layouts: 20.5 us -> 1.46 us  [the longest x1 0.72 us: body(): later = shift_line(framed_cot[:2], 'ta', -1)]
    ppermute x6 -> x18, starting transfers between devices: 8.3 us -> 26.4 us  [ring(): lax.ppermute(array, axis, [(i, (i + by) % length) for i in range(length)])]
    ppermute x3 -> x9, waiting for transfers between devices: 18.6 us -> 3.59 us  [to_chip(): return lax.ppermute(array, ('ha', 'wa'), pairs)]
    ppermute x10 -> x8, waiting for transfers between devices: 16.7 us -> 3.08 us  [shift_line(): return lax.ppermute(array, axis, pairs)]
    ppermute x3 -> x9, starting transfers between devices: 3.63 us -> 11.3 us  [to_chip(): return lax.ppermute(array, ('ha', 'wa'), pairs)]
    ppermute x6 -> x18, waiting for transfers between devices: 11.9 us -> 4.99 us  [ring(): lax.ppermute(array, axis, [(i, (i + by) % length) for i in range(length)])]
    select_n x2 -> x0, local copies, waits for them, and re-layouts: 5.22 us -> none  [half_of(): return jnp.where(which == 0, first, second)]
    concatenate x4 -> x3, other arithmetic: 5.37 us -> 0.54 us  [body(): gathered = jnp.roll(jnp.stack(gathered), me_t + 1, axis=0)]
  transfers between devices with their start and end apart: 21 -> 38, of which waited for: 10 -> 7; matrix products, arithmetic and copies ran while one was open for 24% -> 2% of each run, Pallas kernels for 14% -> 18%
where the time goes in v2:
time: 100 us
  starting transfers between devices  59.5 us (60%)
  Pallas kernels  18.6 us (19%)
  waiting for transfers between devices  11.7 us (12%)
  local copies, waits for them, and re-layouts  7.33 us (7%)
  other arithmetic  1.93 us (2%)
  between operations  1.01 us (1%)
    ppermute x18, starting transfers between devices, ring(): lax.ppermute(array, axis, [(i, (i + by) % length) for i in range(length)])  26.4 us
    ppermute x8, starting transfers between devices, shift_line(): return lax.ppermute(array, axis, pairs)  19 us
    ppermute x9, starting transfers between devices, to_chip(): return lax.ppermute(array, ('ha', 'wa'), pairs)  11.3 us
    pallas_call x3, Pallas kernels, body(): call(functools.partial(taps_kernel, height, width, offset, frames), tuple...  6.93 us
    unnamed x18, local copies, waits for them, and re-layouts  5.81 us
    pallas_call x1, Pallas kernels, body(): call(functools.partial(backward_kernel, height, width), shape_of(cells, c...  5.05 us
    ppermute x18, waiting for transfers between devices, ring(): lax.ppermute(array, axis, [(i, (i + by) % length) for i in range(length)])  4.99 us
    pallas_call x1, Pallas kernels, body(): call(functools.partial(forward_kernel, height, width), shape_of(cells, ch...  4.66 us
  transfers between devices with their start and end apart: 38, of which 7 were waited for; matrix products, arithmetic and copies ran while one was open for 2% of the time, Pallas kernels for 18%

profile of v2, /device:TPU:0, one launch (start us, length us, event | category | flops | bytes accessed | tf_op | source)
XLA Modules:
  0.0 100.0 jit_solution(4355183759496580034)
XLA Ops:
  4.1 2.4 %collective-permute-start = (bf16[2,4,16,256]{3,2,1,0:T(8,128)(2,1)S(1)}, bf16[2,4,16,256]{3,2,1,0:T(8,128)(2,1)S(1)}, u32[]{:S(2)}, u32[]{:S(2)}) collective-permute-start(bf16[2,4,16,256]{3,2,1,0:T(8,128)(2,1)S(1)} %get-tuple-element.31), channel_id=1, source_target_pairs={{0,2},{2,4},{4,6},{1,3},{3,5},{5,7},{8,10},{10,12},{12,14},{9,11},... | collective-permute-start | bytes 196616 | tf_op jit(solution)/shard_map/ppermute | solution.py:41
  9.8 1.9 %collective-permute-done.1.below = bf16[2,4,16,256]{3,2,1,0:T(8,128)(2,1)S(1)} collective-permute-done((bf16[2,4,16,256]{3,2,1,0:T(8,128)(2,1)S(1)}, bf16[2,4,16,256]{3,2,1,0:T(8,128)(2,1)S(1)}, u32[]{:S(2)}, u32[]{:S(2)}) %collective-permute-start.1) | collective-permute-done | bytes 65568 | tf_op jit(solution)/shard_map/ppermute | solution.py:41
  12.5 3.4 %collective-permute-start.2 = (bf16[2,4,32,256]{3,2,1,0:T(8,128)(2,1)}, bf16[2,4,32,256]{3,2,1,0:T(8,128)(2,1)S(1)}, u32[]{:S(2)}, u32[]{:S(2)}) collective-permute-start(bf16[2,4,32,256]{3,2,1,0:T(8,128)(2,1)} %get-tuple-element.35), channel_id=1, source_target_pairs={{0,1},{2,3},{4,5},{6,7},{8,9},{10,11},{12,13},{14,15},{16,17},{18,... | collective-permute-start | bytes 393224 | tf_op jit(solution)/shard_map/ppermute | solution.py:41
  17.9 3.5 %collective-permute-start.4 = (bf16[2,256,256]{2,1,0:T(8,128)(2,1)}, bf16[2,256,256]{2,1,0:T(8,128)(2,1)S(1)}, u32[]{:S(2)}, u32[]{:S(2)}) collective-permute-start(bf16[2,256,256]{2,1,0:T(8,128)(2,1)} %bitcast.5), channel_id=1, source_target_pairs={{0,8},{8,16},{16,24},{1,9},{9,17},{17,25},{2,10},{10,18},{18,26},{... | collective-permute-start | bytes 786440 | tf_op jit(solution)/shard_map/ppermute | solution.py:41
  21.4 2.4 %collective-permute-start.8 = (bf16[256,1024]{1,0:T(8,128)(2,1)S(1)}, bf16[256,1024]{1,0:T(8,128)(2,1)S(1)}, u32[]{:S(2)}, u32[]{:S(2)}) collective-permute-start(bf16[256,1024]{1,0:T(8,128)(2,1)S(1)} %get-tuple-element.39.refs_1_), channel_id=1, source_target_pairs={{0,2},{2,0},{4,6},{6,4},{1,3},{3,1},{5,7},{7,5},{8,10},{10,8},{12,... | collective-permute-start | bytes 1572872 | tf_op jit(solution)/shard_map/ppermute | solution.py:46
  26.7 4.6 %collective-permute-start.5 = (bf16[2,96,256]{2,1,0:T(8,128)(2,1)S(1)}, bf16[2,96,256]{2,1,0:T(8,128)(2,1)S(1)}, u32[]{:S(2)}, u32[]{:S(2)}) collective-permute-start(bf16[2,96,256]{2,1,0:T(8,128)(2,1)S(1)} %slice.20), channel_id=1, source_target_pairs={{0,8},{8,16},{16,24},{1,9},{9,17},{17,25},{2,10},{10,18},{18,26},{... | collective-permute-start | bytes 294920 | tf_op jit(solution)/shard_map/ppermute | solution.py:41
  32.9 2.0 %copy-done.7 = bf16[3,3,3,256,256]{4,3,2,1,0:T(8,128)(2,1)S(1)} copy-done((bf16[3,3,3,256,256]{4,3,2,1,0:T(8,128)(2,1)S(1)}, bf16[3,3,3,256,256]{4,3,2,1,0:T(8,128)(2,1)}, u32[]{:S(2)}) %copy-start.7) | copy-done | bytes 3538968
  34.9 5.0 %shard_map.71 = bf16[1024,256]{1,0:T(8,128)(2,1)} custom-call(bf16[1024,256]{1,0:T(8,128)(2,1)S(1)} %bitcast.84, f32[1,256]{1,0:T(1,128)S(1)} %bitcast.88, bf16[4,256,256]{2,1,0:T(8,128)(2,1)S(1)} %bitcast.83, bf16[4,96,256]{2,1,0:T(8,128)(2,1)S(1)} %get-tuple-element.38.edges, bf16[2,256,256]{2,1,0:T(8,128)(2,1)S(1)} %collective-permute-done.6.later.cot, ...), custom_call_target="tpu_custom_call" | custom-call | flops 3623878656 | bytes 5636096 | tf_op jit(solution)/shard_map/pallas_call | solution.py:363
  40.0 4.7 %shard_map.70 = bf16[1024,256]{1,0:T(8,128)(2,1)} custom-call(bf16[1024,256]{1,0:T(8,128)(2,1)S(1)} %bitcast.85, bf16[4,256,256]{2,1,0:T(8,128)(2,1)S(1)} %bitcast.86, bf16[4,96,256]{2,1,0:T(8,128)(2,1)S(1)} %get-tuple-element.37.edges, bf16[2,256,256]{2,1,0:T(8,128)(2,1)S(1)} %collective-permute-done.4.earlier, ...), custom_call_target="tpu_custom_call" | custom-call | flops 3623878656 | bytes 5636096 | tf_op jit(solution)/shard_map/pallas_call | solution.py:355
  44.7 2.3 %shard_map.75 = (f32[9,32,256]{2,1,0:T(8,128)S(1)}, bf16[9,32,256]{2,1,0:T(8,128)(2,1)S(1)}, bf16[9,32,256]{2,1,0:T(8,128)(2,1)S(1)}, bf16[9,32,256]{2,1,0:T(8,128)(2,1)S(1)}) custom-call(s32[4]{0:T(128)S(1)} %pad_add_fusion.refs_0_, bf16[256,1024]{1,0:T(8,128)(2,1)S(1)} %get-tuple-element.39.refs_1_, bf16[256,1024]{1,0:T(8,128)(2,1)S(1)} %collective-permute-done.8.refs_2_, ...), custom_call_target="tpu_custom_call" | custom-call | flops 1207959552 | bytes 2097152 | tf_op jit(solution)/shard_map/pallas_call | solution.py:326
  47.0 3.5 %collective-permute-start.31 = (bf16[9,32,256]{2,1,0:T(8,128)(2,1)S(1)}, bf16[9,32,256]{2,1,0:T(8,128)(2,1)S(1)}, u32[]{:S(2)}, u32[]{:S(2)}) collective-permute-start(bf16[9,32,256]{2,1,0:T(8,128)(2,1)S(1)} %get-tuple-element.55), channel_id=1, source_target_pairs={{0,5},{1,4},{2,7},{3,6},{4,1},{5,0},{6,3},{7,2},{8,13},{9,12},{10,... | collective-permute-start | bytes 442376 | tf_op jit(solution)/shard_map/ppermute | solution.py:58
  51.1 2.3 %shard_map.74 = (f32[9,32,256]{2,1,0:T(8,128)S(1)}, bf16[9,32,256]{2,1,0:T(8,128)(2,1)S(1)}, bf16[9,32,256]{2,1,0:T(8,128)(2,1)S(1)}, bf16[9,32,256]{2,1,0:T(8,128)(2,1)S(1)}) custom-call(s32[4]{0:T(128)S(1)} %pad_add_fusion.refs_0_, bf16[256,1024]{1,0:T(8,128)(2,1)S(1)} %get-tuple-element.39.refs_1_, bf16[256,1024]{1,0:T(8,128)(2,1)S(1)} %collective-permute-done.8.refs_2_, ...), custom_call_target="tpu_custom_call" | custom-call | flops 1207959552 | bytes 2097152 | tf_op jit(solution)/shard_map/pallas_call | solution.py:326
  53.5 2.9 %collective-permute-start.22 = (bf16[9,32,256]{2,1,0:T(8,128)(2,1)S(1)}, bf16[9,32,256]{2,1,0:T(8,128)(2,1)S(1)}, u32[]{:S(2)}, u32[]{:S(2)}) collective-permute-start(bf16[9,32,256]{2,1,0:T(8,128)(2,1)S(1)} %get-tuple-element.51), channel_id=1, source_target_pairs={{0,5},{1,4},{2,7},{3,6},{4,1},{5,0},{6,3},{7,2},{8,13},{9,12},{10,... | collective-permute-start | bytes 442376 | tf_op jit(solution)/shard_map/ppermute | solution.py:58
  56.4 2.3 %shard_map.73 = (f32[9,32,256]{2,1,0:T(8,128)S(1)}, bf16[9,32,256]{2,1,0:T(8,128)(2,1)S(1)}, bf16[9,32,256]{2,1,0:T(8,128)(2,1)S(1)}, bf16[9,32,256]{2,1,0:T(8,128)(2,1)S(1)}) custom-call(s32[4]{0:T(128)S(1)} %pad_add_fusion.refs_0_, bf16[256,1024]{1,0:T(8,128)(2,1)S(1)} %get-tuple-element.39.refs_1_, bf16[256,1024]{1,0:T(8,128)(2,1)S(1)} %collective-permute-done.8.refs_2_, ...), custom_call_target="tpu_custom_call" | custom-call | flops 1207959552 | bytes 2097152 | tf_op jit(solution)/shard_map/pallas_call | solution.py:326
  59.4 2.8 %collective-permute-start.13 = (bf16[9,32,256]{2,1,0:T(8,128)(2,1)S(1)}, bf16[9,32,256]{2,1,0:T(8,128)(2,1)S(1)}, u32[]{:S(2)}, u32[]{:S(2)}) collective-permute-start(bf16[9,32,256]{2,1,0:T(8,128)(2,1)S(1)} %get-tuple-element.47), channel_id=1, source_target_pairs={{0,5},{1,4},{2,7},{3,6},{4,1},{5,0},{6,3},{7,2},{8,13},{9,12},{10,... | collective-permute-start | bytes 442376 | tf_op jit(solution)/shard_map/ppermute | solution.py:58
  64.4 1.6 %collective-permute-start.34 = (bf16[72,256]{1,0:T(8,128)(2,1)S(1)}, bf16[72,256]{1,0:T(8,128)(2,1)S(1)}, u32[]{:S(2)}, u32[]{:S(2)}) collective-permute-start(bf16[72,256]{1,0:T(8,128)(2,1)S(1)} %get-tuple-element.63), channel_id=1, source_target_pairs={{0,24},{8,0},{16,8},{24,16},{1,25},{9,1},{17,9},{25,17},{2,26},{10... | collective-permute-start | bytes 110600 | tf_op jit(solution)/shard_map/ppermute | solution.py:63
  65.9 2.3 %collective-permute-done.20 = bf16[9,32,256]{2,1,0:T(8,128)(2,1)S(1)} collective-permute-done((bf16[9,32,256]{2,1,0:T(8,128)(2,1)S(1)}, bf16[9,32,256]{2,1,0:T(8,128)(2,1)S(1)}, u32[]{:S(2)}, u32[]{:S(2)}) %collective-permute-start.20) | collective-permute-done | bytes 147488 | tf_op jit(solution)/shard_map/ppermute | solution.py:58
  68.2 2.6 %collective-permute-start.33 = (bf16[72,256]{1,0:T(8,128)(2,1)S(1)}, bf16[72,256]{1,0:T(8,128)(2,1)S(1)}, u32[]{:S(2)}, u32[]{:S(2)}) collective-permute-start(bf16[72,256]{1,0:T(8,128)(2,1)S(1)} %get-tuple-element.64), channel_id=1, source_target_pairs={{0,16},{8,24},{16,0},{24,8},{1,17},{9,25},{17,1},{25,9},{2,18},{10... | collective-permute-start | bytes 110600 | tf_op jit(solution)/shard_map/ppermute | solution.py:63
  71.0 3.8 %collective-permute-start.25 = (bf16[72,256]{1,0:T(8,128)(2,1)S(1)}, bf16[72,256]{1,0:T(8,128)(2,1)S(1)}, u32[]{:S(2)}, u32[]{:S(2)}) collective-permute-start(bf16[72,256]{1,0:T(8,128)(2,1)S(1)} %get-tuple-element.60), channel_id=1, source_target_pairs={{0,24},{8,0},{16,8},{24,16},{1,25},{9,1},{17,9},{25,17},{2,26},{10... | collective-permute-start | bytes 110600 | tf_op jit(solution)/shard_map/ppermute | solution.py:63
  75.7 3.2 %collective-permute-start.16 = (bf16[72,256]{1,0:T(8,128)(2,1)S(1)}, bf16[72,256]{1,0:T(8,128)(2,1)S(1)}, u32[]{:S(2)}, u32[]{:S(2)}) collective-permute-start(bf16[72,256]{1,0:T(8,128)(2,1)S(1)} %get-tuple-element.57), channel_id=1, source_target_pairs={{0,24},{8,0},{16,8},{24,16},{1,25},{9,1},{17,9},{25,17},{2,26},{10... | collective-permute-start | bytes 110600 | tf_op jit(solution)/shard_map/ppermute | solution.py:63
  80.2 3.8 %collective-permute-start.35 = (bf16[72,256]{1,0:T(8,128)(2,1)S(1)}, bf16[72,256]{1,0:T(8,128)(2,1)S(1)}, u32[]{:S(2)}, u32[]{:S(2)}) collective-permute-start(bf16[72,256]{1,0:T(8,128)(2,1)S(1)} %fusion.24), channel_id=1, source_target_pairs={{0,24},{8,0},{16,8},{24,16},{1,25},{9,1},{17,9},{25,17},{2,26},{10... | collective-permute-start | bytes 110600 | tf_op jit(solution)/shard_map/ppermute | solution.py:63
  84.6 3.2 %collective-permute-start.26 = (bf16[72,256]{1,0:T(8,128)(2,1)S(1)}, bf16[72,256]{1,0:T(8,128)(2,1)S(1)}, u32[]{:S(2)}, u32[]{:S(2)}) collective-permute-start(bf16[72,256]{1,0:T(8,128)(2,1)S(1)} %fusion.28), channel_id=1, source_target_pairs={{0,24},{8,0},{16,8},{24,16},{1,25},{9,1},{17,9},{25,17},{2,26},{10... | collective-permute-start | bytes 110600 | tf_op jit(solution)/shard_map/ppermute | solution.py:63
  89.1 3.7 %collective-permute-start.17 = (bf16[72,256]{1,0:T(8,128)(2,1)S(1)}, bf16[72,256]{1,0:T(8,128)(2,1)S(1)}, u32[]{:S(2)}, u32[]{:S(2)}) collective-permute-start(bf16[72,256]{1,0:T(8,128)(2,1)S(1)} %fusion.32), channel_id=1, source_target_pairs={{0,24},{8,0},{16,8},{24,16},{1,25},{9,1},{17,9},{25,17},{2,26},{10... | collective-permute-start | bytes 110600 | tf_op jit(solution)/shard_map/ppermute | solution.py:63
  95.0 2.7 %collective-permute-done.18 = bf16[72,256]{1,0:T(8,128)(2,1)S(1)} collective-permute-done((bf16[72,256]{1,0:T(8,128)(2,1)S(1)}, bf16[72,256]{1,0:T(8,128)(2,1)S(1)}, u32[]{:S(2)}, u32[]{:S(2)}) %collective-permute-start.18) | collective-permute-done | bytes 36896 | tf_op jit(solution)/shard_map/ppermute | solution.py:63
  (100 shorter events, 26.1 us)
Async XLA Ops:
  8.5 22.7 %collective-permute-start.6 = (bf16[2,256,256]{2,1,0:T(8,128)(2,1)}, bf16[2,256,256]{2,1,0:T(8,128)(2,1)S(1)}, u32[]{:S(2)}, u32[]{:S(2)}) collective-permute-start(bf16[2,256,256]{2,1,0:T(8,128)(2,1)} %bitcast.7), channel_id=1, source_target_pairs={{8,0},{16,8},{24,16},{9,1},{17,9},{25,17},{10,2},{18,10},{26,18},{... | collective-permute-start | bytes 786440 | tf_op jit(solution)/shard_map/ppermute | solution.py:41
  12.5 11.4 %collective-permute-start.2 = (bf16[2,4,32,256]{3,2,1,0:T(8,128)(2,1)}, bf16[2,4,32,256]{3,2,1,0:T(8,128)(2,1)S(1)}, u32[]{:S(2)}, u32[]{:S(2)}) collective-permute-start(bf16[2,4,32,256]{3,2,1,0:T(8,128)(2,1)} %get-tuple-element.35), channel_id=1, source_target_pairs={{0,1},{2,3},{4,5},{6,7},{8,9},{10,11},{12,13},{14,15},{16,17},{18,... | collective-permute-start | bytes 393224 | tf_op jit(solution)/shard_map/ppermute | solution.py:41
  15.9 8.0 %collective-permute-start.3 = (bf16[2,4,32,256]{3,2,1,0:T(8,128)(2,1)}, bf16[2,4,32,256]{3,2,1,0:T(8,128)(2,1)S(1)}, u32[]{:S(2)}, u32[]{:S(2)}) collective-permute-start(bf16[2,4,32,256]{3,2,1,0:T(8,128)(2,1)} %get-tuple-element.36), channel_id=1, source_target_pairs={{1,0},{3,2},{5,4},{7,6},{9,8},{11,10},{13,12},{15,14},{17,16},{19,... | collective-permute-start | bytes 393224 | tf_op jit(solution)/shard_map/ppermute | solution.py:41
  17.9 22.1 %collective-permute-start.4 = (bf16[2,256,256]{2,1,0:T(8,128)(2,1)}, bf16[2,256,256]{2,1,0:T(8,128)(2,1)S(1)}, u32[]{:S(2)}, u32[]{:S(2)}) collective-permute-start(bf16[2,256,256]{2,1,0:T(8,128)(2,1)} %bitcast.5), channel_id=1, source_target_pairs={{0,8},{8,16},{16,24},{1,9},{9,17},{17,25},{2,10},{10,18},{18,26},{... | collective-permute-start | bytes 786440 | tf_op jit(solution)/shard_map/ppermute | solution.py:41
  21.4 23.3 %collective-permute-start.8 = (bf16[256,1024]{1,0:T(8,128)(2,1)S(1)}, bf16[256,1024]{1,0:T(8,128)(2,1)S(1)}, u32[]{:S(2)}, u32[]{:S(2)}) collective-permute-start(bf16[256,1024]{1,0:T(8,128)(2,1)S(1)} %get-tuple-element.39.refs_1_), channel_id=1, source_target_pairs={{0,2},{2,0},{4,6},{6,4},{1,3},{3,1},{5,7},{7,5},{8,10},{10,8},{12,... | collective-permute-start | bytes 1572872 | tf_op jit(solution)/shard_map/ppermute | solution.py:46
  26.7 13.3 %collective-permute-start.5 = (bf16[2,96,256]{2,1,0:T(8,128)(2,1)S(1)}, bf16[2,96,256]{2,1,0:T(8,128)(2,1)S(1)}, u32[]{:S(2)}, u32[]{:S(2)}) collective-permute-start(bf16[2,96,256]{2,1,0:T(8,128)(2,1)S(1)} %slice.20), channel_id=1, source_target_pairs={{0,8},{8,16},{16,24},{1,9},{9,17},{17,25},{2,10},{10,18},{18,26},{... | collective-permute-start | bytes 294920 | tf_op jit(solution)/shard_map/ppermute | solution.py:41
  31.2 13.4 %collective-permute-start.9 = (bf16[4,352,128]{2,1,0:T(8,128)(2,1)S(1)}, bf16[4,352,128]{2,1,0:T(8,128)(2,1)S(1)}, u32[]{:S(2)}, u32[]{:S(2)}) collective-permute-start(bf16[4,352,128]{2,1,0:T(8,128)(2,1)S(1)} %get-tuple-element.41), channel_id=1, source_target_pairs={{0,2},{2,0},{4,6},{6,4},{1,3},{3,1},{5,7},{7,5},{8,10},{10,8},{12,... | collective-permute-start | bytes 1081352 | tf_op jit(solution)/shard_map/ppermute | solution.py:46
  32.8 18.3 %collective-permute-start.10 = (bf16[2,352,128]{2,1,0:T(8,128)(2,1)S(1)}, bf16[2,352,128]{2,1,0:T(8,128)(2,1)S(1)}, u32[]{:S(2)}, u32[]{:S(2)}) collective-permute-start(bf16[2,352,128]{2,1,0:T(8,128)(2,1)S(1)} %get-tuple-element.43), channel_id=1, source_target_pairs={{0,2},{2,0},{4,6},{6,4},{1,3},{3,1},{5,7},{7,5},{8,10},{10,8},{12,... | collective-permute-start | bytes 540680 | tf_op jit(solution)/shard_map/ppermute | solution.py:46
  47.0 11.7 %collective-permute-start.31 = (bf16[9,32,256]{2,1,0:T(8,128)(2,1)S(1)}, bf16[9,32,256]{2,1,0:T(8,128)(2,1)S(1)}, u32[]{:S(2)}, u32[]{:S(2)}) collective-permute-start(bf16[9,32,256]{2,1,0:T(8,128)(2,1)S(1)} %get-tuple-element.55), channel_id=1, source_target_pairs={{0,5},{1,4},{2,7},{3,6},{4,1},{5,0},{6,3},{7,2},{8,13},{9,12},{10,... | collective-permute-start | bytes 442376 | tf_op jit(solution)/shard_map/ppermute | solution.py:58
  50.5 8.9 %collective-permute-start.30 = (bf16[9,32,256]{2,1,0:T(8,128)(2,1)S(1)}, bf16[9,32,256]{2,1,0:T(8,128)(2,1)S(1)}, u32[]{:S(2)}, u32[]{:S(2)}) collective-permute-start(bf16[9,32,256]{2,1,0:T(8,128)(2,1)S(1)} %get-tuple-element.54), channel_id=1, source_target_pairs={{0,4},{1,5},{2,6},{3,7},{4,0},{5,1},{6,2},{7,3},{8,12},{9,13},{10,... | collective-permute-start | bytes 442376 | tf_op jit(solution)/shard_map/ppermute | solution.py:58
  50.5 11.8 %collective-permute-start.29 = (bf16[9,32,256]{2,1,0:T(8,128)(2,1)S(1)}, bf16[9,32,256]{2,1,0:T(8,128)(2,1)S(1)}, u32[]{:S(2)}, u32[]{:S(2)}) collective-permute-start(bf16[9,32,256]{2,1,0:T(8,128)(2,1)S(1)} %get-tuple-element.53), channel_id=1, source_target_pairs={{0,1},{1,0},{2,3},{3,2},{4,5},{5,4},{6,7},{7,6},{8,9},{9,8},{10,11... | collective-permute-start | bytes 442376 | tf_op jit(solution)/shard_map/ppermute | solution.py:58
  53.5 8.9 %collective-permute-start.22 = (bf16[9,32,256]{2,1,0:T(8,128)(2,1)S(1)}, bf16[9,32,256]{2,1,0:T(8,128)(2,1)S(1)}, u32[]{:S(2)}, u32[]{:S(2)}) collective-permute-start(bf16[9,32,256]{2,1,0:T(8,128)(2,1)S(1)} %get-tuple-element.51), channel_id=1, source_target_pairs={{0,5},{1,4},{2,7},{3,6},{4,1},{5,0},{6,3},{7,2},{8,13},{9,12},{10,... | collective-permute-start | bytes 442376 | tf_op jit(solution)/shard_map/ppermute | solution.py:58
  56.4 8.0 %collective-permute-start.21 = (bf16[9,32,256]{2,1,0:T(8,128)(2,1)S(1)}, bf16[9,32,256]{2,1,0:T(8,128)(2,1)S(1)}, u32[]{:S(2)}, u32[]{:S(2)}) collective-permute-start(bf16[9,32,256]{2,1,0:T(8,128)(2,1)S(1)} %get-tuple-element.50), channel_id=1, source_target_pairs={{0,4},{1,5},{2,6},{3,7},{4,0},{5,1},{6,2},{7,3},{8,12},{9,13},{10,... | collective-permute-start | bytes 442376 | tf_op jit(solution)/shard_map/ppermute | solution.py:58
  58.7 9.5 %collective-permute-start.20 = (bf16[9,32,256]{2,1,0:T(8,128)(2,1)S(1)}, bf16[9,32,256]{2,1,0:T(8,128)(2,1)S(1)}, u32[]{:S(2)}, u32[]{:S(2)}) collective-permute-start(bf16[9,32,256]{2,1,0:T(8,128)(2,1)S(1)} %get-tuple-element.49), channel_id=1, source_target_pairs={{0,1},{1,0},{2,3},{3,2},{4,5},{5,4},{6,7},{7,6},{8,9},{9,8},{10,11... | collective-permute-start | bytes 442376 | tf_op jit(solution)/shard_map/ppermute | solution.py:58
  59.4 11.5 %collective-permute-start.13 = (bf16[9,32,256]{2,1,0:T(8,128)(2,1)S(1)}, bf16[9,32,256]{2,1,0:T(8,128)(2,1)S(1)}, u32[]{:S(2)}, u32[]{:S(2)}) collective-permute-start(bf16[9,32,256]{2,1,0:T(8,128)(2,1)S(1)} %get-tuple-element.47), channel_id=1, source_target_pairs={{0,5},{1,4},{2,7},{3,6},{4,1},{5,0},{6,3},{7,2},{8,13},{9,12},{10,... | collective-permute-start | bytes 442376 | tf_op jit(solution)/shard_map/ppermute | solution.py:58
  62.3 8.8 %collective-permute-start.12 = (bf16[9,32,256]{2,1,0:T(8,128)(2,1)S(1)}, bf16[9,32,256]{2,1,0:T(8,128)(2,1)S(1)}, u32[]{:S(2)}, u32[]{:S(2)}) collective-permute-start(bf16[9,32,256]{2,1,0:T(8,128)(2,1)S(1)} %get-tuple-element.46), channel_id=1, source_target_pairs={{0,4},{1,5},{2,6},{3,7},{4,0},{5,1},{6,2},{7,3},{8,12},{9,13},{10,... | collective-permute-start | bytes 442376 | tf_op jit(solution)/shard_map/ppermute | solution.py:58
  62.4 12.4 %collective-permute-start.11 = (bf16[9,32,256]{2,1,0:T(8,128)(2,1)S(1)}, bf16[9,32,256]{2,1,0:T(8,128)(2,1)S(1)}, u32[]{:S(2)}, u32[]{:S(2)}) collective-permute-start(bf16[9,32,256]{2,1,0:T(8,128)(2,1)S(1)} %get-tuple-element.45), channel_id=1, source_target_pairs={{0,1},{1,0},{2,3},{3,2},{4,5},{5,4},{6,7},{7,6},{8,9},{9,8},{10,11... | collective-permute-start | bytes 442376 | tf_op jit(solution)/shard_map/ppermute | solution.py:58
  64.4 10.6 %collective-permute-start.34 = (bf16[72,256]{1,0:T(8,128)(2,1)S(1)}, bf16[72,256]{1,0:T(8,128)(2,1)S(1)}, u32[]{:S(2)}, u32[]{:S(2)}) collective-permute-start(bf16[72,256]{1,0:T(8,128)(2,1)S(1)} %get-tuple-element.63), channel_id=1, source_target_pairs={{0,24},{8,0},{16,8},{24,16},{1,25},{9,1},{17,9},{25,17},{2,26},{10... | collective-permute-start | bytes 110600 | tf_op jit(solution)/shard_map/ppermute | solution.py:63
  71.0 9.0 %collective-permute-start.25 = (bf16[72,256]{1,0:T(8,128)(2,1)S(1)}, bf16[72,256]{1,0:T(8,128)(2,1)S(1)}, u32[]{:S(2)}, u32[]{:S(2)}) collective-permute-start(bf16[72,256]{1,0:T(8,128)(2,1)S(1)} %get-tuple-element.60), channel_id=1, source_target_pairs={{0,24},{8,0},{16,8},{24,16},{1,25},{9,1},{17,9},{25,17},{2,26},{10... | collective-permute-start | bytes 110600 | tf_op jit(solution)/shard_map/ppermute | solution.py:63
  75.0 8.9 %collective-permute-start.23 = (bf16[72,256]{1,0:T(8,128)(2,1)S(1)}, bf16[72,256]{1,0:T(8,128)(2,1)S(1)}, u32[]{:S(2)}, u32[]{:S(2)}) collective-permute-start(bf16[72,256]{1,0:T(8,128)(2,1)S(1)} %get-tuple-element.59), channel_id=1, source_target_pairs={{0,8},{8,16},{16,24},{24,0},{1,9},{9,17},{17,25},{25,1},{2,10},{10... | collective-permute-start | bytes 110600 | tf_op jit(solution)/shard_map/ppermute | solution.py:63
  75.7 8.3 %collective-permute-start.16 = (bf16[72,256]{1,0:T(8,128)(2,1)S(1)}, bf16[72,256]{1,0:T(8,128)(2,1)S(1)}, u32[]{:S(2)}, u32[]{:S(2)}) collective-permute-start(bf16[72,256]{1,0:T(8,128)(2,1)S(1)} %get-tuple-element.57), channel_id=1, source_target_pairs={{0,24},{8,0},{16,8},{24,16},{1,25},{9,1},{17,9},{25,17},{2,26},{10... | collective-permute-start | bytes 110600 | tf_op jit(solution)/shard_map/ppermute | solution.py:63
  80.2 8.8 %collective-permute-start.35 = (bf16[72,256]{1,0:T(8,128)(2,1)S(1)}, bf16[72,256]{1,0:T(8,128)(2,1)S(1)}, u32[]{:S(2)}, u32[]{:S(2)}) collective-permute-start(bf16[72,256]{1,0:T(8,128)(2,1)S(1)} %fusion.24), channel_id=1, source_target_pairs={{0,24},{8,0},{16,8},{24,16},{1,25},{9,1},{17,9},{25,17},{2,26},{10... | collective-permute-start | bytes 110600 | tf_op jit(solution)/shard_map/ppermute | solution.py:63
  83.9 8.9 %collective-permute-start.37 = (bf16[72,256]{1,0:T(8,128)(2,1)S(1)}, bf16[72,256]{1,0:T(8,128)(2,1)S(1)}, u32[]{:S(2)}, u32[]{:S(2)}) collective-permute-start(bf16[72,256]{1,0:T(8,128)(2,1)S(1)} %fusion.24), channel_id=1, source_target_pairs={{0,8},{8,16},{16,24},{24,0},{1,9},{9,17},{17,25},{25,1},{2,10},{10... | collective-permute-start | bytes 110600 | tf_op jit(solution)/shard_map/ppermute | solution.py:63
  84.6 8.4 %collective-permute-start.26 = (bf16[72,256]{1,0:T(8,128)(2,1)S(1)}, bf16[72,256]{1,0:T(8,128)(2,1)S(1)}, u32[]{:S(2)}, u32[]{:S(2)}) collective-permute-start(bf16[72,256]{1,0:T(8,128)(2,1)S(1)} %fusion.28), channel_id=1, source_target_pairs={{0,24},{8,0},{16,8},{24,16},{1,25},{9,1},{17,9},{25,17},{2,26},{10... | collective-permute-start | bytes 110600 | tf_op jit(solution)/shard_map/ppermute | solution.py:63
  (23 other events, 188.2 us)

commit v3 on v2

v3 whole, which is shorter than its diff:
```python
import functools

import jax
import jax.numpy as jnp
from jax import lax
from jax.experimental import pallas as pl
from jax.experimental.pallas import tpu as pltpu
from jax.sharding import PartitionSpec as P

EPSILON = 1e-06
FIRST_TAPS = 10
AXES = ("ta", "ha", "wa")
BF16 = jnp.bfloat16
F32 = jnp.float32


def dot(a, b):
    return jnp.dot(a, b, preferred_element_type=F32)


def dot_t(a, b):
    return lax.dot_general(a, b, (((1,), (1,)), ((), ())), preferred_element_type=F32)


def call(kernel, out_shape, flops, moved, scratch=(), scalars=0, arrays=0, left=0, limit=8):
    specs = [pl.BlockSpec(memory_space=pltpu.SMEM)] * scalars
    specs += [pl.BlockSpec(memory_space=pltpu.VMEM)] * arrays
    specs += [pl.BlockSpec(memory_space=pl.ANY)] * left
    return pl.pallas_call(
        kernel,
        out_shape=out_shape,
        in_specs=specs,
        scratch_shapes=list(scratch),
        compiler_params=pltpu.CompilerParams(vmem_limit_bytes=limit * 2**20),
        cost_estimate=pl.CostEstimate(flops=flops, bytes_accessed=moved, transcendentals=0),
    )


def shift_line(array, axis, by):
    length = lax.axis_size(axis)
    pairs = [(i, i + by) for i in range(length) if 0 <= i + by < length]
    return lax.ppermute(array, axis, pairs)


def swap_core(array):
    length = lax.axis_size("ha")
    return lax.ppermute(array, "ha", [(i, i ^ 1) for i in range(length)])


def swap_pairs(array, axis, odd):
    length = lax.axis_size(axis)
    pairs = []
    for i in range(odd, length - 1, 2):
        pairs += [(i, i + 1), (i + 1, i)]
    return lax.ppermute(array, axis, pairs) if pairs else None


def to_chip(array, du, dw):
    chips, width = lax.axis_size("ha") // 2, lax.axis_size("wa")
    pairs = []
    for u in range(chips):
        for core in range(2):
            for w in range(width):
                source = (2 * u + core) * width + w
                target = (2 * ((u + du) % chips) + core) * width + (w + dw) % width
                pairs.append((source, target))
    return lax.ppermute(array, ("ha", "wa"), pairs)


def ring(array, axis, by):
    length = lax.axis_size(axis)
    return lax.ppermute(array, axis, [(i, (i + by) % length) for i in range(length)])


CORNERS = 16


def prepare_kernel(x_ref, gain_ref, act_ref, act_t_ref, last):
    frames = x_ref.shape[0]
    values = x_ref[...].reshape(-1, x_ref.shape[-1]).astype(F32)
    inverse = lax.rsqrt(jnp.mean(values * values, axis=-1, keepdims=True) + EPSILON)
    normed = values * inverse * gain_ref[...]
    activated = (normed * jax.nn.sigmoid(normed)).astype(BF16)
    act_ref[...] = activated.reshape(x_ref.shape)
    act_t_ref[...] = activated.T
    last[...] = act_ref[frames - 2 :]


def rows_kernel(where_ref, cot, later, earlier, act, for_even, for_odd, lefts, rights):
    _, height, width, _ = cot.shape
    even = where_ref[0] == 0
    for place, refs in enumerate(((cot, later), (earlier, act))):
        at = 0
        for ref in refs:
            to = at + ref.shape[0]
            up, down = ref[:, 0], ref[:, height - 1]
            for_even[place, at:to] = jnp.where(even, down, up)
            for_odd[place, at:to] = jnp.where(even, up, down)
            cells = ref[...].astype(F32)
            lefts[place, at:to] = cells[:, :, 0, :].astype(BF16)
            rights[place, at:to] = cells[:, :, width - 1, :].astype(BF16)
            at = to


def both_sides(is_even, refs, shape):
    by_even = refs[0][...] if len(refs) > 0 else jnp.zeros(shape, BF16)
    by_odd = refs[1][...] if len(refs) > 1 else jnp.zeros(shape, BF16)
    return jnp.where(is_even, by_odd, by_even), jnp.where(is_even, by_even, by_odd)


def columns_kernel(count, where_ref, lefts, rights, *refs):
    swapped, (for_even, for_odd) = refs[:count], refs[count:]
    _, frames, height, channels = lefts.shape
    even_h, even_w = where_ref[0] == 0, where_ref[1] == 0
    width = swapped[0].shape[2]
    above, below = both_sides(even_h, swapped, swapped[0].shape)
    nothing = jnp.zeros((2, frames, CORNERS - 2, channels), F32)
    sides = []
    for source, at in ((lefts, 0), (rights, width - 1)):
        over = above.astype(F32)[:, :, at : at + 1, :]
        under = below.astype(F32)[:, :, at : at + 1, :]
        parts = [source[...].astype(F32), over, under, nothing]
        sides.append(jnp.concatenate(parts, axis=2).astype(BF16))
    for_even[...] = jnp.where(even_w, sides[1], sides[0])
    for_odd[...] = jnp.where(even_w, sides[0], sides[1])


def halves(core, values, chips):
    block = values.shape[-1] // (2 * chips)
    values = values.astype(F32)
    first, second = (
        jnp.concatenate(
            [
                values[..., (2 * u + which) * block : (2 * u + which + 1) * block]
                for u in range(chips)
            ],
            axis=-1,
        )
        for which in range(2)
    )
    own = jnp.where(core == 0, first, second)
    other = jnp.where(core == 0, second, first)
    return own.astype(BF16), other.astype(BF16)


def bundle_kernel(chips, width, counts, where_ref, cot, later, act_t, *refs):
    cot_edges, act_edges, mine, send = refs[sum(counts) :]
    core, even_w = where_ref[0], where_ref[1] == 0
    own, inner, channels = cot.shape
    tall = inner // width + CORNERS
    frames, size, half = mine.shape
    rows = both_sides(core == 0, refs[: counts[0]], (2, frames, width, channels))
    columns = both_sides(even_w, refs[counts[0] : sum(counts)], (2, frames, tall, channels))
    for place, target in enumerate((cot_edges, act_edges)):
        target[...] = jnp.concatenate([side[place] for side in rows + columns], axis=1)
    cells = act_t.shape[1]
    at = cells // half * channels
    for block in range(cells // half):
        send[block * channels : (block + 1) * channels] = act_t[
            :, block * half : (block + 1) * half
        ]
    for t in range(frames):
        inside, inside_send = halves(core, cot[t] if t < own else later[t - own], chips)
        outside, outside_send = halves(core, cot_edges[t], chips)
        mine[t, :inner], mine[t, inner:] = inside, outside
        send[at + t * size : at + t * size + inner] = inside_send
        send[at + t * size + inner : at + (t + 1) * size] = outside_send


def spread_frame(center, edges, height, width, target, at):
    channels = center.shape[-1]
    tall = height + CORNERS
    above, below = edges[:width], edges[width : 2 * width]
    rows = jnp.concatenate([above, center, below], axis=0)
    target[1, at : at + (height + 2) * width, :] = rows
    rows = rows.astype(F32).reshape(height + 2, width, channels)
    place = lax.broadcasted_iota(jnp.int32, rows.shape, 1)
    for k, start, edge, by in ((0, 2 * width, 0, 1), (2, 2 * width + tall, width - 1, width - 1)):
        column = edges[start : start + tall].astype(F32)
        column = jnp.concatenate(
            [column[height : height + 1], column[:height], column[height + 1 : height + 2]], axis=0
        )
        moved = jnp.where(place == edge, column[:, None, :], pltpu.roll(rows, by, 1))
        target[k, at : at + (height + 2) * width, :] = moved.astype(BF16).reshape(-1, channels)


def taps_kernel(height, width, all_taps, *refs):
    inner = height * width
    places, act_a, mine, other, *outs, terms_ref, spread_a, spread_b = refs
    count = len(outs)
    channels, cells = act_a.shape
    frames = cells // inner
    part = terms_ref.shape[1]
    spreads = (spread_a, spread_b)
    step = (height + 2) * width
    blocks = cells // part
    tall = mine.shape[1]
    lowest = 2 - max(tap[0] for tap in all_taps)
    for side, spread in enumerate(spreads):
        for at in range(lowest, frames + 2 - min(tap[0] for tap in all_taps)):
            if side == 0:
                frame = mine[at]
            else:
                start = blocks * channels + at * tall
                frame = other[start : start + tall]
            spread_frame(frame[:inner], frame[inner:], height, width, spread, (at - lowest) * step)
    acts = jnp.concatenate(
        [act_a[...]] + [other[b * channels : (b + 1) * channels] for b in range(blocks)], axis=1
    )

    def shifted(offset, j, k):
        pieces = []
        for spread in spreads:
            for t in range(frames):
                start = (t + 2 - offset - lowest) * step + (2 - j) * width
                pieces.append(spread[2 - k, start : start + inner, :])
        return jnp.concatenate(pieces, axis=0)

    for first in range(0, len(all_taps), 2):
        taps = all_taps[first : first + 2]
        terms = dot(acts, jnp.concatenate([shifted(*tap) for tap in taps], axis=1)).T
        for place in range(len(taps)):
            terms_ref[first + place] = terms[place * part : (place + 1) * part]
    owned = part // count
    for place, out in enumerate(outs):
        start = pl.multiple_of(places[place] * owned, owned)
        out[...] = terms_ref[:, pl.ds(start, owned), :].astype(out.dtype)


def parts_kernel(groups, count, where_ref, *refs):
    total = refs[-1]
    depth, part, channels = total.shape
    outs = refs[-1 - depth : -1]
    rows = total.reshape(depth * part, channels)
    at = 0
    for group in range(groups):
        terms = refs[group * count : (group + 1) * count]
        taps, owned, _ = terms[0].shape
        summed = terms[0][...]
        for term in terms[1:]:
            summed = summed + term[...].astype(F32)
        rows[at : at + taps * owned] = summed.reshape(taps * owned, channels)
        at += taps * owned
    if at < depth * part:
        rows[at:] = jnp.zeros((depth * part - at, channels), F32)
    for place, out in enumerate(outs):
        out[...] = total[where_ref[place]].astype(out.dtype)


def conv_sum(height, width, frames, spread, weight, backward):
    total = None
    for i in range(3):
        for j in range(3):
            at_t, at_h = (2 - i, 2 - j) if backward else (i, j)
            columns = []
            for k in range(3):
                at_w = 2 - k if backward else k
                pieces = []
                for t in range(frames):
                    start = ((t + at_t) * (height + 2) + at_h) * width
                    pieces.append(spread[at_w, start : start + height * width, :])
                columns.append(jnp.concatenate(pieces, axis=0))
            left = jnp.concatenate(columns, axis=1)
            if backward:
                term = dot_t(left, jnp.concatenate([weight[i, j, k] for k in range(3)], axis=1))
            else:
                term = dot(left, jnp.concatenate([weight[i, j, k] for k in range(3)], axis=0))
            total = term if total is None else total + term
    return total


def spread_all(height, width, centers, edges, spread):
    frame = 0
    for center in centers:
        for t in range(center.shape[0]):
            at = frame * (height + 2) * width
            spread_frame(center[t], edges[frame], height, width, spread, at)
            frame += 1


def forward_kernel(height, width, x_ref, earlier, act, edges, weight, after, out, spread):
    frames = act.shape[0]
    spread_all(height, width, (earlier, act), edges, spread)
    mixed = conv_sum(height, width, frames, spread, weight, False)
    out[...] = (x_ref[...].astype(F32) + mixed).astype(BF16)


def backward_kernel(
    height, width, x_ref, gain_ref, cot, later, edges, weight, after, out, spread
):
    frames = cot.shape[0]
    spread_all(height, width, (cot, later), edges, spread)
    grad_act = conv_sum(height, width, frames, spread, weight, True)
    values = x_ref[...].astype(F32)
    inverse = lax.rsqrt(jnp.mean(values * values, axis=-1, keepdims=True) + EPSILON)
    unit_rms = values * inverse
    gain = gain_ref[...]
    normed = unit_rms * gain
    logistic = jax.nn.sigmoid(normed)
    grad_unit = grad_act * logistic * (1.0 + normed * (1.0 - logistic)) * gain
    grad_norm = inverse * (
        grad_unit - unit_rms * jnp.mean(grad_unit * unit_rms, axis=-1, keepdims=True)
    )
    out[...] = (cot[...].reshape(out.shape).astype(F32) + grad_norm).astype(BF16)


def shape_of(*dims, dtype=BF16):
    return jax.ShapeDtypeStruct(dims, dtype)


def body(features, norm_gain, conv_weight, cotangent):
    frames, height, width, channels = features.shape
    inner = height * width
    cells = frames * inner
    depth, rows_of, cols_of = (lax.axis_size(axis) for axis in AXES)
    chips = rows_of // 2
    owned = channels // (rows_of * cols_of)
    half = channels // 2
    me_t, me_h, me_w = (lax.axis_index(axis) for axis in AXES)
    chip = me_h // 2
    where = jnp.stack([me_h % 2, me_w % 2]).astype(jnp.int32)
    flat_x = features.reshape(cells, channels)
    framed_cot = cotangent.reshape(frames, inner, channels)
    gain = norm_gain.reshape(1, channels)
    product = 2 * cells * channels * channels
    size = 2 * cells * channels
    tall = height + CORNERS
    around = 2 * width + 2 * tall

    act, act_t, last = call(
        prepare_kernel,
        (
            shape_of(*features.shape),
            shape_of(channels, cells),
            shape_of(2, *features.shape[1:]),
        ),
        10 * cells * channels,
        2 * size,
        arrays=2,
        limit=12,
    )(features, gain)
    later = shift_line(cotangent[:2], "ta", -1)
    earlier = shift_line(last, "ta", 1)
    for_even, for_odd, lefts, rights = call(
        rows_kernel,
        (
            shape_of(2, frames + 2, width, channels),
            shape_of(2, frames + 2, width, channels),
            shape_of(2, frames + 2, height, channels),
            shape_of(2, frames + 2, height, channels),
        ),
        0,
        2 * size,
        scalars=1,
        arrays=4,
        limit=12,
    )(where, cotangent, later, earlier, act)
    rows = [swap_pairs(for_even, "ha", 0), swap_pairs(for_odd, "ha", 1)]
    rows = [array for array in rows if array is not None]
    for_even, for_odd = call(
        functools.partial(columns_kernel, len(rows)),
        (shape_of(2, frames + 2, tall, channels),) * 2,
        0,
        size // 2,
        scalars=1,
        arrays=2 + len(rows),
    )(where, lefts, rights, *rows)
    columns = [swap_pairs(for_even, "wa", 0), swap_pairs(for_odd, "wa", 1)]
    columns = [array for array in columns if array is not None]
    later = later.reshape(2, inner, channels)
    cot_edges, act_edges, mine, send = call(
        functools.partial(bundle_kernel, chips, width, (len(rows), len(columns))),
        (shape_of(frames + 2, around, channels),) * 2
        + (
            shape_of(frames + 2, inner + around, half),
            shape_of(cells // half * channels + (frames + 2) * (inner + around), half),
        ),
        0,
        3 * size,
        scalars=1,
        arrays=3 + len(rows) + len(columns),
        limit=12,
    )(where, framed_cot, later, act_t, *rows, *columns)
    other = swap_core(send)

    count = chips * cols_of
    moves = [(du, dw) for du in range(chips) for dw in range(cols_of)]
    places = jnp.stack(
        [((chip + du) % chips) * cols_of + (me_w + dw) % cols_of for du, dw in moves]
    ).astype(jnp.int32)
    offsets = [(i, j, k) for i in range(3) for j in range(3) for k in range(3)]
    terms = []
    for taps in (offsets[:FIRST_TAPS], offsets[FIRST_TAPS:]):
        reach = frames + taps[-1][0] - taps[0][0]
        spread = pltpu.VMEM((3, reach * (height + 2) * width, half), BF16)
        pieces = call(
            functools.partial(taps_kernel, height, width, taps),
            tuple(
                shape_of(len(taps), owned, channels, dtype=F32 if place == 0 else BF16)
                for place in range(count)
            ),
            len(taps) * product,
            4 * size,
            (pltpu.VMEM((len(taps), half, channels), F32), spread, spread),
            scalars=1,
            arrays=3,
            limit=24,
        )(places, act_t, mine, other)
        moved = [to_chip(piece, *move) for piece, move in zip(pieces[1:], moves[1:])]
        terms.append([pieces[0]] + moved)
        after = pieces[0]

    framed_act = act.reshape(frames, inner, channels)
    earlier = earlier.reshape(2, inner, channels)
    flat = shape_of(cells, channels)
    spread = pltpu.VMEM((3, (frames + 2) * (height + 2) * width, channels), BF16)
    touched = conv_weight.size * 2 + 4 * size
    grad_features = call(
        functools.partial(backward_kernel, height, width),
        flat,
        27 * product,
        touched,
        (spread,),
        arrays=6,
        left=1,
        limit=24,
    )(flat_x, gain, framed_cot, later, cot_edges, conv_weight, after)
    decoded = call(
        functools.partial(forward_kernel, height, width),
        flat,
        27 * product,
        touched,
        (spread,),
        arrays=5,
        left=1,
        limit=24,
    )(flat_x, earlier, framed_act, act_edges, conv_weight, after)

    part = -(-27 * owned // (16 * depth)) * 16
    owners = jnp.stack([(me_t + by) % depth for by in range(depth)]).astype(jnp.int32)
    own, *sends = call(
        functools.partial(parts_kernel, len(terms), count),
        tuple(
            shape_of(part, channels, dtype=F32 if by == 0 else BF16) for by in range(depth)
        ),
        0,
        2 * size,
        (pltpu.VMEM((depth, part, channels), F32),),
        scalars=1,
        arrays=count * len(terms),
        left=2,
    )(owners, *terms[0], *terms[1], grad_features, decoded)
    for by, sent in enumerate(sends, 1):
        own = own + ring(sent, "ta", by).astype(F32)
    scale = float(cells * depth * rows_of * cols_of) ** (-0.5)
    own = (own * scale).astype(BF16)
    gathered = [ring(own, "ta", by) for by in range(depth - 1, 0, -1)] + [own]
    gathered = jnp.roll(jnp.stack(gathered), me_t + 1, axis=0)
    grad_weight = gathered.reshape(depth * part, channels)[: 27 * owned]
    grad_weight = jnp.swapaxes(grad_weight.reshape(27, owned, channels), 1, 2).astype(F32)
    return (
        decoded.reshape(features.shape),
        grad_features.reshape(features.shape),
        grad_weight.reshape(3, 3, 3, channels, owned),
    )


def solution(mesh):
    placed = (P("ta", "ha", "wa", None), P(), P(), P("ta", "ha", "wa", None))
    return jax.shard_map(
        body,
        mesh=mesh,
        in_specs=placed,
        out_specs=(
            P("ta", "ha", "wa", None),
            P("ta", "ha", "wa", None),
            P(None, None, None, None, ("ha", "wa")),
        ),
        check_vma=False,
    )
```

time: 100 us -> 91.6 us (0.916)
  starting transfers between devices: 59.5 us -> 29.6 us
  waiting for transfers between devices: 11.7 us -> 31.5 us
  Pallas kernels: 18.6 us -> 21.2 us
    ppermute x18 -> x6, starting transfers between devices: 26.4 us -> 9.34 us  [ring(): lax.ppermute(array, axis, [(i, (i + by) % length) for i in range(length)])]
    ppermute x8 -> x2, starting transfers between devices: 19 us -> 6.24 us  [shift_line(): return lax.ppermute(array, axis, pairs)]
    ppermute x18 -> x6, waiting for transfers between devices: 4.99 us -> 12.6 us  [ring(): lax.ppermute(array, axis, [(i, (i + by) % length) for i in range(length)])]
    ppermute x8 -> x2, waiting for transfers between devices: 3.08 us -> 8.26 us  [shift_line(): return lax.ppermute(array, axis, pairs)]
    ppermute x0 -> x3, waiting for transfers between devices: none -> 4.77 us  [swap_pairs(): return lax.ppermute(array, axis, pairs) if pairs else None]
    ppermute x9 -> x6, starting transfers between devices: 11.3 us -> 7.45 us  [to_chip(): return lax.ppermute(array, ('ha', 'wa'), pairs)]
    pallas_call x8, Pallas kernels: 17.9 us -> 20.8 us  [the longest x2 5.9 us: body(): call(functools.partial(taps_kernel, height, width, taps), tuple((shape_of...]
    ppermute x3 -> x1, waiting for transfers between devices: 0.01 us -> 2.37 us  [swap_core(): return lax.ppermute(array, 'ha', [(i, i ^ 1) for i in range(length)])]
  transfers between devices with their start and end apart: 38 -> 18, of which waited for: 7 -> 10; matrix products, arithmetic and copies ran while one was open for 2% -> 1% of each run, Pallas kernels for 18% -> 14%
where the time goes in v3:
time: 91.6 us; the launch traced here: 90.9 us
  waiting for transfers between devices  31.5 us (34%)
  starting transfers between devices  29.6 us (32%)
  Pallas kernels  21.2 us (23%)
  local copies, waits for them, and re-layouts  6.51 us (7%)
  other arithmetic  1.29 us (1%)
    ppermute x6, waiting for transfers between devices, ring(): lax.ppermute(array, axis, [(i, (i + by) % length) for i in range(length)])  12.6 us
    ppermute x6, starting transfers between devices, ring(): lax.ppermute(array, axis, [(i, (i + by) % length) for i in range(length)])  9.34 us
    ppermute x2, waiting for transfers between devices, shift_line(): return lax.ppermute(array, axis, pairs)  8.26 us
    ppermute x6, starting transfers between devices, to_chip(): return lax.ppermute(array, ('ha', 'wa'), pairs)  7.45 us
    ppermute x2, starting transfers between devices, shift_line(): return lax.ppermute(array, axis, pairs)  6.24 us
    pallas_call x2, Pallas kernels, body(): call(functools.partial(taps_kernel, height, width, taps), tuple((shape_of...  5.9 us
    unnamed x31, local copies, waits for them, and re-layouts  5.46 us
    pallas_call x1, Pallas kernels, body(): call(functools.partial(backward_kernel, height, width), flat, 27 * produc...  5.06 us
  transfers between devices with their start and end apart: 18, of which 10 were waited for; matrix products, arithmetic and copies ran while one was open for 1% of the time, Pallas kernels for 14%

profile of v3, /device:TPU:0, one launch (start us, length us, event | category | flops | bytes accessed | tf_op | source)
XLA Modules:
  0.0 90.9 jit_solution(1478095302996350608)
XLA Ops:
  2.9 4.9 %collective-permute-start = (bf16[2,16,16,256]{3,2,1,0:T(8,128)(2,1)S(1)}, bf16[2,16,16,256]{3,2,1,0:T(8,128)(2,1)S(1)}, u32[]{:S(2)}, u32[]{:S(2)}) collective-permute-start(bf16[2,16,16,256]{3,2,1,0:T(8,128)(2,1)S(1)} %get-tuple-element.27), channel_id=1, source_target_pairs={{0,8},{8,16},{16,24},{1,9},{9,17},{17,25},{2,10},{10,18},{18,26},{... | collective-permute-start | bytes 786440 | tf_op jit(solution)/shard_map/ppermute | solution.py:42
  10.2 3.2 %collective-permute-done.earlier = bf16[2,16,16,256]{3,2,1,0:T(8,128)(2,1)S(1)} collective-permute-done((bf16[2,16,16,256]{3,2,1,0:T(8,128)(2,1)S(1)}, bf16[2,16,16,256]{3,2,1,0:T(8,128)(2,1)S(1)}, u32[]{:S(2)}, u32[]{:S(2)}) %collective-permute-start) | collective-permute-done | bytes 262176 | tf_op jit(solution)/shard_map/ppermute | solution.py:42
  13.3 5.1 %collective-permute-done.1.later = bf16[2,16,16,256]{3,2,1,0:T(8,128)(2,1)S(1)} collective-permute-done((bf16[2,16,16,256]{3,2,1,0:T(8,128)(2,1)S(1)}, bf16[2,16,16,256]{3,2,1,0:T(8,128)(2,1)S(1)}, u32[]{:S(2)}, u32[]{:S(2)}) %collective-permute-start.1) | collective-permute-done | bytes 262176 | tf_op jit(solution)/shard_map/ppermute | solution.py:42
  22.0 1.5 %collective-permute-start.4 = (bf16[2,6,32,256]{3,2,1,0:T(8,128)(2,1)S(1)}, bf16[2,6,32,256]{3,2,1,0:T(8,128)(2,1)S(1)}, u32[]{:S(2)}, u32[]{:S(2)}) collective-permute-start(bf16[2,6,32,256]{3,2,1,0:T(8,128)(2,1)S(1)} %get-tuple-element.34), channel_id=1, source_target_pairs={{0,1},{1,0},{2,3},{3,2},{4,5},{5,4},{6,7},{7,6},{8,9},{9,8},{10,11... | collective-permute-start | bytes 589832 | tf_op jit(solution)/shard_map/ppermute | solution.py:55
  23.6 4.2 %collective-permute-done.4.refs_2_ = bf16[2,6,32,256]{3,2,1,0:T(8,128)(2,1)S(1)} collective-permute-done((bf16[2,6,32,256]{3,2,1,0:T(8,128)(2,1)S(1)}, bf16[2,6,32,256]{3,2,1,0:T(8,128)(2,1)S(1)}, u32[]{:S(2)}, u32[]{:S(2)}) %collective-permute-start.4) | collective-permute-done | bytes 196640 | tf_op jit(solution)/shard_map/ppermute | solution.py:55
  27.7 2.1 %shard_map.70 = (bf16[6,96,256]{2,1,0:T(8,128)(2,1)S(1)}, bf16[6,96,256]{2,1,0:T(8,128)(2,1)S(1)}, bf16[6,352,128]{2,1,0:T(8,128)(2,1)S(1)}, bf16[4160,128]{1,0:T(8,128)(2,1)}) custom-call(s32[2]{0:T(128)S(1)} %pad_add_fusion.where_ref, bf16[4,256,256]{2,1,0:T(8,128)(2,1)S(1)} %bitcast.36, bf16[2,256,256]{2,1,0:T(8,128)(2,1)S(1)} %bitcast.38, ...), custom_call_target="tpu_custom_call" | custom-call | bytes 1572864 | tf_op jit(solution)/shard_map/pallas_call | solution.py:371
  31.3 4.3 %collective-permute-start.5 = (bf16[4160,128]{1,0:T(8,128)(2,1)}, bf16[4160,128]{1,0:T(8,128)(2,1)S(1)}, u32[]{:S(2)}, u32[]{:S(2)}) collective-permute-start(bf16[4160,128]{1,0:T(8,128)(2,1)} %get-tuple-element.37), channel_id=1, source_target_pairs={{0,2},{2,0},{4,6},{6,4},{1,3},{3,1},{5,7},{7,5},{8,10},{10,8},{12,... | collective-permute-start | bytes 3194888 | tf_op jit(solution)/shard_map/ppermute | solution.py:47
  35.7 2.4 %collective-permute-done.5.refs_3_ = bf16[4160,128]{1,0:T(8,128)(2,1)S(1)} collective-permute-done((bf16[4160,128]{1,0:T(8,128)(2,1)}, bf16[4160,128]{1,0:T(8,128)(2,1)S(1)}, u32[]{:S(2)}, u32[]{:S(2)}) %collective-permute-start.5) | collective-permute-done | bytes 1064992 | tf_op jit(solution)/shard_map/ppermute | solution.py:47
  39.1 2.5 %shard_map.74 = (f32[10,32,256]{2,1,0:T(8,128)S(1)}, bf16[10,32,256]{2,1,0:T(8,128)(2,1)S(1)}, bf16[10,32,256]{2,1,0:T(8,128)(2,1)S(1)}, bf16[10,32,256]{2,1,0:T(8,128)(2,1)S(1)}) custom-call(s32[4]{0:T(128)S(1)} %pad_add_fusion.1.refs_0_, bf16[256,1024]{1,0:T(8,128)(2,1)S(1)} %get-tuple-element.29.act_t.refs_1_, bf16[6,352,128]{2,1,0:T(8,128)(2,1)S(1)} %copy-done.9, ...), custom_call_target="tpu_custom_call" | custom-call | flops 1342177280 | bytes 2097152 | tf_op jit(solution)/shard_map/pallas_call | solution.py:396
  41.6 1.6 %collective-permute-start.6 = (bf16[10,32,256]{2,1,0:T(8,128)(2,1)S(1)}, bf16[10,32,256]{2,1,0:T(8,128)(2,1)S(1)}, u32[]{:S(2)}, u32[]{:S(2)}) collective-permute-start(bf16[10,32,256]{2,1,0:T(8,128)(2,1)S(1)} %get-tuple-element.41), channel_id=1, source_target_pairs={{0,1},{1,0},{2,3},{3,2},{4,5},{5,4},{6,7},{7,6},{8,9},{9,8},{10,11... | collective-permute-start | bytes 491528 | tf_op jit(solution)/shard_map/ppermute | solution.py:67
  43.2 2.2 %collective-permute-start.7 = (bf16[10,32,256]{2,1,0:T(8,128)(2,1)S(1)}, bf16[10,32,256]{2,1,0:T(8,128)(2,1)S(1)}, u32[]{:S(2)}, u32[]{:S(2)}) collective-permute-start(bf16[10,32,256]{2,1,0:T(8,128)(2,1)S(1)} %get-tuple-element.42), channel_id=1, source_target_pairs={{0,4},{1,5},{2,6},{3,7},{4,0},{5,1},{6,2},{7,3},{8,12},{9,13},{10,... | collective-permute-start | bytes 491528 | tf_op jit(solution)/shard_map/ppermute | solution.py:67
  45.5 3.4 %shard_map.71 = (f32[17,32,256]{2,1,0:T(8,128)S(1)}, bf16[17,32,256]{2,1,0:T(8,128)(2,1)S(1)}, bf16[17,32,256]{2,1,0:T(8,128)(2,1)S(1)}, bf16[17,32,256]{2,1,0:T(8,128)(2,1)S(1)}) custom-call(s32[4]{0:T(128)S(1)} %pad_add_fusion.1.refs_0_, bf16[256,1024]{1,0:T(8,128)(2,1)S(1)} %get-tuple-element.29.act_t.refs_1_, bf16[6,352,128]{2,1,0:T(8,128)(2,1)S(1)} %copy-done.9, ...), custom_call_target="tpu_custom_call" | custom-call | flops 2281701376 | bytes 2097152 | tf_op jit(solution)/shard_map/pallas_call | solution.py:396
  49.0 1.5 %collective-permute-start.9 = (bf16[17,32,256]{2,1,0:T(8,128)(2,1)S(1)}, bf16[17,32,256]{2,1,0:T(8,128)(2,1)S(1)}, u32[]{:S(2)}, u32[]{:S(2)}) collective-permute-start(bf16[17,32,256]{2,1,0:T(8,128)(2,1)S(1)} %get-tuple-element.44), channel_id=1, source_target_pairs={{0,1},{1,0},{2,3},{3,2},{4,5},{5,4},{6,7},{7,6},{8,9},{9,8},{10,11... | collective-permute-start | bytes 835592 | tf_op jit(solution)/shard_map/ppermute | solution.py:67
  50.5 2.0 %collective-permute-start.10 = (bf16[17,32,256]{2,1,0:T(8,128)(2,1)S(1)}, bf16[17,32,256]{2,1,0:T(8,128)(2,1)S(1)}, u32[]{:S(2)}, u32[]{:S(2)}) collective-permute-start(bf16[17,32,256]{2,1,0:T(8,128)(2,1)S(1)} %get-tuple-element.45), channel_id=1, source_target_pairs={{0,4},{1,5},{2,6},{3,7},{4,0},{5,1},{6,2},{7,3},{8,12},{9,13},{10,... | collective-permute-start | bytes 835592 | tf_op jit(solution)/shard_map/ppermute | solution.py:67
  52.5 5.1 %shard_map.73.refs_8_ = bf16[1024,256]{1,0:T(8,128)(2,1)} custom-call(bf16[1024,256]{1,0:T(8,128)(2,1)S(1)} %bitcast.40, f32[1,256]{1,0:T(1,128)S(1)} %bitcast.47, bf16[4,256,256]{2,1,0:T(8,128)(2,1)S(1)} %bitcast.37, bf16[2,256,256]{2,1,0:T(8,128)(2,1)S(1)} %bitcast.39, bf16[6,96,256]{2,1,0:T(8,128)(2,1)S(1)} %copy-done.11, ...), custom_call_target="tpu_custom_call" | custom-call | flops 3623878656 | bytes 5636096 | tf_op jit(solution)/shard_map/pallas_call | solution.py:418
  57.6 4.7 %shard_map.72.refs_9_ = bf16[1024,256]{1,0:T(8,128)(2,1)} custom-call(bf16[1024,256]{1,0:T(8,128)(2,1)S(1)} %bitcast.41, bf16[2,256,256]{2,1,0:T(8,128)(2,1)S(1)} %bitcast.45, bf16[4,256,256]{2,1,0:T(8,128)(2,1)S(1)} %bitcast.42, bf16[6,96,256]{2,1,0:T(8,128)(2,1)S(1)} %get-tuple-element.35.edges, bf16[3,3,3,256,256]{4,3,2,1,0:T(8,128)(2,1)S(1)} %copy-done.7, ...), custom_call_target="tpu_custom_call" | custom-call | flops 3623878656 | bytes 5636096 | tf_op jit(solution)/shard_map/pallas_call | solution.py:428
  62.3 3.5 %collective-permute-done.11.refs_7_ = bf16[17,32,256]{2,1,0:T(8,128)(2,1)S(1)} collective-permute-done((bf16[17,32,256]{2,1,0:T(8,128)(2,1)S(1)}, bf16[17,32,256]{2,1,0:T(8,128)(2,1)S(1)}, u32[]{:S(2)}, u32[]{:S(2)}) %collective-permute-start.11) | collective-permute-done | bytes 278560 | tf_op jit(solution)/shard_map/ppermute | solution.py:67
  67.7 1.6 %collective-permute-start.14 = (bf16[224,256]{1,0:T(8,128)(2,1)S(1)}, bf16[224,256]{1,0:T(8,128)(2,1)S(1)}, u32[]{:S(2)}, u32[]{:S(2)}) collective-permute-start(bf16[224,256]{1,0:T(8,128)(2,1)S(1)} %get-tuple-element.50), channel_id=1, source_target_pairs={{0,24},{8,0},{16,8},{24,16},{1,25},{9,1},{17,9},{25,17},{2,26},{10... | collective-permute-start | bytes 344072 | tf_op jit(solution)/shard_map/ppermute | solution.py:72
  69.3 1.5 %collective-permute-start.13 = (bf16[224,256]{1,0:T(8,128)(2,1)S(1)}, bf16[224,256]{1,0:T(8,128)(2,1)S(1)}, u32[]{:S(2)}, u32[]{:S(2)}) collective-permute-start(bf16[224,256]{1,0:T(8,128)(2,1)S(1)} %get-tuple-element.49), channel_id=1, source_target_pairs={{0,16},{8,24},{16,0},{24,8},{1,17},{9,25},{17,1},{25,9},{2,18},{10... | collective-permute-start | bytes 344072 | tf_op jit(solution)/shard_map/ppermute | solution.py:72
  70.8 1.6 %collective-permute-start.12 = (bf16[224,256]{1,0:T(8,128)(2,1)S(1)}, bf16[224,256]{1,0:T(8,128)(2,1)S(1)}, u32[]{:S(2)}, u32[]{:S(2)}) collective-permute-start(bf16[224,256]{1,0:T(8,128)(2,1)S(1)} %get-tuple-element.48), channel_id=1, source_target_pairs={{0,8},{8,16},{16,24},{24,0},{1,9},{9,17},{17,25},{25,1},{2,10},{10... | collective-permute-start | bytes 344072 | tf_op jit(solution)/shard_map/ppermute | solution.py:72
  72.7 6.4 %collective-permute-done.13 = bf16[224,256]{1,0:T(8,128)(2,1)S(1)} collective-permute-done((bf16[224,256]{1,0:T(8,128)(2,1)S(1)}, bf16[224,256]{1,0:T(8,128)(2,1)S(1)}, u32[]{:S(2)}, u32[]{:S(2)}) %collective-permute-start.13) | collective-permute-done | bytes 114720 | tf_op jit(solution)/shard_map/ppermute | solution.py:72
  80.2 1.6 %collective-permute-start.16 = (bf16[224,256]{1,0:T(8,128)(2,1)S(1)}, bf16[224,256]{1,0:T(8,128)(2,1)S(1)}, u32[]{:S(2)}, u32[]{:S(2)}) collective-permute-start(bf16[224,256]{1,0:T(8,128)(2,1)S(1)} %multiply_convert_fusion), channel_id=1, source_target_pairs={{0,16},{8,24},{16,0},{24,8},{1,17},{9,25},{17,1},{25,9},{2,18},{10... | collective-permute-start | bytes 344072 | tf_op jit(solution)/shard_map/ppermute | solution.py:72
  81.9 1.9 %collective-permute-start.17 = (bf16[224,256]{1,0:T(8,128)(2,1)S(1)}, bf16[224,256]{1,0:T(8,128)(2,1)S(1)}, u32[]{:S(2)}, u32[]{:S(2)}) collective-permute-start(bf16[224,256]{1,0:T(8,128)(2,1)S(1)} %multiply_convert_fusion), channel_id=1, source_target_pairs={{0,8},{8,16},{16,24},{24,0},{1,9},{9,17},{17,25},{25,1},{2,10},{10... | collective-permute-start | bytes 344072 | tf_op jit(solution)/shard_map/ppermute | solution.py:72
  85.2 4.5 %collective-permute-done.16 = bf16[224,256]{1,0:T(8,128)(2,1)S(1)} collective-permute-done((bf16[224,256]{1,0:T(8,128)(2,1)S(1)}, bf16[224,256]{1,0:T(8,128)(2,1)S(1)}, u32[]{:S(2)}, u32[]{:S(2)}) %collective-permute-start.16) | collective-permute-done | bytes 114720 | tf_op jit(solution)/shard_map/ppermute | solution.py:72
  (61 shorter events, 16.9 us)
Async XLA Ops:
  0.6 17.8 %copy-start = (bf16[4,16,16,256]{3,2,1,0:T(8,128)(2,1)S(1)}, bf16[4,16,16,256]{3,2,1,0:T(8,128)(2,1)}, u32[]{:S(2)}) copy-start(bf16[4,16,16,256]{3,2,1,0:T(8,128)(2,1)} %cot.1) | copy-start | bytes 1572868
  2.9 10.5 %collective-permute-start = (bf16[2,16,16,256]{3,2,1,0:T(8,128)(2,1)S(1)}, bf16[2,16,16,256]{3,2,1,0:T(8,128)(2,1)S(1)}, u32[]{:S(2)}, u32[]{:S(2)}) collective-permute-start(bf16[2,16,16,256]{3,2,1,0:T(8,128)(2,1)S(1)} %get-tuple-element.27), channel_id=1, source_target_pairs={{0,8},{8,16},{16,24},{1,9},{9,17},{17,25},{2,10},{10,18},{18,26},{... | collective-permute-start | bytes 786440 | tf_op jit(solution)/shard_map/ppermute | solution.py:42
  8.8 9.7 %collective-permute-start.1 = (bf16[2,16,16,256]{3,2,1,0:T(8,128)(2,1)S(1)}, bf16[2,16,16,256]{3,2,1,0:T(8,128)(2,1)S(1)}, u32[]{:S(2)}, u32[]{:S(2)}) collective-permute-start(bf16[2,16,16,256]{3,2,1,0:T(8,128)(2,1)S(1)} %slice.6), channel_id=1, source_target_pairs={{8,0},{16,8},{24,16},{9,1},{17,9},{25,17},{10,2},{18,10},{26,18},{... | collective-permute-start | bytes 786440 | tf_op jit(solution)/shard_map/ppermute | solution.py:42
  19.4 1.4 %collective-permute-start.2 = (bf16[2,6,16,256]{3,2,1,0:T(8,128)(2,1)S(1)}, bf16[2,6,16,256]{3,2,1,0:T(8,128)(2,1)S(1)}, u32[]{:S(2)}, u32[]{:S(2)}) collective-permute-start(bf16[2,6,16,256]{3,2,1,0:T(8,128)(2,1)S(1)} %get-tuple-element.30), channel_id=1, source_target_pairs={{0,2},{2,0},{4,6},{6,4},{1,3},{3,1},{5,7},{7,5},{8,10},{10,8},{12,... | collective-permute-start | bytes 294920 | tf_op jit(solution)/shard_map/ppermute | solution.py:55
  19.5 1.3 %collective-permute-start.3 = (bf16[2,6,16,256]{3,2,1,0:T(8,128)(2,1)S(1)}, bf16[2,6,16,256]{3,2,1,0:T(8,128)(2,1)S(1)}, u32[]{:S(2)}, u32[]{:S(2)}) collective-permute-start(bf16[2,6,16,256]{3,2,1,0:T(8,128)(2,1)S(1)} %get-tuple-element.31), channel_id=1, source_target_pairs={{2,4},{4,2},{3,5},{5,3},{10,12},{12,10},{11,13},{13,11},{18,20},{2... | collective-permute-start | bytes 294920 | tf_op jit(solution)/shard_map/ppermute | solution.py:55
  22.0 5.7 %collective-permute-start.4 = (bf16[2,6,32,256]{3,2,1,0:T(8,128)(2,1)S(1)}, bf16[2,6,32,256]{3,2,1,0:T(8,128)(2,1)S(1)}, u32[]{:S(2)}, u32[]{:S(2)}) collective-permute-start(bf16[2,6,32,256]{3,2,1,0:T(8,128)(2,1)S(1)} %get-tuple-element.34), channel_id=1, source_target_pairs={{0,1},{1,0},{2,3},{3,2},{4,5},{5,4},{6,7},{7,6},{8,9},{9,8},{10,11... | collective-permute-start | bytes 589832 | tf_op jit(solution)/shard_map/ppermute | solution.py:55
  31.3 6.8 %collective-permute-start.5 = (bf16[4160,128]{1,0:T(8,128)(2,1)}, bf16[4160,128]{1,0:T(8,128)(2,1)S(1)}, u32[]{:S(2)}, u32[]{:S(2)}) collective-permute-start(bf16[4160,128]{1,0:T(8,128)(2,1)} %get-tuple-element.37), channel_id=1, source_target_pairs={{0,2},{2,0},{4,6},{6,4},{1,3},{3,1},{5,7},{7,5},{8,10},{10,8},{12,... | collective-permute-start | bytes 3194888 | tf_op jit(solution)/shard_map/ppermute | solution.py:47
  41.6 16.0 %collective-permute-start.6 = (bf16[10,32,256]{2,1,0:T(8,128)(2,1)S(1)}, bf16[10,32,256]{2,1,0:T(8,128)(2,1)S(1)}, u32[]{:S(2)}, u32[]{:S(2)}) collective-permute-start(bf16[10,32,256]{2,1,0:T(8,128)(2,1)S(1)} %get-tuple-element.41), channel_id=1, source_target_pairs={{0,1},{1,0},{2,3},{3,2},{4,5},{5,4},{6,7},{7,6},{8,9},{9,8},{10,11... | collective-permute-start | bytes 491528 | tf_op jit(solution)/shard_map/ppermute | solution.py:67
  43.2 19.0 %collective-permute-start.7 = (bf16[10,32,256]{2,1,0:T(8,128)(2,1)S(1)}, bf16[10,32,256]{2,1,0:T(8,128)(2,1)S(1)}, u32[]{:S(2)}, u32[]{:S(2)}) collective-permute-start(bf16[10,32,256]{2,1,0:T(8,128)(2,1)S(1)} %get-tuple-element.42), channel_id=1, source_target_pairs={{0,4},{1,5},{2,6},{3,7},{4,0},{5,1},{6,2},{7,3},{8,12},{9,13},{10,... | collective-permute-start | bytes 491528 | tf_op jit(solution)/shard_map/ppermute | solution.py:67
  45.4 7.1 %copy-start.2 = (bf16[4,16,16,256]{3,2,1,0:T(8,128)(2,1)S(1)}, bf16[4,16,16,256]{3,2,1,0:T(8,128)(2,1)}, u32[]{:S(2)}) copy-start(bf16[4,16,16,256]{3,2,1,0:T(8,128)(2,1)} %x_ref.1) | copy-start | bytes 1572868
  45.4 7.1 %copy-start.6 = (f32[256]{0:T(256)S(1)}, f32[256]{0:T(256)}, u32[]{:S(2)}) copy-start(f32[256]{0:T(256)} %param.5) | copy-start | bytes 3076
  45.4 7.1 %copy-start.7 = (bf16[3,3,3,256,256]{4,3,2,1,0:T(8,128)(2,1)S(1)}, bf16[3,3,3,256,256]{4,3,2,1,0:T(8,128)(2,1)}, u32[]{:S(2)}) copy-start(bf16[3,3,3,256,256]{4,3,2,1,0:T(8,128)(2,1)} %weight.3) | copy-start | bytes 10616836
  45.4 7.1 %copy-start.11 = (bf16[6,96,256]{2,1,0:T(8,128)(2,1)S(1)}, bf16[6,96,256]{2,1,0:T(8,128)(2,1)}, u32[]{:S(2)}) copy-start(bf16[6,96,256]{2,1,0:T(8,128)(2,1)} %copy-done.10) | copy-start | bytes 884740
  45.4 16.8 %collective-permute-start.8 = (bf16[10,32,256]{2,1,0:T(8,128)(2,1)S(1)}, bf16[10,32,256]{2,1,0:T(8,128)(2,1)S(1)}, u32[]{:S(2)}, u32[]{:S(2)}) collective-permute-start(bf16[10,32,256]{2,1,0:T(8,128)(2,1)S(1)} %get-tuple-element.43), channel_id=1, source_target_pairs={{0,5},{1,4},{2,7},{3,6},{4,1},{5,0},{6,3},{7,2},{8,13},{9,12},{10,... | collective-permute-start | bytes 491528 | tf_op jit(solution)/shard_map/ppermute | solution.py:67
  49.0 13.3 %collective-permute-start.9 = (bf16[17,32,256]{2,1,0:T(8,128)(2,1)S(1)}, bf16[17,32,256]{2,1,0:T(8,128)(2,1)S(1)}, u32[]{:S(2)}, u32[]{:S(2)}) collective-permute-start(bf16[17,32,256]{2,1,0:T(8,128)(2,1)S(1)} %get-tuple-element.44), channel_id=1, source_target_pairs={{0,1},{1,0},{2,3},{3,2},{4,5},{5,4},{6,7},{7,6},{8,9},{9,8},{10,11... | collective-permute-start | bytes 835592 | tf_op jit(solution)/shard_map/ppermute | solution.py:67
  50.5 11.8 %collective-permute-start.10 = (bf16[17,32,256]{2,1,0:T(8,128)(2,1)S(1)}, bf16[17,32,256]{2,1,0:T(8,128)(2,1)S(1)}, u32[]{:S(2)}, u32[]{:S(2)}) collective-permute-start(bf16[17,32,256]{2,1,0:T(8,128)(2,1)S(1)} %get-tuple-element.45), channel_id=1, source_target_pairs={{0,4},{1,5},{2,6},{3,7},{4,0},{5,1},{6,2},{7,3},{8,12},{9,13},{10,... | collective-permute-start | bytes 835592 | tf_op jit(solution)/shard_map/ppermute | solution.py:67
  57.6 8.2 %collective-permute-start.11 = (bf16[17,32,256]{2,1,0:T(8,128)(2,1)S(1)}, bf16[17,32,256]{2,1,0:T(8,128)(2,1)S(1)}, u32[]{:S(2)}, u32[]{:S(2)}) collective-permute-start(bf16[17,32,256]{2,1,0:T(8,128)(2,1)S(1)} %get-tuple-element.46), channel_id=1, source_target_pairs={{0,5},{1,4},{2,7},{3,6},{4,1},{5,0},{6,3},{7,2},{8,13},{9,12},{10,... | collective-permute-start | bytes 835592 | tf_op jit(solution)/shard_map/ppermute | solution.py:67
  57.6 8.2 %copy-start.3 = (bf16[1024,256]{1,0:T(8,128)(2,1)S(1)}, bf16[1024,256]{1,0:T(8,128)(2,1)}, u32[]{:S(2)}) copy-start(bf16[1024,256]{1,0:T(8,128)(2,1)} %shard_map.73.refs_8_) | copy-start | bytes 1572868
  67.7 5.0 %collective-permute-start.14 = (bf16[224,256]{1,0:T(8,128)(2,1)S(1)}, bf16[224,256]{1,0:T(8,128)(2,1)S(1)}, u32[]{:S(2)}, u32[]{:S(2)}) collective-permute-start(bf16[224,256]{1,0:T(8,128)(2,1)S(1)} %get-tuple-element.50), channel_id=1, source_target_pairs={{0,24},{8,0},{16,8},{24,16},{1,25},{9,1},{17,9},{25,17},{2,26},{10... | collective-permute-start | bytes 344072 | tf_op jit(solution)/shard_map/ppermute | solution.py:72
  69.3 9.8 %collective-permute-start.13 = (bf16[224,256]{1,0:T(8,128)(2,1)S(1)}, bf16[224,256]{1,0:T(8,128)(2,1)S(1)}, u32[]{:S(2)}, u32[]{:S(2)}) collective-permute-start(bf16[224,256]{1,0:T(8,128)(2,1)S(1)} %get-tuple-element.49), channel_id=1, source_target_pairs={{0,16},{8,24},{16,0},{24,8},{1,17},{9,25},{17,1},{25,9},{2,18},{10... | collective-permute-start | bytes 344072 | tf_op jit(solution)/shard_map/ppermute | solution.py:72
  70.8 8.3 %collective-permute-start.12 = (bf16[224,256]{1,0:T(8,128)(2,1)S(1)}, bf16[224,256]{1,0:T(8,128)(2,1)S(1)}, u32[]{:S(2)}, u32[]{:S(2)}) collective-permute-start(bf16[224,256]{1,0:T(8,128)(2,1)S(1)} %get-tuple-element.48), channel_id=1, source_target_pairs={{0,8},{8,16},{16,24},{24,0},{1,9},{9,17},{17,25},{25,1},{2,10},{10... | collective-permute-start | bytes 344072 | tf_op jit(solution)/shard_map/ppermute | solution.py:72
  79.1 6.1 %collective-permute-start.15 = (bf16[224,256]{1,0:T(8,128)(2,1)S(1)}, bf16[224,256]{1,0:T(8,128)(2,1)S(1)}, u32[]{:S(2)}, u32[]{:S(2)}) collective-permute-start(bf16[224,256]{1,0:T(8,128)(2,1)S(1)} %multiply_convert_fusion), channel_id=1, source_target_pairs={{0,24},{8,0},{16,8},{24,16},{1,25},{9,1},{17,9},{25,17},{2,26},{10... | collective-permute-start | bytes 344072 | tf_op jit(solution)/shard_map/ppermute | solution.py:72
  80.2 9.5 %collective-permute-start.16 = (bf16[224,256]{1,0:T(8,128)(2,1)S(1)}, bf16[224,256]{1,0:T(8,128)(2,1)S(1)}, u32[]{:S(2)}, u32[]{:S(2)}) collective-permute-start(bf16[224,256]{1,0:T(8,128)(2,1)S(1)} %multiply_convert_fusion), channel_id=1, source_target_pairs={{0,16},{8,24},{16,0},{24,8},{1,17},{9,25},{17,1},{25,9},{2,18},{10... | collective-permute-start | bytes 344072 | tf_op jit(solution)/shard_map/ppermute | solution.py:72
  81.9 7.9 %collective-permute-start.17 = (bf16[224,256]{1,0:T(8,128)(2,1)S(1)}, bf16[224,256]{1,0:T(8,128)(2,1)S(1)}, u32[]{:S(2)}, u32[]{:S(2)}) collective-permute-start(bf16[224,256]{1,0:T(8,128)(2,1)S(1)} %multiply_convert_fusion), channel_id=1, source_target_pairs={{0,8},{8,16},{16,24},{24,0},{1,9},{9,17},{17,25},{25,1},{2,10},{10... | collective-permute-start | bytes 344072 | tf_op jit(solution)/shard_map/ppermute | solution.py:72
  (6 other events, 5.4 us)

commit v4 on v3

--- a/solution.py
+++ b/solution.py
@@ -86,7 +86,7 @@
     last[...] = act_ref[frames - 2 :]
 
 
-def rows_kernel(where_ref, cot, later, earlier, act, for_even, for_odd, lefts, rights):
+def rows_kernel(where_ref, cot, later, earlier, act, after, for_even, for_odd, lefts, rights):
     _, height, width, _ = cot.shape
     even = where_ref[0] == 0
     for place, refs in enumerate(((cot, later), (earlier, act))):
@@ -103,24 +103,26 @@
 
 
 def both_sides(is_even, refs, shape):
+    shape = refs[0].shape if refs else shape
     by_even = refs[0][...] if len(refs) > 0 else jnp.zeros(shape, BF16)
     by_odd = refs[1][...] if len(refs) > 1 else jnp.zeros(shape, BF16)
     return jnp.where(is_even, by_odd, by_even), jnp.where(is_even, by_even, by_odd)
 
 
-def columns_kernel(count, where_ref, lefts, rights, *refs):
+def columns_kernel(count, slot, where_ref, lefts, rights, *refs):
     swapped, (for_even, for_odd) = refs[:count], refs[count:]
     _, frames, height, channels = lefts.shape
     even_h, even_w = where_ref[0] == 0, where_ref[1] == 0
     width = swapped[0].shape[2]
     above, below = both_sides(even_h, swapped, swapped[0].shape)
-    nothing = jnp.zeros((2, frames, CORNERS - 2, channels), F32)
+    nothing = jnp.zeros((2, slot - frames, channels), F32)
     sides = []
     for source, at in ((lefts, 0), (rights, width - 1)):
-        over = above.astype(F32)[:, :, at : at + 1, :]
-        under = below.astype(F32)[:, :, at : at + 1, :]
-        parts = [source[...].astype(F32), over, under, nothing]
-        sides.append(jnp.concatenate(parts, axis=2).astype(BF16))
+        over = above.astype(F32)[:, :, at, :]
+        under = below.astype(F32)[:, :, at, :]
+        columns = source[...].astype(F32).reshape(2, frames * height, channels)
+        parts = [columns, over, nothing, under, nothing]
+        sides.append(jnp.concatenate(parts, axis=1).astype(BF16))
     for_even[...] = jnp.where(even_w, sides[1], sides[0])
     for_odd[...] = jnp.where(even_w, sides[0], sides[1])
 
@@ -143,28 +145,51 @@
     return own.astype(BF16), other.astype(BF16)
 
 
-def bundle_kernel(chips, width, counts, where_ref, cot, later, act_t, *refs):
-    cot_edges, act_edges, mine, send = refs[sum(counts) :]
-    core, even_w = where_ref[0], where_ref[1] == 0
-    own, inner, channels = cot.shape
-    tall = inner // width + CORNERS
-    frames, size, half = mine.shape
-    rows = both_sides(core == 0, refs[: counts[0]], (2, frames, width, channels))
-    columns = both_sides(even_w, refs[counts[0] : sum(counts)], (2, frames, tall, channels))
-    for place, target in enumerate((cot_edges, act_edges)):
-        target[...] = jnp.concatenate([side[place] for side in rows + columns], axis=1)
-    cells = act_t.shape[1]
+def own_kernel(chips, where_ref, cot, act_t, mine, send):
+    core = where_ref[0]
+    frames, inner, half = mine.shape
+    channels, cells = act_t.shape
     at = cells // half * channels
     for block in range(cells // half):
         send[block * channels : (block + 1) * channels] = act_t[
             :, block * half : (block + 1) * half
         ]
     for t in range(frames):
-        inside, inside_send = halves(core, cot[t] if t < own else later[t - own], chips)
+        inside, inside_send = halves(core, cot[t], chips)
+        mine[t] = inside
+        send[at + t * inner : at + (t + 1) * inner] = inside_send
+
+
+def bundle_kernel(chips, slot, counts, where_ref, later, *refs):
+    cot_edges, act_edges, mine, send = refs[sum(counts) :]
+    core, even_w = where_ref[0], where_ref[1] == 0
+    more, inner, channels = later.shape
+    frames, around, _ = cot_edges.shape
+    rows = both_sides(core == 0, refs[: counts[0]], None)
+    width = rows[0].shape[2]
+    height = inner // width
+    packed = (2, frames * height + 2 * slot, channels)
+    columns = both_sides(even_w, refs[counts[0] : sum(counts)], packed)
+    columns = [side.astype(F32) for side in columns]
+    nothing = jnp.zeros((frames, CORNERS - 2, channels), F32)
+    at = frames * height
+    for place, target in enumerate((cot_edges, act_edges)):
+        parts = [side[place].astype(F32) for side in rows]
+        for side in columns:
+            parts.append(side[place, :at].reshape(frames, height, channels))
+            parts.append(side[place, at : at + frames][:, None, :])
+            parts.append(side[place, at + slot : at + slot + frames][:, None, :])
+            parts.append(nothing)
+        target[...] = jnp.concatenate(parts, axis=1).astype(BF16)
+    for t in range(more):
+        inside, inside_send = halves(core, later[t], chips)
+        mine[t * inner : (t + 1) * inner] = inside
+        send[t * inner : (t + 1) * inner] = inside_send
+    at = more * inner
+    for t in range(frames):
         outside, outside_send = halves(core, cot_edges[t], chips)
-        mine[t, :inner], mine[t, inner:] = inside, outside
-        send[at + t * size : at + t * size + inner] = inside_send
-        send[at + t * size + inner : at + (t + 1) * size] = outside_send
+        mine[at + t * around : at + (t + 1) * around] = outside
+        send[at + t * around : at + (t + 1) * around] = outside_send
 
 
 def spread_frame(center, edges, height, width, target, at):
@@ -186,7 +211,8 @@
 
 def taps_kernel(height, width, all_taps, *refs):
     inner = height * width
-    places, act_a, mine, other, *outs, terms_ref, spread_a, spread_b = refs
+    places, act_a, *rest = refs
+    mine, mine_more, other, other_more, *outs, terms_ref, spread_a, spread_b = rest
     count = len(outs)
     channels, cells = act_a.shape
     frames = cells // inner
@@ -194,16 +220,21 @@
     spreads = (spread_a, spread_b)
     step = (height + 2) * width
     blocks = cells // part
-    tall = mine.shape[1]
+    more = 2 * inner
+    around = (mine_more.shape[0] - more) // (frames + 2)
     lowest = 2 - max(tap[0] for tap in all_taps)
     for side, spread in enumerate(spreads):
         for at in range(lowest, frames + 2 - min(tap[0] for tap in all_taps)):
-            if side == 0:
-                frame = mine[at]
+            extra = (mine_more, other_more)[side]
+            if at >= frames:
+                center = extra[(at - frames) * inner : (at - frames + 1) * inner]
+            elif side == 0:
+                center = mine[at]
             else:
-                start = blocks * channels + at * tall
-                frame = other[start : start + tall]
-            spread_frame(frame[:inner], frame[inner:], height, width, spread, (at - lowest) * step)
+                start = blocks * channels + at * inner
+                center = other[start : start + inner]
+            edges = extra[more + at * around : more + (at + 1) * around]
+            spread_frame(center, edges, height, width, spread, (at - lowest) * step)
     acts = jnp.concatenate(
         [act_a[...]] + [other[b * channels : (b + 1) * channels] for b in range(blocks)], axis=1
     )
@@ -278,17 +309,19 @@
             frame += 1
 
 
-def forward_kernel(height, width, x_ref, earlier, act, edges, weight, after, out, spread):
+def forward_kernel(height, width, x_ref, earlier, act, edges, weight, after, out, token, spread):
     frames = act.shape[0]
+    token[...] = jnp.zeros_like(token)
     spread_all(height, width, (earlier, act), edges, spread)
     mixed = conv_sum(height, width, frames, spread, weight, False)
     out[...] = (x_ref[...].astype(F32) + mixed).astype(BF16)
 
 
 def backward_kernel(
-    height, width, x_ref, gain_ref, cot, later, edges, weight, after, out, spread
+    height, width, x_ref, gain_ref, cot, later, edges, weight, after, out, token, spread
 ):
     frames = cot.shape[0]
+    token[...] = jnp.zeros_like(token)
     spread_all(height, width, (cot, later), edges, spread)
     grad_act = conv_sum(height, width, frames, spread, weight, True)
     values = x_ref[...].astype(F32)
@@ -320,6 +353,7 @@
     chip = me_h // 2
     where = jnp.stack([me_h % 2, me_w % 2]).astype(jnp.int32)
     flat_x = features.reshape(cells, channels)
+    slot = -(-(frames + 2) // 8) * 8
     framed_cot = cotangent.reshape(frames, inner, channels)
     gain = norm_gain.reshape(1, channels)
     product = 2 * cells * channels * channels
@@ -341,6 +375,19 @@
     )(features, gain)
     later = shift_line(cotangent[:2], "ta", -1)
     earlier = shift_line(last, "ta", 1)
+    mine, send = call(
+        functools.partial(own_kernel, chips),
+        (
+            shape_of(frames, inner, half),
+            shape_of(cells // half * channels + cells, half),
+        ),
+        0,
+        2 * size,
+        scalars=1,
+        arrays=2,
+        limit=12,
+    )(where, framed_cot, act_t)
+    other = swap_core(send)
     for_even, for_odd, lefts, rights = call(
         rows_kernel,
         (
@@ -353,13 +400,14 @@
         2 * size,
         scalars=1,
         arrays=4,
+        left=1,
         limit=12,
-    )(where, cotangent, later, earlier, act)
+    )(where, cotangent, later, earlier, act, other)
     rows = [swap_pairs(for_even, "ha", 0), swap_pairs(for_odd, "ha", 1)]
     rows = [array for array in rows if array is not None]
     for_even, for_odd = call(
-        functools.partial(columns_kernel, len(rows)),
-        (shape_of(2, frames + 2, tall, channels),) * 2,
+        functools.partial(columns_kernel, len(rows), slot),
+        (shape_of(2, (frames + 2) * height + 2 * slot, channels),) * 2,
         0,
         size // 2,
         scalars=1,
@@ -368,20 +416,17 @@
     columns = [swap_pairs(for_even, "wa", 0), swap_pairs(for_odd, "wa", 1)]
     columns = [array for array in columns if array is not None]
     later = later.reshape(2, inner, channels)
-    cot_edges, act_edges, mine, send = call(
-        functools.partial(bundle_kernel, chips, width, (len(rows), len(columns))),
+    cot_edges, act_edges, mine_more, send_more = call(
+        functools.partial(bundle_kernel, chips, slot, (len(rows), len(columns))),
         (shape_of(frames + 2, around, channels),) * 2
-        + (
-            shape_of(frames + 2, inner + around, half),
-            shape_of(cells // half * channels + (frames + 2) * (inner + around), half),
-        ),
+        + (shape_of(2 * inner + (frames + 2) * around, half),) * 2,
         0,
-        3 * size,
+        size,
         scalars=1,
-        arrays=3 + len(rows) + len(columns),
+        arrays=1 + len(rows) + len(columns),
         limit=12,
-    )(where, framed_cot, later, act_t, *rows, *columns)
-    other = swap_core(send)
+    )(where, later, *rows, *columns)
+    other_more = swap_core(send_more)
 
     count = chips * cols_of
     moves = [(du, dw) for du in range(chips) for dw in range(cols_of)]
@@ -403,19 +448,19 @@
             4 * size,
             (pltpu.VMEM((len(taps), half, channels), F32), spread, spread),
             scalars=1,
-            arrays=3,
-            limit=24,
-        )(places, act_t, mine, other)
+            arrays=5,
+            limit=16,
+        )(places, act_t, mine, mine_more, other, other_more)
         moved = [to_chip(piece, *move) for piece, move in zip(pieces[1:], moves[1:])]
         terms.append([pieces[0]] + moved)
         after = pieces[0]
 
     framed_act = act.reshape(frames, inner, channels)
     earlier = earlier.reshape(2, inner, channels)
-    flat = shape_of(cells, channels)
+    flat = (shape_of(cells, channels), shape_of(8, 128, dtype=F32))
     spread = pltpu.VMEM((3, (frames + 2) * (height + 2) * width, channels), BF16)
     touched = conv_weight.size * 2 + 4 * size
-    grad_features = call(
+    grad_features, token_a = call(
         functools.partial(backward_kernel, height, width),
         flat,
         27 * product,
@@ -423,9 +468,9 @@
         (spread,),
         arrays=6,
         left=1,
-        limit=24,
+        limit=16,
     )(flat_x, gain, framed_cot, later, cot_edges, conv_weight, after)
-    decoded = call(
+    decoded, token_b = call(
         functools.partial(forward_kernel, height, width),
         flat,
         27 * product,
@@ -433,7 +478,7 @@
         (spread,),
         arrays=5,
         left=1,
-        limit=24,
+        limit=16,
     )(flat_x, earlier, framed_act, act_edges, conv_weight, after)
 
     part = -(-27 * owned // (16 * depth)) * 16
@@ -449,7 +494,7 @@
         scalars=1,
         arrays=count * len(terms),
         left=2,
-    )(owners, *terms[0], *terms[1], grad_features, decoded)
+    )(owners, *terms[0], *terms[1], token_a, token_b)
     for by, sent in enumerate(sends, 1):
         own = own + ring(sent, "ta", by).astype(F32)
     scale = float(cells * depth * rows_of * cols_of) ** (-0.5)

time: 91.6 us -> 88 us (0.961)
  local copies, waits for them, and re-layouts: 6.51 us -> 3.89 us
  waiting for transfers between devices: 31.5 us -> 30.2 us
    unnamed x31 -> x25, local copies, waits for them, and re-layouts: 5.46 us -> 3.79 us
    ppermute x1 -> x2, waiting for transfers between devices: 2.37 us -> 1.24 us  [swap_core(): return lax.ppermute(array, 'ha', [(i, i ^ 1) for i in range(length)])]
    slice x1, local copies, waits for them, and re-layouts: 0.97 us -> 0.02 us  [body(): later = shift_line(cotangent[:2], 'ta', -1)]
    ppermute x1 -> x2, starting transfers between devices: 4.27 us -> 4.79 us  [swap_core(): return lax.ppermute(array, 'ha', [(i, i ^ 1) for i in range(length)])]
    pallas_call x2 -> x3, Pallas kernels: 3.36 us -> 3.63 us  [the longest x1 1.53 us: body(): call(functools.partial(bundle_kernel, chips, slot, (len(rows), len(column...]
  transfers between devices with their start and end apart: 18 -> 19, of which waited for: 10 -> 10; matrix products, arithmetic and copies ran while one was open for 1% -> 0% of each run, Pallas kernels for 14% -> 15%
where the time goes in v4:
time: 88 us; the launch traced here: 87.4 us
  waiting for transfers between devices  30.2 us (34%)
  starting transfers between devices  29.6 us (34%)
  Pallas kernels  21.5 us (24%)
  local copies, waits for them, and re-layouts  3.89 us (4%)
  other arithmetic  1.29 us (1%)
  between operations  0.89 us (1%)
    ppermute x6, waiting for transfers between devices, ring(): lax.ppermute(array, axis, [(i, (i + by) % length) for i in range(length)])  12.6 us
    ppermute x6, starting transfers between devices, ring(): lax.ppermute(array, axis, [(i, (i + by) % length) for i in range(length)])  9.34 us
    ppermute x2, waiting for transfers between devices, shift_line(): return lax.ppermute(array, axis, pairs)  9.01 us
    ppermute x6, starting transfers between devices, to_chip(): return lax.ppermute(array, ('ha', 'wa'), pairs)  7.44 us
    pallas_call x2, Pallas kernels, body(): call(functools.partial(taps_kernel, height, width, taps), tuple((shape_of...  5.89 us
    ppermute x2, starting transfers between devices, shift_line(): return lax.ppermute(array, axis, pairs)  5.8 us
    pallas_call x1, Pallas kernels, body(): call(functools.partial(backward_kernel, height, width), flat, 27 * produc...  5.08 us
    ppermute x2, starting transfers between devices, swap_core(): return lax.ppermute(array, 'ha', [(i, i ^ 1) for i in range(length)])  4.79 us
  transfers between devices with their start and end apart: 19, of which 10 were waited for; matrix products, arithmetic and copies ran while one was open for 0% of the time, Pallas kernels for 15%

profile of v4, /device:TPU:0, one launch (start us, length us, event | category | flops | bytes accessed | tf_op | source)
XLA Modules:
  0.0 87.4 jit_solution(4152647130365939591)
XLA Ops:
  5.3 4.5 %collective-permute-start = (bf16[2,16,16,256]{3,2,1,0:T(8,128)(2,1)S(1)}, bf16[2,16,16,256]{3,2,1,0:T(8,128)(2,1)S(1)}, u32[]{:S(2)}, u32[]{:S(2)}) collective-permute-start(bf16[2,16,16,256]{3,2,1,0:T(8,128)(2,1)S(1)} %get-tuple-element.33), channel_id=1, source_target_pairs={{0,8},{8,16},{16,24},{1,9},{9,17},{17,25},{2,10},{10,18},{18,26},{... | collective-permute-start | bytes 786440 | tf_op jit(solution)/shard_map/ppermute | solution.py:42
  11.1 4.9 %collective-permute-done.earlier = bf16[2,16,16,256]{3,2,1,0:T(8,128)(2,1)S(1)} collective-permute-done((bf16[2,16,16,256]{3,2,1,0:T(8,128)(2,1)S(1)}, bf16[2,16,16,256]{3,2,1,0:T(8,128)(2,1)S(1)}, u32[]{:S(2)}, u32[]{:S(2)}) %collective-permute-start) | collective-permute-done | bytes 262176 | tf_op jit(solution)/shard_map/ppermute | solution.py:42
  16.0 4.2 %collective-permute-done.1.later = bf16[2,16,16,256]{3,2,1,0:T(8,128)(2,1)S(1)} collective-permute-done((bf16[2,16,16,256]{3,2,1,0:T(8,128)(2,1)S(1)}, bf16[2,16,16,256]{3,2,1,0:T(8,128)(2,1)S(1)}, u32[]{:S(2)}, u32[]{:S(2)}) %collective-permute-start.1) | collective-permute-done | bytes 262176 | tf_op jit(solution)/shard_map/ppermute | solution.py:42
  23.7 1.5 %collective-permute-start.5 = (bf16[2,112,256]{2,1,0:T(8,128)(2,1)S(1)}, bf16[2,112,256]{2,1,0:T(8,128)(2,1)S(1)}, u32[]{:S(2)}, u32[]{:S(2)}) collective-permute-start(bf16[2,112,256]{2,1,0:T(8,128)(2,1)S(1)} %get-tuple-element.41), channel_id=1, source_target_pairs={{0,1},{1,0},{2,3},{3,2},{4,5},{5,4},{6,7},{7,6},{8,9},{9,8},{10,11... | collective-permute-start | bytes 344072 | tf_op jit(solution)/shard_map/ppermute | solution.py:55
  25.2 3.3 %collective-permute-done.5.refs_2_ = bf16[2,112,256]{2,1,0:T(8,128)(2,1)S(1)} collective-permute-done((bf16[2,112,256]{2,1,0:T(8,128)(2,1)S(1)}, bf16[2,112,256]{2,1,0:T(8,128)(2,1)S(1)}, u32[]{:S(2)}, u32[]{:S(2)}) %collective-permute-start.5) | collective-permute-done | bytes 114720 | tf_op jit(solution)/shard_map/ppermute | solution.py:55
  28.5 1.5 %shard_map.71 = (bf16[6,96,256]{2,1,0:T(8,128)(2,1)S(1)}, bf16[6,96,256]{2,1,0:T(8,128)(2,1)S(1)}, bf16[1088,128]{1,0:T(8,128)(2,1)S(1)}, bf16[1088,128]{1,0:T(8,128)(2,1)}) custom-call(s32[2]{0:T(128)S(1)} %pad_add_fusion.where_ref, bf16[2,256,256]{2,1,0:T(8,128)(2,1)S(1)} %bitcast.38, bf16[2,6,16,256]{3,2,1,0:T(8,128)(2,1)S(1)} %collective-permute-done.3.refs_0_, ...), custom_call_target="tpu_custom_call" | custom-call | bytes 524288 | tf_op jit(solution)/shard_map/pallas_call | solution.py:419
  30.1 4.3 %collective-permute-start.6 = (bf16[1088,128]{1,0:T(8,128)(2,1)}, bf16[1088,128]{1,0:T(8,128)(2,1)S(1)}, u32[]{:S(2)}, u32[]{:S(2)}) collective-permute-start(bf16[1088,128]{1,0:T(8,128)(2,1)} %get-tuple-element.45), channel_id=1, source_target_pairs={{0,2},{2,0},{4,6},{6,4},{1,3},{3,1},{5,7},{7,5},{8,10},{10,8},{12,... | collective-permute-start | bytes 835592 | tf_op jit(solution)/shard_map/ppermute | solution.py:47
  36.7 2.5 %shard_map.75 = (f32[10,32,256]{2,1,0:T(8,128)S(1)}, bf16[10,32,256]{2,1,0:T(8,128)(2,1)S(1)}, bf16[10,32,256]{2,1,0:T(8,128)(2,1)S(1)}, bf16[10,32,256]{2,1,0:T(8,128)(2,1)S(1)}) custom-call(s32[4]{0:T(128)S(1)} %pad_add_fusion.1.refs_0_, bf16[256,1024]{1,0:T(8,128)(2,1)S(1)} %get-tuple-element.35.act_t.refs_1_, bf16[4,256,128]{2,1,0:T(8,128)(2,1)S(1)} %copy-done.8, ...), custom_call_target="tpu_custom_call" | custom-call | flops 1342177280 | bytes 2097152 | tf_op jit(solution)/shard_map/pallas_call | solution.py:441
  39.1 1.6 %collective-permute-start.7 = (bf16[10,32,256]{2,1,0:T(8,128)(2,1)S(1)}, bf16[10,32,256]{2,1,0:T(8,128)(2,1)S(1)}, u32[]{:S(2)}, u32[]{:S(2)}) collective-permute-start(bf16[10,32,256]{2,1,0:T(8,128)(2,1)S(1)} %get-tuple-element.51), channel_id=1, source_target_pairs={{0,1},{1,0},{2,3},{3,2},{4,5},{5,4},{6,7},{7,6},{8,9},{9,8},{10,11... | collective-permute-start | bytes 491528 | tf_op jit(solution)/shard_map/ppermute | solution.py:67
  40.7 2.2 %collective-permute-start.8 = (bf16[10,32,256]{2,1,0:T(8,128)(2,1)S(1)}, bf16[10,32,256]{2,1,0:T(8,128)(2,1)S(1)}, u32[]{:S(2)}, u32[]{:S(2)}) collective-permute-start(bf16[10,32,256]{2,1,0:T(8,128)(2,1)S(1)} %get-tuple-element.52), channel_id=1, source_target_pairs={{0,4},{1,5},{2,6},{3,7},{4,0},{5,1},{6,2},{7,3},{8,12},{9,13},{10,... | collective-permute-start | bytes 491528 | tf_op jit(solution)/shard_map/ppermute | solution.py:67
  43.1 3.4 %shard_map.72 = (f32[17,32,256]{2,1,0:T(8,128)S(1)}, bf16[17,32,256]{2,1,0:T(8,128)(2,1)S(1)}, bf16[17,32,256]{2,1,0:T(8,128)(2,1)S(1)}, bf16[17,32,256]{2,1,0:T(8,128)(2,1)S(1)}) custom-call(s32[4]{0:T(128)S(1)} %pad_add_fusion.1.refs_0_, bf16[256,1024]{1,0:T(8,128)(2,1)S(1)} %get-tuple-element.35.act_t.refs_1_, bf16[4,256,128]{2,1,0:T(8,128)(2,1)S(1)} %copy-done.8, ...), custom_call_target="tpu_custom_call" | custom-call | flops 2281701376 | bytes 2097152 | tf_op jit(solution)/shard_map/pallas_call | solution.py:441
  46.5 1.5 %collective-permute-start.10 = (bf16[17,32,256]{2,1,0:T(8,128)(2,1)S(1)}, bf16[17,32,256]{2,1,0:T(8,128)(2,1)S(1)}, u32[]{:S(2)}, u32[]{:S(2)}) collective-permute-start(bf16[17,32,256]{2,1,0:T(8,128)(2,1)S(1)} %get-tuple-element.54), channel_id=1, source_target_pairs={{0,1},{1,0},{2,3},{3,2},{4,5},{5,4},{6,7},{7,6},{8,9},{9,8},{10,11... | collective-permute-start | bytes 835592 | tf_op jit(solution)/shard_map/ppermute | solution.py:67
  48.0 2.0 %collective-permute-start.11 = (bf16[17,32,256]{2,1,0:T(8,128)(2,1)S(1)}, bf16[17,32,256]{2,1,0:T(8,128)(2,1)S(1)}, u32[]{:S(2)}, u32[]{:S(2)}) collective-permute-start(bf16[17,32,256]{2,1,0:T(8,128)(2,1)S(1)} %get-tuple-element.55), channel_id=1, source_target_pairs={{0,4},{1,5},{2,6},{3,7},{4,0},{5,1},{6,2},{7,3},{8,12},{9,13},{10,... | collective-permute-start | bytes 835592 | tf_op jit(solution)/shard_map/ppermute | solution.py:67
  50.0 5.1 %shard_map.74 = (bf16[1024,256]{1,0:T(8,128)(2,1)}, f32[8,128]{1,0:T(8,128)S(1)}) custom-call(bf16[1024,256]{1,0:T(8,128)(2,1)S(1)} %bitcast.41, f32[1,256]{1,0:T(1,128)S(1)} %bitcast.45, bf16[4,256,256]{2,1,0:T(8,128)(2,1)S(1)} %bitcast.37, bf16[2,256,256]{2,1,0:T(8,128)(2,1)S(1)} %bitcast.39, bf16[6,96,256]{2,1,0:T(8,128)(2,1)S(1)} %get-tuple-element.48.edges, ...), custom_call_target="tpu_custom_call" | custom-call | flops 3623878656 | bytes 5636096 | tf_op jit(solution)/shard_map/pallas_call | solution.py:463
  55.1 4.7 %shard_map.73 = (bf16[1024,256]{1,0:T(8,128)(2,1)}, f32[8,128]{1,0:T(8,128)S(1)}) custom-call(bf16[1024,256]{1,0:T(8,128)(2,1)S(1)} %bitcast.42, bf16[2,256,256]{2,1,0:T(8,128)(2,1)S(1)} %bitcast.43, bf16[4,256,256]{2,1,0:T(8,128)(2,1)S(1)} %bitcast.40, bf16[6,96,256]{2,1,0:T(8,128)(2,1)S(1)} %get-tuple-element.42.edges, ...), custom_call_target="tpu_custom_call" | custom-call | flops 3623878656 | bytes 5636096 | tf_op jit(solution)/shard_map/pallas_call | solution.py:473
  59.8 3.5 %collective-permute-done.12.refs_7_ = bf16[17,32,256]{2,1,0:T(8,128)(2,1)S(1)} collective-permute-done((bf16[17,32,256]{2,1,0:T(8,128)(2,1)S(1)}, bf16[17,32,256]{2,1,0:T(8,128)(2,1)S(1)}, u32[]{:S(2)}, u32[]{:S(2)}) %collective-permute-start.12) | collective-permute-done | bytes 278560 | tf_op jit(solution)/shard_map/ppermute | solution.py:67
  64.2 1.6 %collective-permute-start.15 = (bf16[224,256]{1,0:T(8,128)(2,1)S(1)}, bf16[224,256]{1,0:T(8,128)(2,1)S(1)}, u32[]{:S(2)}, u32[]{:S(2)}) collective-permute-start(bf16[224,256]{1,0:T(8,128)(2,1)S(1)} %get-tuple-element.62), channel_id=1, source_target_pairs={{0,24},{8,0},{16,8},{24,16},{1,25},{9,1},{17,9},{25,17},{2,26},{10... | collective-permute-start | bytes 344072 | tf_op jit(solution)/shard_map/ppermute | solution.py:72
  65.8 1.5 %collective-permute-start.14 = (bf16[224,256]{1,0:T(8,128)(2,1)S(1)}, bf16[224,256]{1,0:T(8,128)(2,1)S(1)}, u32[]{:S(2)}, u32[]{:S(2)}) collective-permute-start(bf16[224,256]{1,0:T(8,128)(2,1)S(1)} %get-tuple-element.61), channel_id=1, source_target_pairs={{0,16},{8,24},{16,0},{24,8},{1,17},{9,25},{17,1},{25,9},{2,18},{10... | collective-permute-start | bytes 344072 | tf_op jit(solution)/shard_map/ppermute | solution.py:72
  67.3 1.6 %collective-permute-start.13 = (bf16[224,256]{1,0:T(8,128)(2,1)S(1)}, bf16[224,256]{1,0:T(8,128)(2,1)S(1)}, u32[]{:S(2)}, u32[]{:S(2)}) collective-permute-start(bf16[224,256]{1,0:T(8,128)(2,1)S(1)} %get-tuple-element.60), channel_id=1, source_target_pairs={{0,8},{8,16},{16,24},{24,0},{1,9},{9,17},{17,25},{25,1},{2,10},{10... | collective-permute-start | bytes 344072 | tf_op jit(solution)/shard_map/ppermute | solution.py:72
  69.2 6.3 %collective-permute-done.14 = bf16[224,256]{1,0:T(8,128)(2,1)S(1)} collective-permute-done((bf16[224,256]{1,0:T(8,128)(2,1)S(1)}, bf16[224,256]{1,0:T(8,128)(2,1)S(1)}, u32[]{:S(2)}, u32[]{:S(2)}) %collective-permute-start.14) | collective-permute-done | bytes 114720 | tf_op jit(solution)/shard_map/ppermute | solution.py:72
  76.7 1.6 %collective-permute-start.17 = (bf16[224,256]{1,0:T(8,128)(2,1)S(1)}, bf16[224,256]{1,0:T(8,128)(2,1)S(1)}, u32[]{:S(2)}, u32[]{:S(2)}) collective-permute-start(bf16[224,256]{1,0:T(8,128)(2,1)S(1)} %multiply_convert_fusion), channel_id=1, source_target_pairs={{0,16},{8,24},{16,0},{24,8},{1,17},{9,25},{17,1},{25,9},{2,18},{10... | collective-permute-start | bytes 344072 | tf_op jit(solution)/shard_map/ppermute | solution.py:72
  78.4 1.9 %collective-permute-start.18 = (bf16[224,256]{1,0:T(8,128)(2,1)S(1)}, bf16[224,256]{1,0:T(8,128)(2,1)S(1)}, u32[]{:S(2)}, u32[]{:S(2)}) collective-permute-start(bf16[224,256]{1,0:T(8,128)(2,1)S(1)} %multiply_convert_fusion), channel_id=1, source_target_pairs={{0,8},{8,16},{16,24},{24,0},{1,9},{9,17},{17,25},{25,1},{2,10},{10... | collective-permute-start | bytes 344072 | tf_op jit(solution)/shard_map/ppermute | solution.py:72
  80.3 1.4 %collective-permute-done.16 = bf16[224,256]{1,0:T(8,128)(2,1)S(1)} collective-permute-done((bf16[224,256]{1,0:T(8,128)(2,1)S(1)}, bf16[224,256]{1,0:T(8,128)(2,1)S(1)}, u32[]{:S(2)}, u32[]{:S(2)}) %collective-permute-start.16) | collective-permute-done | bytes 114720 | tf_op jit(solution)/shard_map/ppermute | solution.py:72
  81.7 4.5 %collective-permute-done.17 = bf16[224,256]{1,0:T(8,128)(2,1)S(1)} collective-permute-done((bf16[224,256]{1,0:T(8,128)(2,1)S(1)}, bf16[224,256]{1,0:T(8,128)(2,1)S(1)}, u32[]{:S(2)}, u32[]{:S(2)}) %collective-permute-start.17) | collective-permute-done | bytes 114720 | tf_op jit(solution)/shard_map/ppermute | solution.py:72
  (58 shorter events, 15.5 us)
Async XLA Ops:
  4.8 25.3 %copy-start.7 = (bf16[4,256,128]{2,1,0:T(8,128)(2,1)}, bf16[4,256,128]{2,1,0:T(8,128)(2,1)S(1)}, u32[]{:S(2)}) copy-start(bf16[4,256,128]{2,1,0:T(8,128)(2,1)S(1)} %get-tuple-element.43.refs_2_) | copy-start | bytes 786436
  4.8 15.4 %collective-permute-start.2 = (bf16[3072,128]{1,0:T(8,128)(2,1)S(1)}, bf16[3072,128]{1,0:T(8,128)(2,1)S(1)}, u32[]{:S(2)}, u32[]{:S(2)}) collective-permute-start(bf16[3072,128]{1,0:T(8,128)(2,1)S(1)} %get-tuple-element.36), channel_id=1, source_target_pairs={{0,2},{2,0},{4,6},{6,4},{1,3},{3,1},{5,7},{7,5},{8,10},{10,8},{12,... | collective-permute-start | bytes 2359304 | tf_op jit(solution)/shard_map/ppermute | solution.py:47
  5.3 10.7 %collective-permute-start = (bf16[2,16,16,256]{3,2,1,0:T(8,128)(2,1)S(1)}, bf16[2,16,16,256]{3,2,1,0:T(8,128)(2,1)S(1)}, u32[]{:S(2)}, u32[]{:S(2)}) collective-permute-start(bf16[2,16,16,256]{3,2,1,0:T(8,128)(2,1)S(1)} %get-tuple-element.33), channel_id=1, source_target_pairs={{0,8},{8,16},{16,24},{1,9},{9,17},{17,25},{2,10},{10,18},{18,26},{... | collective-permute-start | bytes 786440 | tf_op jit(solution)/shard_map/ppermute | solution.py:42
  9.8 10.3 %collective-permute-start.1 = (bf16[2,16,16,256]{3,2,1,0:T(8,128)(2,1)S(1)}, bf16[2,16,16,256]{3,2,1,0:T(8,128)(2,1)S(1)}, u32[]{:S(2)}, u32[]{:S(2)}) collective-permute-start(bf16[2,16,16,256]{3,2,1,0:T(8,128)(2,1)S(1)} %slice.6), channel_id=1, source_target_pairs={{8,0},{16,8},{24,16},{9,1},{17,9},{25,17},{10,2},{18,10},{26,18},{... | collective-permute-start | bytes 786440 | tf_op jit(solution)/shard_map/ppermute | solution.py:42
  21.1 1.4 %collective-permute-start.3 = (bf16[2,6,16,256]{3,2,1,0:T(8,128)(2,1)S(1)}, bf16[2,6,16,256]{3,2,1,0:T(8,128)(2,1)S(1)}, u32[]{:S(2)}, u32[]{:S(2)}) collective-permute-start(bf16[2,6,16,256]{3,2,1,0:T(8,128)(2,1)S(1)} %get-tuple-element.37), channel_id=1, source_target_pairs={{0,2},{2,0},{4,6},{6,4},{1,3},{3,1},{5,7},{7,5},{8,10},{10,8},{12,... | collective-permute-start | bytes 294920 | tf_op jit(solution)/shard_map/ppermute | solution.py:55
  21.2 1.3 %collective-permute-start.4 = (bf16[2,6,16,256]{3,2,1,0:T(8,128)(2,1)S(1)}, bf16[2,6,16,256]{3,2,1,0:T(8,128)(2,1)S(1)}, u32[]{:S(2)}, u32[]{:S(2)}) collective-permute-start(bf16[2,6,16,256]{3,2,1,0:T(8,128)(2,1)S(1)} %get-tuple-element.38), channel_id=1, source_target_pairs={{2,4},{4,2},{3,5},{5,3},{10,12},{12,10},{11,13},{13,11},{18,20},{2... | collective-permute-start | bytes 294920 | tf_op jit(solution)/shard_map/ppermute | solution.py:55
  23.7 4.8 %collective-permute-start.5 = (bf16[2,112,256]{2,1,0:T(8,128)(2,1)S(1)}, bf16[2,112,256]{2,1,0:T(8,128)(2,1)S(1)}, u32[]{:S(2)}, u32[]{:S(2)}) collective-permute-start(bf16[2,112,256]{2,1,0:T(8,128)(2,1)S(1)} %get-tuple-element.41), channel_id=1, source_target_pairs={{0,1},{1,0},{2,3},{3,2},{4,5},{5,4},{6,7},{7,6},{8,9},{9,8},{10,11... | collective-permute-start | bytes 344072 | tf_op jit(solution)/shard_map/ppermute | solution.py:55
  30.1 5.7 %collective-permute-start.6 = (bf16[1088,128]{1,0:T(8,128)(2,1)}, bf16[1088,128]{1,0:T(8,128)(2,1)S(1)}, u32[]{:S(2)}, u32[]{:S(2)}) collective-permute-start(bf16[1088,128]{1,0:T(8,128)(2,1)} %get-tuple-element.45), channel_id=1, source_target_pairs={{0,2},{2,0},{4,6},{6,4},{1,3},{3,1},{5,7},{7,5},{8,10},{10,8},{12,... | collective-permute-start | bytes 835592 | tf_op jit(solution)/shard_map/ppermute | solution.py:47
  39.1 16.0 %collective-permute-start.7 = (bf16[10,32,256]{2,1,0:T(8,128)(2,1)S(1)}, bf16[10,32,256]{2,1,0:T(8,128)(2,1)S(1)}, u32[]{:S(2)}, u32[]{:S(2)}) collective-permute-start(bf16[10,32,256]{2,1,0:T(8,128)(2,1)S(1)} %get-tuple-element.51), channel_id=1, source_target_pairs={{0,1},{1,0},{2,3},{3,2},{4,5},{5,4},{6,7},{7,6},{8,9},{9,8},{10,11... | collective-permute-start | bytes 491528 | tf_op jit(solution)/shard_map/ppermute | solution.py:67
  40.7 19.1 %collective-permute-start.8 = (bf16[10,32,256]{2,1,0:T(8,128)(2,1)S(1)}, bf16[10,32,256]{2,1,0:T(8,128)(2,1)S(1)}, u32[]{:S(2)}, u32[]{:S(2)}) collective-permute-start(bf16[10,32,256]{2,1,0:T(8,128)(2,1)S(1)} %get-tuple-element.52), channel_id=1, source_target_pairs={{0,4},{1,5},{2,6},{3,7},{4,0},{5,1},{6,2},{7,3},{8,12},{9,13},{10,... | collective-permute-start | bytes 491528 | tf_op jit(solution)/shard_map/ppermute | solution.py:67
  43.0 7.1 %copy-start.1 = (bf16[4,16,16,256]{3,2,1,0:T(8,128)(2,1)S(1)}, bf16[4,16,16,256]{3,2,1,0:T(8,128)(2,1)}, u32[]{:S(2)}) copy-start(bf16[4,16,16,256]{3,2,1,0:T(8,128)(2,1)} %cot.1) | copy-start | bytes 1572868
  43.0 7.1 %copy-start.3 = (bf16[4,16,16,256]{3,2,1,0:T(8,128)(2,1)S(1)}, bf16[4,16,16,256]{3,2,1,0:T(8,128)(2,1)}, u32[]{:S(2)}) copy-start(bf16[4,16,16,256]{3,2,1,0:T(8,128)(2,1)} %x_ref.1) | copy-start | bytes 1572868
  43.0 7.1 %copy-start.5 = (f32[256]{0:T(256)S(1)}, f32[256]{0:T(256)}, u32[]{:S(2)}) copy-start(f32[256]{0:T(256)} %param.5) | copy-start | bytes 3076
  43.0 7.1 %copy-start.6 = (bf16[3,3,3,256,256]{4,3,2,1,0:T(8,128)(2,1)S(1)}, bf16[3,3,3,256,256]{4,3,2,1,0:T(8,128)(2,1)}, u32[]{:S(2)}) copy-start(bf16[3,3,3,256,256]{4,3,2,1,0:T(8,128)(2,1)} %weight.3) | copy-start | bytes 10616836
  43.0 16.8 %collective-permute-start.9 = (bf16[10,32,256]{2,1,0:T(8,128)(2,1)S(1)}, bf16[10,32,256]{2,1,0:T(8,128)(2,1)S(1)}, u32[]{:S(2)}, u32[]{:S(2)}) collective-permute-start(bf16[10,32,256]{2,1,0:T(8,128)(2,1)S(1)} %get-tuple-element.53), channel_id=1, source_target_pairs={{0,5},{1,4},{2,7},{3,6},{4,1},{5,0},{6,3},{7,2},{8,13},{9,12},{10,... | collective-permute-start | bytes 491528 | tf_op jit(solution)/shard_map/ppermute | solution.py:67
  46.5 13.3 %collective-permute-start.10 = (bf16[17,32,256]{2,1,0:T(8,128)(2,1)S(1)}, bf16[17,32,256]{2,1,0:T(8,128)(2,1)S(1)}, u32[]{:S(2)}, u32[]{:S(2)}) collective-permute-start(bf16[17,32,256]{2,1,0:T(8,128)(2,1)S(1)} %get-tuple-element.54), channel_id=1, source_target_pairs={{0,1},{1,0},{2,3},{3,2},{4,5},{5,4},{6,7},{7,6},{8,9},{9,8},{10,11... | collective-permute-start | bytes 835592 | tf_op jit(solution)/shard_map/ppermute | solution.py:67
  48.0 11.8 %collective-permute-start.11 = (bf16[17,32,256]{2,1,0:T(8,128)(2,1)S(1)}, bf16[17,32,256]{2,1,0:T(8,128)(2,1)S(1)}, u32[]{:S(2)}, u32[]{:S(2)}) collective-permute-start(bf16[17,32,256]{2,1,0:T(8,128)(2,1)S(1)} %get-tuple-element.55), channel_id=1, source_target_pairs={{0,4},{1,5},{2,6},{3,7},{4,0},{5,1},{6,2},{7,3},{8,12},{9,13},{10,... | collective-permute-start | bytes 835592 | tf_op jit(solution)/shard_map/ppermute | solution.py:67
  55.1 8.2 %collective-permute-start.12 = (bf16[17,32,256]{2,1,0:T(8,128)(2,1)S(1)}, bf16[17,32,256]{2,1,0:T(8,128)(2,1)S(1)}, u32[]{:S(2)}, u32[]{:S(2)}) collective-permute-start(bf16[17,32,256]{2,1,0:T(8,128)(2,1)S(1)} %get-tuple-element.56), channel_id=1, source_target_pairs={{0,5},{1,4},{2,7},{3,6},{4,1},{5,0},{6,3},{7,2},{8,13},{9,12},{10,... | collective-permute-start | bytes 835592 | tf_op jit(solution)/shard_map/ppermute | solution.py:67
  64.2 5.0 %collective-permute-start.15 = (bf16[224,256]{1,0:T(8,128)(2,1)S(1)}, bf16[224,256]{1,0:T(8,128)(2,1)S(1)}, u32[]{:S(2)}, u32[]{:S(2)}) collective-permute-start(bf16[224,256]{1,0:T(8,128)(2,1)S(1)} %get-tuple-element.62), channel_id=1, source_target_pairs={{0,24},{8,0},{16,8},{24,16},{1,25},{9,1},{17,9},{25,17},{2,26},{10... | collective-permute-start | bytes 344072 | tf_op jit(solution)/shard_map/ppermute | solution.py:72
  65.8 9.7 %collective-permute-start.14 = (bf16[224,256]{1,0:T(8,128)(2,1)S(1)}, bf16[224,256]{1,0:T(8,128)(2,1)S(1)}, u32[]{:S(2)}, u32[]{:S(2)}) collective-permute-start(bf16[224,256]{1,0:T(8,128)(2,1)S(1)} %get-tuple-element.61), channel_id=1, source_target_pairs={{0,16},{8,24},{16,0},{24,8},{1,17},{9,25},{17,1},{25,9},{2,18},{10... | collective-permute-start | bytes 344072 | tf_op jit(solution)/shard_map/ppermute | solution.py:72
  67.3 8.3 %collective-permute-start.13 = (bf16[224,256]{1,0:T(8,128)(2,1)S(1)}, bf16[224,256]{1,0:T(8,128)(2,1)S(1)}, u32[]{:S(2)}, u32[]{:S(2)}) collective-permute-start(bf16[224,256]{1,0:T(8,128)(2,1)S(1)} %get-tuple-element.60), channel_id=1, source_target_pairs={{0,8},{8,16},{16,24},{24,0},{1,9},{9,17},{17,25},{25,1},{2,10},{10... | collective-permute-start | bytes 344072 | tf_op jit(solution)/shard_map/ppermute | solution.py:72
  75.6 6.1 %collective-permute-start.16 = (bf16[224,256]{1,0:T(8,128)(2,1)S(1)}, bf16[224,256]{1,0:T(8,128)(2,1)S(1)}, u32[]{:S(2)}, u32[]{:S(2)}) collective-permute-start(bf16[224,256]{1,0:T(8,128)(2,1)S(1)} %multiply_convert_fusion), channel_id=1, source_target_pairs={{0,24},{8,0},{16,8},{24,16},{1,25},{9,1},{17,9},{25,17},{2,26},{10... | collective-permute-start | bytes 344072 | tf_op jit(solution)/shard_map/ppermute | solution.py:72
  76.7 9.5 %collective-permute-start.17 = (bf16[224,256]{1,0:T(8,128)(2,1)S(1)}, bf16[224,256]{1,0:T(8,128)(2,1)S(1)}, u32[]{:S(2)}, u32[]{:S(2)}) collective-permute-start(bf16[224,256]{1,0:T(8,128)(2,1)S(1)} %multiply_convert_fusion), channel_id=1, source_target_pairs={{0,16},{8,24},{16,0},{24,8},{1,17},{9,25},{17,1},{25,9},{2,18},{10... | collective-permute-start | bytes 344072 | tf_op jit(solution)/shard_map/ppermute | solution.py:72
  78.4 7.8 %collective-permute-start.18 = (bf16[224,256]{1,0:T(8,128)(2,1)S(1)}, bf16[224,256]{1,0:T(8,128)(2,1)S(1)}, u32[]{:S(2)}, u32[]{:S(2)}) collective-permute-start(bf16[224,256]{1,0:T(8,128)(2,1)S(1)} %multiply_convert_fusion), channel_id=1, source_target_pairs={{0,8},{8,16},{16,24},{24,0},{1,9},{9,17},{17,25},{25,1},{2,10},{10... | collective-permute-start | bytes 344072 | tf_op jit(solution)/shard_map/ppermute | solution.py:72
  (4 other events, 3.7 us)

commit v5 on v4

--- a/solution.py
+++ b/solution.py
@@ -8,7 +8,7 @@
 from jax.sharding import PartitionSpec as P
 
 EPSILON = 1e-06
-FIRST_TAPS = 10
+FIRST_TAPS = 8
 AXES = ("ta", "ha", "wa")
 BF16 = jnp.bfloat16
 F32 = jnp.float32
@@ -67,15 +67,19 @@
     return lax.ppermute(array, ("ha", "wa"), pairs)
 
 
-def ring(array, axis, by):
+def partner(place, by, length):
+    return place ^ by if length & (length - 1) == 0 else (place + by) % length
+
+
+def to_partner(array, axis, by):
     length = lax.axis_size(axis)
-    return lax.ppermute(array, axis, [(i, (i + by) % length) for i in range(length)])
+    return lax.ppermute(array, axis, [(i, partner(i, by, length)) for i in range(length)])
 
 
 CORNERS = 16
 
 
-def prepare_kernel(x_ref, gain_ref, act_ref, act_t_ref, last):
+def prepare_kernel(where_ref, x_ref, gain_ref, cot_ref, act_ref, act_t_ref, for_even, for_odd, kept):
     frames = x_ref.shape[0]
     values = x_ref[...].reshape(-1, x_ref.shape[-1]).astype(F32)
     inverse = lax.rsqrt(jnp.mean(values * values, axis=-1, keepdims=True) + EPSILON)
@@ -83,10 +87,17 @@
     activated = (normed * jax.nn.sigmoid(normed)).astype(BF16)
     act_ref[...] = activated.reshape(x_ref.shape)
     act_t_ref[...] = activated.T
-    last[...] = act_ref[frames - 2 :]
-
-
-def rows_kernel(where_ref, cot, later, earlier, act, after, for_even, for_odd, lefts, rights):
+    kept[...] = cot_ref[...]
+    last, first = act_ref[frames - 2 :], cot_ref[:2]
+    even = where_ref[2] == 0
+    for_even[...] = jnp.where(even, last, first)
+    for_odd[...] = jnp.where(even, first, last)
+
+
+def rows_kernel(count, where_ref, cot, act, *refs):
+    met = refs[:count]
+    later, earlier, for_even, for_odd, lefts, rights = refs[-6:]
+    earlier[...], later[...] = both_sides(where_ref[2] == 0, met, later.shape)
     _, height, width, _ = cot.shape
     even = where_ref[0] == 0
     for place, refs in enumerate(((cot, later), (earlier, act))):
@@ -110,7 +121,7 @@
 
 
 def columns_kernel(count, slot, where_ref, lefts, rights, *refs):
-    swapped, (for_even, for_odd) = refs[:count], refs[count:]
+    swapped, (for_even, for_odd) = refs[:count], refs[-2:]
     _, frames, height, channels = lefts.shape
     even_h, even_w = where_ref[0] == 0, where_ref[1] == 0
     width = swapped[0].shape[2]
@@ -145,7 +156,7 @@
     return own.astype(BF16), other.astype(BF16)
 
 
-def own_kernel(chips, where_ref, cot, act_t, mine, send):
+def own_kernel(chips, where_ref, cot, act_t, after, mine, send):
     core = where_ref[0]
     frames, inner, half = mine.shape
     channels, cells = act_t.shape
@@ -351,7 +362,7 @@
     half = channels // 2
     me_t, me_h, me_w = (lax.axis_index(axis) for axis in AXES)
     chip = me_h // 2
-    where = jnp.stack([me_h % 2, me_w % 2]).astype(jnp.int32)
+    where = jnp.stack([me_h % 2, me_w % 2, me_t % 2]).astype(jnp.int32)
     flat_x = features.reshape(cells, channels)
     slot = -(-(frames + 2) // 8) * 8
     framed_cot = cotangent.reshape(frames, inner, channels)
@@ -361,20 +372,39 @@
     tall = height + CORNERS
     around = 2 * width + 2 * tall
 
-    act, act_t, last = call(
+    act, act_t, for_even, for_odd, kept = call(
         prepare_kernel,
         (
             shape_of(*features.shape),
             shape_of(channels, cells),
             shape_of(2, *features.shape[1:]),
+            shape_of(2, *features.shape[1:]),
+            shape_of(*features.shape),
         ),
         10 * cells * channels,
+        3 * size,
+        scalars=1,
+        arrays=3,
+        limit=12,
+    )(where, features, gain, cotangent)
+    met = [swap_pairs(for_even, "ta", 0), swap_pairs(for_odd, "ta", 1)]
+    met = [array for array in met if array is not None]
+    later, earlier, for_even, for_odd, lefts, rights = call(
+        functools.partial(rows_kernel, len(met)),
+        (
+            shape_of(2, *features.shape[1:]),
+            shape_of(2, *features.shape[1:]),
+            shape_of(2, frames + 2, width, channels),
+            shape_of(2, frames + 2, width, channels),
+            shape_of(2, frames + 2, height, channels),
+            shape_of(2, frames + 2, height, channels),
+        ),
+        0,
         2 * size,
-        arrays=2,
+        scalars=1,
+        arrays=2 + len(met),
         limit=12,
-    )(features, gain)
-    later = shift_line(cotangent[:2], "ta", -1)
-    earlier = shift_line(last, "ta", 1)
+    )(where, kept, act, *met)
     mine, send = call(
         functools.partial(own_kernel, chips),
         (
@@ -385,24 +415,10 @@
         2 * size,
         scalars=1,
         arrays=2,
-        limit=12,
-    )(where, framed_cot, act_t)
-    other = swap_core(send)
-    for_even, for_odd, lefts, rights = call(
-        rows_kernel,
-        (
-            shape_of(2, frames + 2, width, channels),
-            shape_of(2, frames + 2, width, channels),
-            shape_of(2, frames + 2, height, channels),
-            shape_of(2, frames + 2, height, channels),
-        ),
-        0,
-        2 * size,
-        scalars=1,
-        arrays=4,
         left=1,
         limit=12,
-    )(where, cotangent, later, earlier, act, other)
+    )(where, kept.reshape(framed_cot.shape), act_t, for_even)
+    other = swap_core(send)
     rows = [swap_pairs(for_even, "ha", 0), swap_pairs(for_odd, "ha", 1)]
     rows = [array for array in rows if array is not None]
     for_even, for_odd = call(
@@ -412,7 +428,8 @@
         size // 2,
         scalars=1,
         arrays=2 + len(rows),
-    )(where, lefts, rights, *rows)
+        left=1,
+    )(where, lefts, rights, *rows, other)
     columns = [swap_pairs(for_even, "wa", 0), swap_pairs(for_odd, "wa", 1)]
     columns = [array for array in columns if array is not None]
     later = later.reshape(2, inner, channels)
@@ -482,7 +499,7 @@
     )(flat_x, earlier, framed_act, act_edges, conv_weight, after)
 
     part = -(-27 * owned // (16 * depth)) * 16
-    owners = jnp.stack([(me_t + by) % depth for by in range(depth)]).astype(jnp.int32)
+    owners = jnp.stack([partner(me_t, by, depth) for by in range(depth)]).astype(jnp.int32)
     own, *sends = call(
         functools.partial(parts_kernel, len(terms), count),
         tuple(
@@ -496,11 +513,17 @@
         left=2,
     )(owners, *terms[0], *terms[1], token_a, token_b)
     for by, sent in enumerate(sends, 1):
-        own = own + ring(sent, "ta", by).astype(F32)
+        own = own + to_partner(sent, "ta", by).astype(F32)
     scale = float(cells * depth * rows_of * cols_of) ** (-0.5)
     own = (own * scale).astype(BF16)
-    gathered = [ring(own, "ta", by) for by in range(depth - 1, 0, -1)] + [own]
-    gathered = jnp.roll(jnp.stack(gathered), me_t + 1, axis=0)
+    gathered = jnp.stack([own] + [to_partner(own, "ta", by) for by in range(1, depth)])
+    if depth & (depth - 1) == 0:
+        places = [me_t ^ rank for rank in range(depth)]
+    else:
+        places = [(me_t - rank) % depth for rank in range(depth)]
+    gathered = jnp.concatenate(
+        [lax.dynamic_index_in_dim(gathered, place, axis=0) for place in places]
+    )
     grad_weight = gathered.reshape(depth * part, channels)[: 27 * owned]
     grad_weight = jnp.swapaxes(grad_weight.reshape(27, owned, channels), 1, 2).astype(F32)
     return (

time: 88 us -> 85.9 us (0.976)
  waiting for transfers between devices: 30.2 us -> 29.1 us
    ppermute x8 -> x6, waiting for transfers between devices: 21.6 us -> 13.9 us  [to_partner(): lax.ppermute(array, axis, [(i, partner(i, by, length)) for i in range(len...]
    ppermute x3 -> x5, waiting for transfers between devices: 3.89 us -> 10 us  [swap_pairs(): return lax.ppermute(array, axis, pairs) if pairs else None]
    ppermute x3 -> x5, starting transfers between devices: 2.26 us -> 6.59 us  [swap_pairs(): return lax.ppermute(array, axis, pairs) if pairs else None]
    ppermute x8 -> x6, starting transfers between devices: 15.1 us -> 10.8 us  [to_partner(): lax.ppermute(array, axis, [(i, partner(i, by, length)) for i in range(len...]
    ppermute x2, starting transfers between devices: 4.79 us -> 3.07 us  [swap_core(): return lax.ppermute(array, 'ha', [(i, i ^ 1) for i in range(length)])]
    unnamed x25 -> x22, local copies, waits for them, and re-layouts: 3.79 us -> 3.75 us
  transfers between devices with their start and end apart: 19 -> 19, of which waited for: 10 -> 9; matrix products, arithmetic and copies ran while one was open for 0% -> 0% of each run, Pallas kernels for 15% -> 16%
where the time goes in v5:
time: 85.9 us; the launch traced here: 85.6 us
  waiting for transfers between devices  29.1 us (34%)
  starting transfers between devices  28.8 us (34%)
  Pallas kernels  21.6 us (25%)
  local copies, waits for them, and re-layouts  3.82 us (4%)
  other arithmetic  1.42 us (2%)
    ppermute x6, waiting for transfers between devices, to_partner(): lax.ppermute(array, axis, [(i, partner(i, by, length)) for i in range(len...  13.9 us
    ppermute x6, starting transfers between devices, to_partner(): lax.ppermute(array, axis, [(i, partner(i, by, length)) for i in range(len...  10.8 us
    ppermute x5, waiting for transfers between devices, swap_pairs(): return lax.ppermute(array, axis, pairs) if pairs else None  10 us
    ppermute x6, starting transfers between devices, to_chip(): return lax.ppermute(array, ('ha', 'wa'), pairs)  8.31 us
    ppermute x5, starting transfers between devices, swap_pairs(): return lax.ppermute(array, axis, pairs) if pairs else None  6.59 us
    pallas_call x2, Pallas kernels, body(): call(functools.partial(taps_kernel, height, width, taps), tuple((shape_of...  6.01 us
    pallas_call x1, Pallas kernels, body(): call(functools.partial(backward_kernel, height, width), flat, 27 * produc...  5.08 us
    pallas_call x1, Pallas kernels, body(): call(functools.partial(forward_kernel, height, width), flat, 27 * product...  4.67 us
  transfers between devices with their start and end apart: 19, of which 9 were waited for; matrix products, arithmetic and copies ran while one was open for 0% of the time, Pallas kernels for 16%

profile of v5, /device:TPU:0, one launch (start us, length us, event | category | flops | bytes accessed | tf_op | source)
XLA Modules:
  0.0 85.6 jit_solution(3676515441982314187)
XLA Ops:
  4.5 3.1 %collective-permute-start = (bf16[2,16,16,256]{3,2,1,0:T(8,128)(2,1)S(1)}, bf16[2,16,16,256]{3,2,1,0:T(8,128)(2,1)S(1)}, u32[]{:S(2)}, u32[]{:S(2)}) collective-permute-start(bf16[2,16,16,256]{3,2,1,0:T(8,128)(2,1)S(1)} %get-tuple-element.39), channel_id=1, source_target_pairs={{0,8},{8,0},{16,24},{24,16},{1,9},{9,1},{17,25},{25,17},{2,10},{10... | collective-permute-start | bytes 786440 | tf_op jit(solution)/shard_map/ppermute | solution.py:55
  8.2 5.6 %collective-permute-done.refs_0_ = bf16[2,16,16,256]{3,2,1,0:T(8,128)(2,1)S(1)} collective-permute-done((bf16[2,16,16,256]{3,2,1,0:T(8,128)(2,1)S(1)}, bf16[2,16,16,256]{3,2,1,0:T(8,128)(2,1)S(1)}, u32[]{:S(2)}, u32[]{:S(2)}) %collective-permute-start) | collective-permute-done | bytes 262176 | tf_op jit(solution)/shard_map/ppermute | solution.py:55
  13.9 1.0 %shard_map.68 = (bf16[2,16,16,256]{3,2,1,0:T(8,128)(2,1)S(1)}, bf16[2,16,16,256]{3,2,1,0:T(8,128)(2,1)S(1)}, bf16[2,6,16,256]{3,2,1,0:T(8,128)(2,1)S(1)}, bf16[2...) custom-call(s32[3]{0:T(128)S(1)} %pad_add_fusion.where_ref, ...), custom_call_target="tpu_custom_call" | custom-call | bytes 1048576 | tf_op jit(solution)/shard_map/pallas_call | solution.py:392
  17.0 1.3 %collective-permute-done.2.refs_0_ = bf16[2,6,16,256]{3,2,1,0:T(8,128)(2,1)S(1)} collective-permute-done((bf16[2,6,16,256]{3,2,1,0:T(8,128)(2,1)S(1)}, bf16[2,6,16,256]{3,2,1,0:T(8,128)(2,1)S(1)}, u32[]{:S(2)}, u32[]{:S(2)}) %collective-permute-start.2) | collective-permute-done | bytes 98336 | tf_op jit(solution)/shard_map/ppermute | solution.py:55
  18.3 1.3 %shard_map.70 = (bf16[2,112,256]{2,1,0:T(8,128)(2,1)S(1)}, bf16[2,112,256]{2,1,0:T(8,128)(2,1)}) custom-call(s32[3]{0:T(128)S(1)} %pad_add_fusion.where_ref, bf16[2,6,16,256]{3,2,1,0:T(8,128)(2,1)S(1)} %get-tuple-element.45.lefts, bf16[2,6,16,256]{3,2,1,0:T(8,128)(2,1)S(1)} %get-tuple-element.46.rights, ...), custom_call_target="tpu_custom_call" | custom-call | bytes 262144 | tf_op jit(solution)/shard_map/pallas_call | solution.py:424
  19.6 1.7 %collective-permute-start.5 = (bf16[2,112,256]{2,1,0:T(8,128)(2,1)S(1)}, bf16[2,112,256]{2,1,0:T(8,128)(2,1)S(1)}, u32[]{:S(2)}, u32[]{:S(2)}) collective-permute-start(bf16[2,112,256]{2,1,0:T(8,128)(2,1)S(1)} %get-tuple-element.49), channel_id=1, source_target_pairs={{0,1},{1,0},{2,3},{3,2},{4,5},{5,4},{6,7},{7,6},{8,9},{9,8},{10,11... | collective-permute-start | bytes 344072 | tf_op jit(solution)/shard_map/ppermute | solution.py:55
  21.2 3.1 %collective-permute-done.5.refs_2_ = bf16[2,112,256]{2,1,0:T(8,128)(2,1)S(1)} collective-permute-done((bf16[2,112,256]{2,1,0:T(8,128)(2,1)S(1)}, bf16[2,112,256]{2,1,0:T(8,128)(2,1)S(1)}, u32[]{:S(2)}, u32[]{:S(2)}) %collective-permute-start.5) | collective-permute-done | bytes 114720 | tf_op jit(solution)/shard_map/ppermute | solution.py:55
  25.2 3.0 %collective-permute-start.6 = (bf16[1088,128]{1,0:T(8,128)(2,1)S(1)}, bf16[1088,128]{1,0:T(8,128)(2,1)S(1)}, u32[]{:S(2)}, u32[]{:S(2)}) collective-permute-start(bf16[1088,128]{1,0:T(8,128)(2,1)S(1)} %get-tuple-element.53), channel_id=1, source_target_pairs={{0,2},{2,0},{4,6},{6,4},{1,3},{3,1},{5,7},{7,5},{8,10},{10,8},{12,... | collective-permute-start | bytes 835592 | tf_op jit(solution)/shard_map/ppermute | solution.py:47
  30.3 2.1 %shard_map.75 = (f32[8,32,256]{2,1,0:T(8,128)S(1)}, bf16[8,32,256]{2,1,0:T(8,128)(2,1)S(1)}, bf16[8,32,256]{2,1,0:T(8,128)(2,1)S(1)}, bf16[8,32,256]{2,1,0:T(8,128)(2,1)S(1)}) custom-call(s32[4]{0:T(128)S(1)} %pad_add_fusion.1.refs_0_, bf16[256,1024]{1,0:T(8,128)(2,1)S(1)} %get-tuple-element.47.act_t.refs_1_, bf16[4,256,128]{2,1,0:T(8,128)(2,1)S(1)} %copy-done.10, ...), custom_call_target="tpu_custom_call" | custom-call | flops 1073741824 | bytes 2097152 | tf_op jit(solution)/shard_map/pallas_call | solution.py:458
  32.4 1.8 %collective-permute-start.7 = (bf16[8,32,256]{2,1,0:T(8,128)(2,1)S(1)}, bf16[8,32,256]{2,1,0:T(8,128)(2,1)S(1)}, u32[]{:S(2)}, u32[]{:S(2)}) collective-permute-start(bf16[8,32,256]{2,1,0:T(8,128)(2,1)S(1)} %get-tuple-element.59), channel_id=1, source_target_pairs={{0,1},{1,0},{2,3},{3,2},{4,5},{5,4},{6,7},{7,6},{8,9},{9,8},{10,11... | collective-permute-start | bytes 393224 | tf_op jit(solution)/shard_map/ppermute | solution.py:67
  34.2 2.9 %collective-permute-start.8 = (bf16[8,32,256]{2,1,0:T(8,128)(2,1)S(1)}, bf16[8,32,256]{2,1,0:T(8,128)(2,1)S(1)}, u32[]{:S(2)}, u32[]{:S(2)}) collective-permute-start(bf16[8,32,256]{2,1,0:T(8,128)(2,1)S(1)} %get-tuple-element.60), channel_id=1, source_target_pairs={{0,4},{1,5},{2,6},{3,7},{4,0},{5,1},{6,2},{7,3},{8,12},{9,13},{10,... | collective-permute-start | bytes 393224 | tf_op jit(solution)/shard_map/ppermute | solution.py:67
  37.2 3.9 %shard_map.72 = (f32[19,32,256]{2,1,0:T(8,128)S(1)}, bf16[19,32,256]{2,1,0:T(8,128)(2,1)S(1)}, bf16[19,32,256]{2,1,0:T(8,128)(2,1)S(1)}, bf16[19,32,256]{2,1,0:T(8,128)(2,1)S(1)}) custom-call(s32[4]{0:T(128)S(1)} %pad_add_fusion.1.refs_0_, bf16[256,1024]{1,0:T(8,128)(2,1)S(1)} %get-tuple-element.47.act_t.refs_1_, bf16[4,256,128]{2,1,0:T(8,128)(2,1)S(1)} %copy-done.10, ...), custom_call_target="tpu_custom_call" | custom-call | flops 2550136832 | bytes 2097152 | tf_op jit(solution)/shard_map/pallas_call | solution.py:458
  41.1 1.5 %collective-permute-start.10 = (bf16[19,32,256]{2,1,0:T(8,128)(2,1)S(1)}, bf16[19,32,256]{2,1,0:T(8,128)(2,1)S(1)}, u32[]{:S(2)}, u32[]{:S(2)}) collective-permute-start(bf16[19,32,256]{2,1,0:T(8,128)(2,1)S(1)} %get-tuple-element.62), channel_id=1, source_target_pairs={{0,1},{1,0},{2,3},{3,2},{4,5},{5,4},{6,7},{7,6},{8,9},{9,8},{10,11... | collective-permute-start | bytes 933896 | tf_op jit(solution)/shard_map/ppermute | solution.py:67
  42.7 2.0 %collective-permute-start.11 = (bf16[19,32,256]{2,1,0:T(8,128)(2,1)S(1)}, bf16[19,32,256]{2,1,0:T(8,128)(2,1)S(1)}, u32[]{:S(2)}, u32[]{:S(2)}) collective-permute-start(bf16[19,32,256]{2,1,0:T(8,128)(2,1)S(1)} %get-tuple-element.63), channel_id=1, source_target_pairs={{0,4},{1,5},{2,6},{3,7},{4,0},{5,1},{6,2},{7,3},{8,12},{9,13},{10,... | collective-permute-start | bytes 933896 | tf_op jit(solution)/shard_map/ppermute | solution.py:67
  44.7 5.1 %shard_map.74 = (bf16[1024,256]{1,0:T(8,128)(2,1)}, f32[8,128]{1,0:T(8,128)S(1)}) custom-call(bf16[1024,256]{1,0:T(8,128)(2,1)S(1)} %bitcast.32, f32[1,256]{1,0:T(1,128)S(1)} %bitcast.38, bf16[4,256,256]{2,1,0:T(8,128)(2,1)S(1)} %bitcast.31, bf16[2,256,256]{2,1,0:T(8,128)(2,1)S(1)} %bitcast.36, bf16[6,96,256]{2,1,0:T(8,128)(2,1)S(1)} %get-tuple-element.56.edges, ...), custom_call_target="tpu_custom_call" | custom-call | flops 3623878656 | bytes 5636096 | tf_op jit(solution)/shard_map/pallas_call | solution.py:480
  49.8 4.7 %shard_map.73 = (bf16[1024,256]{1,0:T(8,128)(2,1)}, f32[8,128]{1,0:T(8,128)S(1)}) custom-call(bf16[1024,256]{1,0:T(8,128)(2,1)S(1)} %bitcast.33, bf16[2,256,256]{2,1,0:T(8,128)(2,1)S(1)} %bitcast.39, bf16[4,256,256]{2,1,0:T(8,128)(2,1)S(1)} %bitcast.34, bf16[6,96,256]{2,1,0:T(8,128)(2,1)S(1)} %get-tuple-element.50.edges, ...), custom_call_target="tpu_custom_call" | custom-call | flops 3623878656 | bytes 5636096 | tf_op jit(solution)/shard_map/pallas_call | solution.py:490
  54.5 4.2 %collective-permute-done.12.refs_7_ = bf16[19,32,256]{2,1,0:T(8,128)(2,1)S(1)} collective-permute-done((bf16[19,32,256]{2,1,0:T(8,128)(2,1)S(1)}, bf16[19,32,256]{2,1,0:T(8,128)(2,1)S(1)}, u32[]{:S(2)}, u32[]{:S(2)}) %collective-permute-start.12) | collective-permute-done | bytes 311328 | tf_op jit(solution)/shard_map/ppermute | solution.py:67
  59.6 3.7 %collective-permute-start.15 = (bf16[224,256]{1,0:T(8,128)(2,1)S(1)}, bf16[224,256]{1,0:T(8,128)(2,1)S(1)}, u32[]{:S(2)}, u32[]{:S(2)}) collective-permute-start(bf16[224,256]{1,0:T(8,128)(2,1)S(1)} %get-tuple-element.70), channel_id=1, source_target_pairs={{0,24},{8,16},{16,8},{24,0},{1,25},{9,17},{17,9},{25,1},{2,26},{10... | collective-permute-start | bytes 344072 | tf_op jit(solution)/shard_map/ppermute | solution.py:76
  63.2 2.5 %collective-permute-start.14 = (bf16[224,256]{1,0:T(8,128)(2,1)S(1)}, bf16[224,256]{1,0:T(8,128)(2,1)S(1)}, u32[]{:S(2)}, u32[]{:S(2)}) collective-permute-start(bf16[224,256]{1,0:T(8,128)(2,1)S(1)} %get-tuple-element.69), channel_id=1, source_target_pairs={{0,16},{8,24},{16,0},{24,8},{1,17},{9,25},{17,1},{25,9},{2,18},{10... | collective-permute-start | bytes 344072 | tf_op jit(solution)/shard_map/ppermute | solution.py:76
  66.8 5.9 %collective-permute-done.14 = bf16[224,256]{1,0:T(8,128)(2,1)S(1)} collective-permute-done((bf16[224,256]{1,0:T(8,128)(2,1)S(1)}, bf16[224,256]{1,0:T(8,128)(2,1)S(1)}, u32[]{:S(2)}, u32[]{:S(2)}) %collective-permute-start.14) | collective-permute-done | bytes 114720 | tf_op jit(solution)/shard_map/ppermute | solution.py:76
  72.7 3.4 %collective-permute-start.18 = (bf16[224,256]{1,0:T(8,128)(2,1)S(1)}, bf16[224,256]{1,0:T(8,128)(2,1)S(1)}, u32[]{:S(2)}, u32[]{:S(2)}) collective-permute-start(bf16[224,256]{1,0:T(8,128)(2,1)S(1)} %multiply_convert_fusion), channel_id=1, source_target_pairs={{0,24},{8,16},{16,8},{24,0},{1,25},{9,17},{17,9},{25,1},{2,26},{10... | collective-permute-start | bytes 344072 | tf_op jit(solution)/shard_map/ppermute | solution.py:76
  76.1 1.1 %collective-permute-start.16 = (bf16[224,256]{1,0:T(8,128)(2,1)S(1)}, bf16[224,256]{1,0:T(8,128)(2,1)S(1)}, u32[]{:S(2)}, u32[]{:S(2)}) collective-permute-start(bf16[224,256]{1,0:T(8,128)(2,1)S(1)} %multiply_convert_fusion), channel_id=1, source_target_pairs={{0,8},{8,0},{16,24},{24,16},{1,9},{9,1},{17,25},{25,17},{2,10},{10... | collective-permute-start | bytes 344072 | tf_op jit(solution)/shard_map/ppermute | solution.py:76
  77.2 3.5 %collective-permute-done.18 = bf16[224,256]{1,0:T(8,128)(2,1)S(1)} collective-permute-done((bf16[224,256]{1,0:T(8,128)(2,1)S(1)}, bf16[224,256]{1,0:T(8,128)(2,1)S(1)}, u32[]{:S(2)}, u32[]{:S(2)}) %collective-permute-start.18) | collective-permute-done | bytes 114720 | tf_op jit(solution)/shard_map/ppermute | solution.py:76
  80.7 3.7 %collective-permute-done.17 = bf16[224,256]{1,0:T(8,128)(2,1)S(1)} collective-permute-done((bf16[224,256]{1,0:T(8,128)(2,1)S(1)}, bf16[224,256]{1,0:T(8,128)(2,1)S(1)}, u32[]{:S(2)}, u32[]{:S(2)}) %collective-permute-start.17) | collective-permute-done | bytes 114720 | tf_op jit(solution)/shard_map/ppermute | solution.py:76
  (55 shorter events, 12.9 us)
Async XLA Ops:
  4.5 9.4 %collective-permute-start = (bf16[2,16,16,256]{3,2,1,0:T(8,128)(2,1)S(1)}, bf16[2,16,16,256]{3,2,1,0:T(8,128)(2,1)S(1)}, u32[]{:S(2)}, u32[]{:S(2)}) collective-permute-start(bf16[2,16,16,256]{3,2,1,0:T(8,128)(2,1)S(1)} %get-tuple-element.39), channel_id=1, source_target_pairs={{0,8},{8,0},{16,24},{24,16},{1,9},{9,1},{17,25},{25,17},{2,10},{10... | collective-permute-start | bytes 786440 | tf_op jit(solution)/shard_map/ppermute | solution.py:55
  7.6 6.3 %collective-permute-start.1 = (bf16[2,16,16,256]{3,2,1,0:T(8,128)(2,1)S(1)}, bf16[2,16,16,256]{3,2,1,0:T(8,128)(2,1)S(1)}, u32[]{:S(2)}, u32[]{:S(2)}) collective-permute-start(bf16[2,16,16,256]{3,2,1,0:T(8,128)(2,1)S(1)} %get-tuple-element.40), channel_id=1, source_target_pairs={{8,16},{16,8},{9,17},{17,9},{10,18},{18,10},{11,19},{19,11},{12,20... | collective-permute-start | bytes 786440 | tf_op jit(solution)/shard_map/ppermute | solution.py:55
  14.9 10.3 %copy-start.7 = (bf16[2,16,16,256]{3,2,1,0:T(8,128)(2,1)}, bf16[2,16,16,256]{3,2,1,0:T(8,128)(2,1)S(1)}, u32[]{:S(2)}) copy-start(bf16[2,16,16,256]{3,2,1,0:T(8,128)(2,1)S(1)} %get-tuple-element.41) | copy-start | bytes 786436
  15.8 2.5 %collective-permute-start.4 = (bf16[3072,128]{1,0:T(8,128)(2,1)S(1)}, bf16[3072,128]{1,0:T(8,128)(2,1)S(1)}, u32[]{:S(2)}, u32[]{:S(2)}) collective-permute-start(bf16[3072,128]{1,0:T(8,128)(2,1)S(1)} %get-tuple-element.48), channel_id=1, source_target_pairs={{0,2},{2,0},{4,6},{6,4},{1,3},{3,1},{5,7},{7,5},{8,10},{10,8},{12,... | collective-permute-start | bytes 2359304 | tf_op jit(solution)/shard_map/ppermute | solution.py:47
  15.9 2.4 %collective-permute-start.2 = (bf16[2,6,16,256]{3,2,1,0:T(8,128)(2,1)S(1)}, bf16[2,6,16,256]{3,2,1,0:T(8,128)(2,1)S(1)}, u32[]{:S(2)}, u32[]{:S(2)}) collective-permute-start(bf16[2,6,16,256]{3,2,1,0:T(8,128)(2,1)S(1)} %get-tuple-element.43.after), channel_id=1, source_target_pairs={{0,2},{2,0},{4,6},{6,4},{1,3},{3,1},{5,7},{7,5},{8,10},{10,8},{12,... | collective-permute-start | bytes 294920 | tf_op jit(solution)/shard_map/ppermute | solution.py:55
  16.4 1.9 %collective-permute-start.3 = (bf16[2,6,16,256]{3,2,1,0:T(8,128)(2,1)S(1)}, bf16[2,6,16,256]{3,2,1,0:T(8,128)(2,1)S(1)}, u32[]{:S(2)}, u32[]{:S(2)}) collective-permute-start(bf16[2,6,16,256]{3,2,1,0:T(8,128)(2,1)S(1)} %get-tuple-element.44), channel_id=1, source_target_pairs={{2,4},{4,2},{3,5},{5,3},{10,12},{12,10},{11,13},{13,11},{18,20},{2... | collective-permute-start | bytes 294920 | tf_op jit(solution)/shard_map/ppermute | solution.py:55
  19.6 4.8 %collective-permute-start.5 = (bf16[2,112,256]{2,1,0:T(8,128)(2,1)S(1)}, bf16[2,112,256]{2,1,0:T(8,128)(2,1)S(1)}, u32[]{:S(2)}, u32[]{:S(2)}) collective-permute-start(bf16[2,112,256]{2,1,0:T(8,128)(2,1)S(1)} %get-tuple-element.49), channel_id=1, source_target_pairs={{0,1},{1,0},{2,3},{3,2},{4,5},{5,4},{6,7},{7,6},{8,9},{9,8},{10,11... | collective-permute-start | bytes 344072 | tf_op jit(solution)/shard_map/ppermute | solution.py:55
  25.2 4.2 %collective-permute-start.6 = (bf16[1088,128]{1,0:T(8,128)(2,1)S(1)}, bf16[1088,128]{1,0:T(8,128)(2,1)S(1)}, u32[]{:S(2)}, u32[]{:S(2)}) collective-permute-start(bf16[1088,128]{1,0:T(8,128)(2,1)S(1)} %get-tuple-element.53), channel_id=1, source_target_pairs={{0,2},{2,0},{4,6},{6,4},{1,3},{3,1},{5,7},{7,5},{8,10},{10,8},{12,... | collective-permute-start | bytes 835592 | tf_op jit(solution)/shard_map/ppermute | solution.py:47
  32.4 17.4 %collective-permute-start.7 = (bf16[8,32,256]{2,1,0:T(8,128)(2,1)S(1)}, bf16[8,32,256]{2,1,0:T(8,128)(2,1)S(1)}, u32[]{:S(2)}, u32[]{:S(2)}) collective-permute-start(bf16[8,32,256]{2,1,0:T(8,128)(2,1)S(1)} %get-tuple-element.59), channel_id=1, source_target_pairs={{0,1},{1,0},{2,3},{3,2},{4,5},{5,4},{6,7},{7,6},{8,9},{9,8},{10,11... | collective-permute-start | bytes 393224 | tf_op jit(solution)/shard_map/ppermute | solution.py:67
  34.2 20.3 %collective-permute-start.8 = (bf16[8,32,256]{2,1,0:T(8,128)(2,1)S(1)}, bf16[8,32,256]{2,1,0:T(8,128)(2,1)S(1)}, u32[]{:S(2)}, u32[]{:S(2)}) collective-permute-start(bf16[8,32,256]{2,1,0:T(8,128)(2,1)S(1)} %get-tuple-element.60), channel_id=1, source_target_pairs={{0,4},{1,5},{2,6},{3,7},{4,0},{5,1},{6,2},{7,3},{8,12},{9,13},{10,... | collective-permute-start | bytes 393224 | tf_op jit(solution)/shard_map/ppermute | solution.py:67
  37.1 7.6 %copy-start.1 = (bf16[4,16,16,256]{3,2,1,0:T(8,128)(2,1)S(1)}, bf16[4,16,16,256]{3,2,1,0:T(8,128)(2,1)}, u32[]{:S(2)}) copy-start(bf16[4,16,16,256]{3,2,1,0:T(8,128)(2,1)} %cot_ref.1) | copy-start | bytes 1572868
  37.1 7.6 %copy-start.3 = (bf16[4,16,16,256]{3,2,1,0:T(8,128)(2,1)S(1)}, bf16[4,16,16,256]{3,2,1,0:T(8,128)(2,1)}, u32[]{:S(2)}) copy-start(bf16[4,16,16,256]{3,2,1,0:T(8,128)(2,1)} %x_ref.1) | copy-start | bytes 1572868
  37.1 7.6 %copy-start.5 = (f32[256]{0:T(256)S(1)}, f32[256]{0:T(256)}, u32[]{:S(2)}) copy-start(f32[256]{0:T(256)} %param.5) | copy-start | bytes 3076
  37.1 7.6 %copy-start.6 = (bf16[3,3,3,256,256]{4,3,2,1,0:T(8,128)(2,1)S(1)}, bf16[3,3,3,256,256]{4,3,2,1,0:T(8,128)(2,1)}, u32[]{:S(2)}) copy-start(bf16[3,3,3,256,256]{4,3,2,1,0:T(8,128)(2,1)} %weight.3) | copy-start | bytes 10616836
  37.1 17.3 %collective-permute-start.9 = (bf16[8,32,256]{2,1,0:T(8,128)(2,1)S(1)}, bf16[8,32,256]{2,1,0:T(8,128)(2,1)S(1)}, u32[]{:S(2)}, u32[]{:S(2)}) collective-permute-start(bf16[8,32,256]{2,1,0:T(8,128)(2,1)S(1)} %get-tuple-element.61), channel_id=1, source_target_pairs={{0,5},{1,4},{2,7},{3,6},{4,1},{5,0},{6,3},{7,2},{8,13},{9,12},{10,... | collective-permute-start | bytes 393224 | tf_op jit(solution)/shard_map/ppermute | solution.py:67
  41.1 13.3 %collective-permute-start.10 = (bf16[19,32,256]{2,1,0:T(8,128)(2,1)S(1)}, bf16[19,32,256]{2,1,0:T(8,128)(2,1)S(1)}, u32[]{:S(2)}, u32[]{:S(2)}) collective-permute-start(bf16[19,32,256]{2,1,0:T(8,128)(2,1)S(1)} %get-tuple-element.62), channel_id=1, source_target_pairs={{0,1},{1,0},{2,3},{3,2},{4,5},{5,4},{6,7},{7,6},{8,9},{9,8},{10,11... | collective-permute-start | bytes 933896 | tf_op jit(solution)/shard_map/ppermute | solution.py:67
  42.7 11.8 %collective-permute-start.11 = (bf16[19,32,256]{2,1,0:T(8,128)(2,1)S(1)}, bf16[19,32,256]{2,1,0:T(8,128)(2,1)S(1)}, u32[]{:S(2)}, u32[]{:S(2)}) collective-permute-start(bf16[19,32,256]{2,1,0:T(8,128)(2,1)S(1)} %get-tuple-element.63), channel_id=1, source_target_pairs={{0,4},{1,5},{2,6},{3,7},{4,0},{5,1},{6,2},{7,3},{8,12},{9,13},{10,... | collective-permute-start | bytes 933896 | tf_op jit(solution)/shard_map/ppermute | solution.py:67
  49.8 8.9 %collective-permute-start.12 = (bf16[19,32,256]{2,1,0:T(8,128)(2,1)S(1)}, bf16[19,32,256]{2,1,0:T(8,128)(2,1)S(1)}, u32[]{:S(2)}, u32[]{:S(2)}) collective-permute-start(bf16[19,32,256]{2,1,0:T(8,128)(2,1)S(1)} %get-tuple-element.64), channel_id=1, source_target_pairs={{0,5},{1,4},{2,7},{3,6},{4,1},{5,0},{6,3},{7,2},{8,13},{9,12},{10,... | collective-permute-start | bytes 933896 | tf_op jit(solution)/shard_map/ppermute | solution.py:67
  59.6 7.2 %collective-permute-start.15 = (bf16[224,256]{1,0:T(8,128)(2,1)S(1)}, bf16[224,256]{1,0:T(8,128)(2,1)S(1)}, u32[]{:S(2)}, u32[]{:S(2)}) collective-permute-start(bf16[224,256]{1,0:T(8,128)(2,1)S(1)} %get-tuple-element.70), channel_id=1, source_target_pairs={{0,24},{8,16},{16,8},{24,0},{1,25},{9,17},{17,9},{25,1},{2,26},{10... | collective-permute-start | bytes 344072 | tf_op jit(solution)/shard_map/ppermute | solution.py:76
  63.2 9.4 %collective-permute-start.14 = (bf16[224,256]{1,0:T(8,128)(2,1)S(1)}, bf16[224,256]{1,0:T(8,128)(2,1)S(1)}, u32[]{:S(2)}, u32[]{:S(2)}) collective-permute-start(bf16[224,256]{1,0:T(8,128)(2,1)S(1)} %get-tuple-element.69), channel_id=1, source_target_pairs={{0,16},{8,24},{16,0},{24,8},{1,17},{9,25},{17,1},{25,9},{2,18},{10... | collective-permute-start | bytes 344072 | tf_op jit(solution)/shard_map/ppermute | solution.py:76
  65.7 7.0 %collective-permute-start.13 = (bf16[224,256]{1,0:T(8,128)(2,1)S(1)}, bf16[224,256]{1,0:T(8,128)(2,1)S(1)}, u32[]{:S(2)}, u32[]{:S(2)}) collective-permute-start(bf16[224,256]{1,0:T(8,128)(2,1)S(1)} %get-tuple-element.68), channel_id=1, source_target_pairs={{0,8},{8,0},{16,24},{24,16},{1,9},{9,1},{17,25},{25,17},{2,10},{10... | collective-permute-start | bytes 344072 | tf_op jit(solution)/shard_map/ppermute | solution.py:76
  72.7 7.9 %collective-permute-start.18 = (bf16[224,256]{1,0:T(8,128)(2,1)S(1)}, bf16[224,256]{1,0:T(8,128)(2,1)S(1)}, u32[]{:S(2)}, u32[]{:S(2)}) collective-permute-start(bf16[224,256]{1,0:T(8,128)(2,1)S(1)} %multiply_convert_fusion), channel_id=1, source_target_pairs={{0,24},{8,16},{16,8},{24,0},{1,25},{9,17},{17,9},{25,1},{2,26},{10... | collective-permute-start | bytes 344072 | tf_op jit(solution)/shard_map/ppermute | solution.py:76
  76.1 8.3 %collective-permute-start.17 = (bf16[224,256]{1,0:T(8,128)(2,1)S(1)}, bf16[224,256]{1,0:T(8,128)(2,1)S(1)}, u32[]{:S(2)}, u32[]{:S(2)}) collective-permute-start(bf16[224,256]{1,0:T(8,128)(2,1)S(1)} %multiply_convert_fusion), channel_id=1, source_target_pairs={{0,16},{8,24},{16,0},{24,8},{1,17},{9,25},{17,1},{25,9},{2,18},{10... | collective-permute-start | bytes 344072 | tf_op jit(solution)/shard_map/ppermute | solution.py:76
  76.1 8.3 %collective-permute-start.16 = (bf16[224,256]{1,0:T(8,128)(2,1)S(1)}, bf16[224,256]{1,0:T(8,128)(2,1)S(1)}, u32[]{:S(2)}, u32[]{:S(2)}) collective-permute-start(bf16[224,256]{1,0:T(8,128)(2,1)S(1)} %multiply_convert_fusion), channel_id=1, source_target_pairs={{0,8},{8,0},{16,24},{24,16},{1,9},{9,1},{17,25},{25,17},{2,10},{10... | collective-permute-start | bytes 344072 | tf_op jit(solution)/shard_map/ppermute | solution.py:76
  (6 other events, 12.6 us)

commit v6 on v5

--- a/solution.py
+++ b/solution.py
@@ -8,7 +8,7 @@
 from jax.sharding import PartitionSpec as P
 
 EPSILON = 1e-06
-FIRST_TAPS = 8
+FIRST_TAPS = 11
 AXES = ("ta", "ha", "wa")
 BF16 = jnp.bfloat16
 F32 = jnp.float32
@@ -121,21 +121,23 @@
 
 
 def columns_kernel(count, slot, where_ref, lefts, rights, *refs):
-    swapped, (for_even, for_odd) = refs[:count], refs[-2:]
+    swapped, targets = refs[:count], refs[count + 1 :]
     _, frames, height, channels = lefts.shape
     even_h, even_w = where_ref[0] == 0, where_ref[1] == 0
     width = swapped[0].shape[2]
     above, below = both_sides(even_h, swapped, swapped[0].shape)
     nothing = jnp.zeros((2, slot - frames, channels), F32)
-    sides = []
-    for source, at in ((lefts, 0), (rights, width - 1)):
+    shape = (2, frames * height, channels)
+    first, last = lefts[...].reshape(shape), rights[...].reshape(shape)
+    for target, (one, other) in zip(targets, ((last, first), (first, last))):
+        target[:, : frames * height] = jnp.where(even_w, one, other)
+    corners = []
+    for at in (0, width - 1):
         over = above.astype(F32)[:, :, at, :]
         under = below.astype(F32)[:, :, at, :]
-        columns = source[...].astype(F32).reshape(2, frames * height, channels)
-        parts = [columns, over, nothing, under, nothing]
-        sides.append(jnp.concatenate(parts, axis=1).astype(BF16))
-    for_even[...] = jnp.where(even_w, sides[1], sides[0])
-    for_odd[...] = jnp.where(even_w, sides[0], sides[1])
+        corners.append(jnp.concatenate([over, nothing, under, nothing], axis=1))
+    for target, (one, other) in zip(targets, (corners[::-1], corners)):
+        target[:, frames * height :] = jnp.where(even_w, one, other).astype(BF16)
 
 
 def halves(core, values, chips):
@@ -421,17 +423,16 @@
     other = swap_core(send)
     rows = [swap_pairs(for_even, "ha", 0), swap_pairs(for_odd, "ha", 1)]
     rows = [array for array in rows if array is not None]
-    for_even, for_odd = call(
+    by_swap = call(
         functools.partial(columns_kernel, len(rows), slot),
-        (shape_of(2, (frames + 2) * height + 2 * slot, channels),) * 2,
+        (shape_of(2, (frames + 2) * height + 2 * slot, channels),) * min(2, cols_of - 1),
         0,
         size // 2,
         scalars=1,
         arrays=2 + len(rows),
         left=1,
     )(where, lefts, rights, *rows, other)
-    columns = [swap_pairs(for_even, "wa", 0), swap_pairs(for_odd, "wa", 1)]
-    columns = [array for array in columns if array is not None]
+    columns = [swap_pairs(array, "wa", odd) for odd, array in enumerate(by_swap)]
     later = later.reshape(2, inner, channels)
     cot_edges, act_edges, mine_more, send_more = call(
         functools.partial(bundle_kernel, chips, slot, (len(rows), len(columns))),

time: 85.9 us -> 85 us (0.990)
    ppermute x6, waiting for transfers between devices: 4.2 us -> 3.14 us  [to_chip(): return lax.ppermute(array, ('ha', 'wa'), pairs)]
  transfers between devices with their start and end apart: 19 -> 19, of which waited for: 9 -> 9; matrix products, arithmetic and copies ran while one was open for 0% -> 0% of each run, Pallas kernels for 16% -> 15%
where the time goes in v6:
time: 85 us; the launch traced here: 84.8 us
  starting transfers between devices  28.8 us (34%)
  waiting for transfers between devices  28.4 us (33%)
  Pallas kernels  20.8 us (24%)
  local copies, waits for them, and re-layouts  4.51 us (5%)
  other arithmetic  1.41 us (2%)
    ppermute x6, waiting for transfers between devices, to_partner(): lax.ppermute(array, axis, [(i, partner(i, by, length)) for i in range(len...  14.2 us
    ppermute x6, starting transfers between devices, to_partner(): lax.ppermute(array, axis, [(i, partner(i, by, length)) for i in range(len...  10.8 us
    ppermute x5, waiting for transfers between devices, swap_pairs(): return lax.ppermute(array, axis, pairs) if pairs else None  10 us
    ppermute x6, starting transfers between devices, to_chip(): return lax.ppermute(array, ('ha', 'wa'), pairs)  8.35 us
    ppermute x5, starting transfers between devices, swap_pairs(): return lax.ppermute(array, axis, pairs) if pairs else None  6.66 us
    pallas_call x2, Pallas kernels, body(): call(functools.partial(taps_kernel, height, width, taps), tuple((shape_of...  5.87 us
    pallas_call x1, Pallas kernels, body(): call(functools.partial(backward_kernel, height, width), flat, 27 * produc...  5.08 us
    pallas_call x1, Pallas kernels, body(): call(functools.partial(forward_kernel, height, width), flat, 27 * product...  4.67 us
  transfers between devices with their start and end apart: 19, of which 9 were waited for; matrix products, arithmetic and copies ran while one was open for 0% of the time, Pallas kernels for 15%

profile of v6, /device:TPU:0, one launch (start us, length us, event | category | flops | bytes accessed | tf_op | source)
XLA Modules:
  0.0 84.8 jit_solution(16362456657260685445)
XLA Ops:
  0.7 1.0 %copy-done = bf16[4,16,16,256]{3,2,1,0:T(8,128)(2,1)S(1)} copy-done((bf16[4,16,16,256]{3,2,1,0:T(8,128)(2,1)S(1)}, bf16[4,16,16,256]{3,2,1,0:T(8,128)(2,1)}, u32[]{:S(2)}) %copy-start) | copy-done | bytes 524312
  4.5 3.1 %collective-permute-start = (bf16[2,16,16,256]{3,2,1,0:T(8,128)(2,1)S(1)}, bf16[2,16,16,256]{3,2,1,0:T(8,128)(2,1)S(1)}, u32[]{:S(2)}, u32[]{:S(2)}) collective-permute-start(bf16[2,16,16,256]{3,2,1,0:T(8,128)(2,1)S(1)} %get-tuple-element.38), channel_id=1, source_target_pairs={{0,8},{8,0},{16,24},{24,16},{1,9},{9,1},{17,25},{25,17},{2,10},{10... | collective-permute-start | bytes 786440 | tf_op jit(solution)/shard_map/ppermute | solution.py:55
  8.3 5.6 %collective-permute-done.refs_0_ = bf16[2,16,16,256]{3,2,1,0:T(8,128)(2,1)S(1)} collective-permute-done((bf16[2,16,16,256]{3,2,1,0:T(8,128)(2,1)S(1)}, bf16[2,16,16,256]{3,2,1,0:T(8,128)(2,1)S(1)}, u32[]{:S(2)}, u32[]{:S(2)}) %collective-permute-start) | collective-permute-done | bytes 262176 | tf_op jit(solution)/shard_map/ppermute | solution.py:55
  13.9 1.0 %shard_map.68 = (bf16[2,16,16,256]{3,2,1,0:T(8,128)(2,1)S(1)}, bf16[2,16,16,256]{3,2,1,0:T(8,128)(2,1)S(1)}, bf16[2,6,16,256]{3,2,1,0:T(8,128)(2,1)S(1)}, bf16[2...) custom-call(s32[3]{0:T(128)S(1)} %pad_add_fusion.where_ref, ...), custom_call_target="tpu_custom_call" | custom-call | bytes 1048576 | tf_op jit(solution)/shard_map/pallas_call | solution.py:394
  17.7 1.3 %collective-permute-done.2.refs_0_ = bf16[2,6,16,256]{3,2,1,0:T(8,128)(2,1)S(1)} collective-permute-done((bf16[2,6,16,256]{3,2,1,0:T(8,128)(2,1)S(1)}, bf16[2,6,16,256]{3,2,1,0:T(8,128)(2,1)S(1)}, u32[]{:S(2)}, u32[]{:S(2)}) %collective-permute-start.2) | collective-permute-done | bytes 98336 | tf_op jit(solution)/shard_map/ppermute | solution.py:55
  19.5 1.7 %collective-permute-start.5 = (bf16[2,112,256]{2,1,0:T(8,128)(2,1)S(1)}, bf16[2,112,256]{2,1,0:T(8,128)(2,1)S(1)}, u32[]{:S(2)}, u32[]{:S(2)}) collective-permute-start(bf16[2,112,256]{2,1,0:T(8,128)(2,1)S(1)} %shard_map.70), channel_id=1, source_target_pairs={{0,1},{1,0},{2,3},{3,2},{4,5},{5,4},{6,7},{7,6},{8,9},{9,8},{10,11... | collective-permute-start | bytes 344072 | tf_op jit(solution)/shard_map/ppermute | solution.py:55
  21.3 3.1 %collective-permute-done.5.refs_2_ = bf16[2,112,256]{2,1,0:T(8,128)(2,1)S(1)} collective-permute-done((bf16[2,112,256]{2,1,0:T(8,128)(2,1)S(1)}, bf16[2,112,256]{2,1,0:T(8,128)(2,1)S(1)}, u32[]{:S(2)}, u32[]{:S(2)}) %collective-permute-start.5) | collective-permute-done | bytes 114720 | tf_op jit(solution)/shard_map/ppermute | solution.py:55
  25.2 3.0 %collective-permute-start.6 = (bf16[1088,128]{1,0:T(8,128)(2,1)S(1)}, bf16[1088,128]{1,0:T(8,128)(2,1)S(1)}, u32[]{:S(2)}, u32[]{:S(2)}) collective-permute-start(bf16[1088,128]{1,0:T(8,128)(2,1)S(1)} %get-tuple-element.51), channel_id=1, source_target_pairs={{0,2},{2,0},{4,6},{6,4},{1,3},{3,1},{5,7},{7,5},{8,10},{10,8},{12,... | collective-permute-start | bytes 835592 | tf_op jit(solution)/shard_map/ppermute | solution.py:47
  30.3 2.6 %shard_map.75 = (f32[11,32,256]{2,1,0:T(8,128)S(1)}, bf16[11,32,256]{2,1,0:T(8,128)(2,1)S(1)}, bf16[11,32,256]{2,1,0:T(8,128)(2,1)S(1)}, bf16[11,32,256]{2,1,0:T(8,128)(2,1)S(1)}) custom-call(s32[4]{0:T(128)S(1)} %pad_add_fusion.1.refs_0_, bf16[256,1024]{1,0:T(8,128)(2,1)S(1)} %get-tuple-element.46.act_t.refs_1_, bf16[4,256,128]{2,1,0:T(8,128)(2,1)S(1)} %copy-done.10, ...), custom_call_target="tpu_custom_call" | custom-call | flops 1476395008 | bytes 2097152 | tf_op jit(solution)/shard_map/pallas_call | solution.py:459
  33.0 1.7 %collective-permute-start.7 = (bf16[11,32,256]{2,1,0:T(8,128)(2,1)S(1)}, bf16[11,32,256]{2,1,0:T(8,128)(2,1)S(1)}, u32[]{:S(2)}, u32[]{:S(2)}) collective-permute-start(bf16[11,32,256]{2,1,0:T(8,128)(2,1)S(1)} %get-tuple-element.57), channel_id=1, source_target_pairs={{0,1},{1,0},{2,3},{3,2},{4,5},{5,4},{6,7},{7,6},{8,9},{9,8},{10,11... | collective-permute-start | bytes 540680 | tf_op jit(solution)/shard_map/ppermute | solution.py:67
  34.7 3.0 %collective-permute-start.8 = (bf16[11,32,256]{2,1,0:T(8,128)(2,1)S(1)}, bf16[11,32,256]{2,1,0:T(8,128)(2,1)S(1)}, u32[]{:S(2)}, u32[]{:S(2)}) collective-permute-start(bf16[11,32,256]{2,1,0:T(8,128)(2,1)S(1)} %get-tuple-element.58), channel_id=1, source_target_pairs={{0,4},{1,5},{2,6},{3,7},{4,0},{5,1},{6,2},{7,3},{8,12},{9,13},{10,... | collective-permute-start | bytes 540680 | tf_op jit(solution)/shard_map/ppermute | solution.py:67
  37.8 3.2 %shard_map.72 = (f32[16,32,256]{2,1,0:T(8,128)S(1)}, bf16[16,32,256]{2,1,0:T(8,128)(2,1)S(1)}, bf16[16,32,256]{2,1,0:T(8,128)(2,1)S(1)}, bf16[16,32,256]{2,1,0:T(8,128)(2,1)S(1)}) custom-call(s32[4]{0:T(128)S(1)} %pad_add_fusion.1.refs_0_, bf16[256,1024]{1,0:T(8,128)(2,1)S(1)} %get-tuple-element.46.act_t.refs_1_, bf16[4,256,128]{2,1,0:T(8,128)(2,1)S(1)} %copy-done.10, ...), custom_call_target="tpu_custom_call" | custom-call | flops 2147483648 | bytes 2097152 | tf_op jit(solution)/shard_map/pallas_call | solution.py:459
  41.0 1.5 %collective-permute-start.10 = (bf16[16,32,256]{2,1,0:T(8,128)(2,1)S(1)}, bf16[16,32,256]{2,1,0:T(8,128)(2,1)S(1)}, u32[]{:S(2)}, u32[]{:S(2)}) collective-permute-start(bf16[16,32,256]{2,1,0:T(8,128)(2,1)S(1)} %get-tuple-element.60), channel_id=1, source_target_pairs={{0,1},{1,0},{2,3},{3,2},{4,5},{5,4},{6,7},{7,6},{8,9},{9,8},{10,11... | collective-permute-start | bytes 786440 | tf_op jit(solution)/shard_map/ppermute | solution.py:67
  42.6 2.0 %collective-permute-start.11 = (bf16[16,32,256]{2,1,0:T(8,128)(2,1)S(1)}, bf16[16,32,256]{2,1,0:T(8,128)(2,1)S(1)}, u32[]{:S(2)}, u32[]{:S(2)}) collective-permute-start(bf16[16,32,256]{2,1,0:T(8,128)(2,1)S(1)} %get-tuple-element.61), channel_id=1, source_target_pairs={{0,4},{1,5},{2,6},{3,7},{4,0},{5,1},{6,2},{7,3},{8,12},{9,13},{10,... | collective-permute-start | bytes 786440 | tf_op jit(solution)/shard_map/ppermute | solution.py:67
  44.6 5.1 %shard_map.74 = (bf16[1024,256]{1,0:T(8,128)(2,1)}, f32[8,128]{1,0:T(8,128)S(1)}) custom-call(bf16[1024,256]{1,0:T(8,128)(2,1)S(1)} %bitcast.32, f32[1,256]{1,0:T(1,128)S(1)} %bitcast.38, bf16[4,256,256]{2,1,0:T(8,128)(2,1)S(1)} %bitcast.31, bf16[2,256,256]{2,1,0:T(8,128)(2,1)S(1)} %bitcast.36, bf16[6,96,256]{2,1,0:T(8,128)(2,1)S(1)} %get-tuple-element.54.edges, ...), custom_call_target="tpu_custom_call" | custom-call | flops 3623878656 | bytes 5636096 | tf_op jit(solution)/shard_map/pallas_call | solution.py:481
  49.7 4.7 %shard_map.73 = (bf16[1024,256]{1,0:T(8,128)(2,1)}, f32[8,128]{1,0:T(8,128)S(1)}) custom-call(bf16[1024,256]{1,0:T(8,128)(2,1)S(1)} %bitcast.33, bf16[2,256,256]{2,1,0:T(8,128)(2,1)S(1)} %bitcast.39, bf16[4,256,256]{2,1,0:T(8,128)(2,1)S(1)} %bitcast.34, bf16[6,96,256]{2,1,0:T(8,128)(2,1)S(1)} %get-tuple-element.48.edges, ...), custom_call_target="tpu_custom_call" | custom-call | flops 3623878656 | bytes 5636096 | tf_op jit(solution)/shard_map/pallas_call | solution.py:491
  54.4 3.1 %collective-permute-done.12.refs_7_ = bf16[16,32,256]{2,1,0:T(8,128)(2,1)S(1)} collective-permute-done((bf16[16,32,256]{2,1,0:T(8,128)(2,1)S(1)}, bf16[16,32,256]{2,1,0:T(8,128)(2,1)S(1)}, u32[]{:S(2)}, u32[]{:S(2)}) %collective-permute-start.12) | collective-permute-done | bytes 262176 | tf_op jit(solution)/shard_map/ppermute | solution.py:67
  58.4 3.7 %collective-permute-start.15 = (bf16[224,256]{1,0:T(8,128)(2,1)S(1)}, bf16[224,256]{1,0:T(8,128)(2,1)S(1)}, u32[]{:S(2)}, u32[]{:S(2)}) collective-permute-start(bf16[224,256]{1,0:T(8,128)(2,1)S(1)} %get-tuple-element.68), channel_id=1, source_target_pairs={{0,24},{8,16},{16,8},{24,0},{1,25},{9,17},{17,9},{25,1},{2,26},{10... | collective-permute-start | bytes 344072 | tf_op jit(solution)/shard_map/ppermute | solution.py:76
  62.1 2.4 %collective-permute-start.14 = (bf16[224,256]{1,0:T(8,128)(2,1)S(1)}, bf16[224,256]{1,0:T(8,128)(2,1)S(1)}, u32[]{:S(2)}, u32[]{:S(2)}) collective-permute-start(bf16[224,256]{1,0:T(8,128)(2,1)S(1)} %get-tuple-element.67), channel_id=1, source_target_pairs={{0,16},{8,24},{16,0},{24,8},{1,17},{9,25},{17,1},{25,9},{2,18},{10... | collective-permute-start | bytes 344072 | tf_op jit(solution)/shard_map/ppermute | solution.py:76
  65.6 6.2 %collective-permute-done.14 = bf16[224,256]{1,0:T(8,128)(2,1)S(1)} collective-permute-done((bf16[224,256]{1,0:T(8,128)(2,1)S(1)}, bf16[224,256]{1,0:T(8,128)(2,1)S(1)}, u32[]{:S(2)}, u32[]{:S(2)}) %collective-permute-start.14) | collective-permute-done | bytes 114720 | tf_op jit(solution)/shard_map/ppermute | solution.py:76
  71.9 3.1 %collective-permute-start.18 = (bf16[224,256]{1,0:T(8,128)(2,1)S(1)}, bf16[224,256]{1,0:T(8,128)(2,1)S(1)}, u32[]{:S(2)}, u32[]{:S(2)}) collective-permute-start(bf16[224,256]{1,0:T(8,128)(2,1)S(1)} %multiply_convert_fusion), channel_id=1, source_target_pairs={{0,24},{8,16},{16,8},{24,0},{1,25},{9,17},{17,9},{25,1},{2,26},{10... | collective-permute-start | bytes 344072 | tf_op jit(solution)/shard_map/ppermute | solution.py:76
  75.0 1.3 %collective-permute-start.16 = (bf16[224,256]{1,0:T(8,128)(2,1)S(1)}, bf16[224,256]{1,0:T(8,128)(2,1)S(1)}, u32[]{:S(2)}, u32[]{:S(2)}) collective-permute-start(bf16[224,256]{1,0:T(8,128)(2,1)S(1)} %multiply_convert_fusion), channel_id=1, source_target_pairs={{0,8},{8,0},{16,24},{24,16},{1,9},{9,1},{17,25},{25,17},{2,10},{10... | collective-permute-start | bytes 344072 | tf_op jit(solution)/shard_map/ppermute | solution.py:76
  76.4 3.1 %collective-permute-done.18 = bf16[224,256]{1,0:T(8,128)(2,1)S(1)} collective-permute-done((bf16[224,256]{1,0:T(8,128)(2,1)S(1)}, bf16[224,256]{1,0:T(8,128)(2,1)S(1)}, u32[]{:S(2)}, u32[]{:S(2)}) %collective-permute-start.18) | collective-permute-done | bytes 114720 | tf_op jit(solution)/shard_map/ppermute | solution.py:76
  79.4 4.1 %collective-permute-done.17 = bf16[224,256]{1,0:T(8,128)(2,1)S(1)} collective-permute-done((bf16[224,256]{1,0:T(8,128)(2,1)S(1)}, bf16[224,256]{1,0:T(8,128)(2,1)S(1)}, u32[]{:S(2)}, u32[]{:S(2)}) %collective-permute-start.17) | collective-permute-done | bytes 114720 | tf_op jit(solution)/shard_map/ppermute | solution.py:76
  (55 shorter events, 13.1 us)
Async XLA Ops:
  4.5 9.4 %collective-permute-start = (bf16[2,16,16,256]{3,2,1,0:T(8,128)(2,1)S(1)}, bf16[2,16,16,256]{3,2,1,0:T(8,128)(2,1)S(1)}, u32[]{:S(2)}, u32[]{:S(2)}) collective-permute-start(bf16[2,16,16,256]{3,2,1,0:T(8,128)(2,1)S(1)} %get-tuple-element.38), channel_id=1, source_target_pairs={{0,8},{8,0},{16,24},{24,16},{1,9},{9,1},{17,25},{25,17},{2,10},{10... | collective-permute-start | bytes 786440 | tf_op jit(solution)/shard_map/ppermute | solution.py:55
  7.6 6.3 %collective-permute-start.1 = (bf16[2,16,16,256]{3,2,1,0:T(8,128)(2,1)S(1)}, bf16[2,16,16,256]{3,2,1,0:T(8,128)(2,1)S(1)}, u32[]{:S(2)}, u32[]{:S(2)}) collective-permute-start(bf16[2,16,16,256]{3,2,1,0:T(8,128)(2,1)S(1)} %get-tuple-element.39), channel_id=1, source_target_pairs={{8,16},{16,8},{9,17},{17,9},{10,18},{18,10},{11,19},{19,11},{12,20... | collective-permute-start | bytes 786440 | tf_op jit(solution)/shard_map/ppermute | solution.py:55
  14.9 10.3 %copy-start.7 = (bf16[2,16,16,256]{3,2,1,0:T(8,128)(2,1)}, bf16[2,16,16,256]{3,2,1,0:T(8,128)(2,1)S(1)}, u32[]{:S(2)}) copy-start(bf16[2,16,16,256]{3,2,1,0:T(8,128)(2,1)S(1)} %get-tuple-element.40) | copy-start | bytes 786436
  16.5 2.4 %collective-permute-start.4 = (bf16[3072,128]{1,0:T(8,128)(2,1)S(1)}, bf16[3072,128]{1,0:T(8,128)(2,1)S(1)}, u32[]{:S(2)}, u32[]{:S(2)}) collective-permute-start(bf16[3072,128]{1,0:T(8,128)(2,1)S(1)} %get-tuple-element.47), channel_id=1, source_target_pairs={{0,2},{2,0},{4,6},{6,4},{1,3},{3,1},{5,7},{7,5},{8,10},{10,8},{12,... | collective-permute-start | bytes 2359304 | tf_op jit(solution)/shard_map/ppermute | solution.py:47
  16.5 2.4 %collective-permute-start.2 = (bf16[2,6,16,256]{3,2,1,0:T(8,128)(2,1)S(1)}, bf16[2,6,16,256]{3,2,1,0:T(8,128)(2,1)S(1)}, u32[]{:S(2)}, u32[]{:S(2)}) collective-permute-start(bf16[2,6,16,256]{3,2,1,0:T(8,128)(2,1)S(1)} %get-tuple-element.42.after), channel_id=1, source_target_pairs={{0,2},{2,0},{4,6},{6,4},{1,3},{3,1},{5,7},{7,5},{8,10},{10,8},{12,... | collective-permute-start | bytes 294920 | tf_op jit(solution)/shard_map/ppermute | solution.py:55
  17.0 1.9 %collective-permute-start.3 = (bf16[2,6,16,256]{3,2,1,0:T(8,128)(2,1)S(1)}, bf16[2,6,16,256]{3,2,1,0:T(8,128)(2,1)S(1)}, u32[]{:S(2)}, u32[]{:S(2)}) collective-permute-start(bf16[2,6,16,256]{3,2,1,0:T(8,128)(2,1)S(1)} %get-tuple-element.43), channel_id=1, source_target_pairs={{2,4},{4,2},{3,5},{5,3},{10,12},{12,10},{11,13},{13,11},{18,20},{2... | collective-permute-start | bytes 294920 | tf_op jit(solution)/shard_map/ppermute | solution.py:55
  19.5 4.9 %collective-permute-start.5 = (bf16[2,112,256]{2,1,0:T(8,128)(2,1)S(1)}, bf16[2,112,256]{2,1,0:T(8,128)(2,1)S(1)}, u32[]{:S(2)}, u32[]{:S(2)}) collective-permute-start(bf16[2,112,256]{2,1,0:T(8,128)(2,1)S(1)} %shard_map.70), channel_id=1, source_target_pairs={{0,1},{1,0},{2,3},{3,2},{4,5},{5,4},{6,7},{7,6},{8,9},{9,8},{10,11... | collective-permute-start | bytes 344072 | tf_op jit(solution)/shard_map/ppermute | solution.py:55
  25.2 4.1 %collective-permute-start.6 = (bf16[1088,128]{1,0:T(8,128)(2,1)S(1)}, bf16[1088,128]{1,0:T(8,128)(2,1)S(1)}, u32[]{:S(2)}, u32[]{:S(2)}) collective-permute-start(bf16[1088,128]{1,0:T(8,128)(2,1)S(1)} %get-tuple-element.51), channel_id=1, source_target_pairs={{0,2},{2,0},{4,6},{6,4},{1,3},{3,1},{5,7},{7,5},{8,10},{10,8},{12,... | collective-permute-start | bytes 835592 | tf_op jit(solution)/shard_map/ppermute | solution.py:47
  33.0 16.7 %collective-permute-start.7 = (bf16[11,32,256]{2,1,0:T(8,128)(2,1)S(1)}, bf16[11,32,256]{2,1,0:T(8,128)(2,1)S(1)}, u32[]{:S(2)}, u32[]{:S(2)}) collective-permute-start(bf16[11,32,256]{2,1,0:T(8,128)(2,1)S(1)} %get-tuple-element.57), channel_id=1, source_target_pairs={{0,1},{1,0},{2,3},{3,2},{4,5},{5,4},{6,7},{7,6},{8,9},{9,8},{10,11... | collective-permute-start | bytes 540680 | tf_op jit(solution)/shard_map/ppermute | solution.py:67
  34.7 19.7 %collective-permute-start.8 = (bf16[11,32,256]{2,1,0:T(8,128)(2,1)S(1)}, bf16[11,32,256]{2,1,0:T(8,128)(2,1)S(1)}, u32[]{:S(2)}, u32[]{:S(2)}) collective-permute-start(bf16[11,32,256]{2,1,0:T(8,128)(2,1)S(1)} %get-tuple-element.58), channel_id=1, source_target_pairs={{0,4},{1,5},{2,6},{3,7},{4,0},{5,1},{6,2},{7,3},{8,12},{9,13},{10,... | collective-permute-start | bytes 540680 | tf_op jit(solution)/shard_map/ppermute | solution.py:67
  37.7 6.9 %copy-start.1 = (bf16[4,16,16,256]{3,2,1,0:T(8,128)(2,1)S(1)}, bf16[4,16,16,256]{3,2,1,0:T(8,128)(2,1)}, u32[]{:S(2)}) copy-start(bf16[4,16,16,256]{3,2,1,0:T(8,128)(2,1)} %cot_ref.1) | copy-start | bytes 1572868
  37.7 6.9 %copy-start.3 = (bf16[4,16,16,256]{3,2,1,0:T(8,128)(2,1)S(1)}, bf16[4,16,16,256]{3,2,1,0:T(8,128)(2,1)}, u32[]{:S(2)}) copy-start(bf16[4,16,16,256]{3,2,1,0:T(8,128)(2,1)} %x_ref.1) | copy-start | bytes 1572868
  37.7 6.9 %copy-start.5 = (f32[256]{0:T(256)S(1)}, f32[256]{0:T(256)}, u32[]{:S(2)}) copy-start(f32[256]{0:T(256)} %param.5) | copy-start | bytes 3076
  37.7 6.9 %copy-start.6 = (bf16[3,3,3,256,256]{4,3,2,1,0:T(8,128)(2,1)S(1)}, bf16[3,3,3,256,256]{4,3,2,1,0:T(8,128)(2,1)}, u32[]{:S(2)}) copy-start(bf16[3,3,3,256,256]{4,3,2,1,0:T(8,128)(2,1)} %weight.3) | copy-start | bytes 10616836
  37.7 16.7 %collective-permute-start.9 = (bf16[11,32,256]{2,1,0:T(8,128)(2,1)S(1)}, bf16[11,32,256]{2,1,0:T(8,128)(2,1)S(1)}, u32[]{:S(2)}, u32[]{:S(2)}) collective-permute-start(bf16[11,32,256]{2,1,0:T(8,128)(2,1)S(1)} %get-tuple-element.59), channel_id=1, source_target_pairs={{0,5},{1,4},{2,7},{3,6},{4,1},{5,0},{6,3},{7,2},{8,13},{9,12},{10,... | collective-permute-start | bytes 540680 | tf_op jit(solution)/shard_map/ppermute | solution.py:67
  41.0 13.3 %collective-permute-start.10 = (bf16[16,32,256]{2,1,0:T(8,128)(2,1)S(1)}, bf16[16,32,256]{2,1,0:T(8,128)(2,1)S(1)}, u32[]{:S(2)}, u32[]{:S(2)}) collective-permute-start(bf16[16,32,256]{2,1,0:T(8,128)(2,1)S(1)} %get-tuple-element.60), channel_id=1, source_target_pairs={{0,1},{1,0},{2,3},{3,2},{4,5},{5,4},{6,7},{7,6},{8,9},{9,8},{10,11... | collective-permute-start | bytes 786440 | tf_op jit(solution)/shard_map/ppermute | solution.py:67
  42.6 11.8 %collective-permute-start.11 = (bf16[16,32,256]{2,1,0:T(8,128)(2,1)S(1)}, bf16[16,32,256]{2,1,0:T(8,128)(2,1)S(1)}, u32[]{:S(2)}, u32[]{:S(2)}) collective-permute-start(bf16[16,32,256]{2,1,0:T(8,128)(2,1)S(1)} %get-tuple-element.61), channel_id=1, source_target_pairs={{0,4},{1,5},{2,6},{3,7},{4,0},{5,1},{6,2},{7,3},{8,12},{9,13},{10,... | collective-permute-start | bytes 786440 | tf_op jit(solution)/shard_map/ppermute | solution.py:67
  49.7 7.8 %collective-permute-start.12 = (bf16[16,32,256]{2,1,0:T(8,128)(2,1)S(1)}, bf16[16,32,256]{2,1,0:T(8,128)(2,1)S(1)}, u32[]{:S(2)}, u32[]{:S(2)}) collective-permute-start(bf16[16,32,256]{2,1,0:T(8,128)(2,1)S(1)} %get-tuple-element.62), channel_id=1, source_target_pairs={{0,5},{1,4},{2,7},{3,6},{4,1},{5,0},{6,3},{7,2},{8,13},{9,12},{10,... | collective-permute-start | bytes 786440 | tf_op jit(solution)/shard_map/ppermute | solution.py:67
  58.4 7.2 %collective-permute-start.15 = (bf16[224,256]{1,0:T(8,128)(2,1)S(1)}, bf16[224,256]{1,0:T(8,128)(2,1)S(1)}, u32[]{:S(2)}, u32[]{:S(2)}) collective-permute-start(bf16[224,256]{1,0:T(8,128)(2,1)S(1)} %get-tuple-element.68), channel_id=1, source_target_pairs={{0,24},{8,16},{16,8},{24,0},{1,25},{9,17},{17,9},{25,1},{2,26},{10... | collective-permute-start | bytes 344072 | tf_op jit(solution)/shard_map/ppermute | solution.py:76
  62.1 9.8 %collective-permute-start.14 = (bf16[224,256]{1,0:T(8,128)(2,1)S(1)}, bf16[224,256]{1,0:T(8,128)(2,1)S(1)}, u32[]{:S(2)}, u32[]{:S(2)}) collective-permute-start(bf16[224,256]{1,0:T(8,128)(2,1)S(1)} %get-tuple-element.67), channel_id=1, source_target_pairs={{0,16},{8,24},{16,0},{24,8},{1,17},{9,25},{17,1},{25,9},{2,18},{10... | collective-permute-start | bytes 344072 | tf_op jit(solution)/shard_map/ppermute | solution.py:76
  64.5 7.3 %collective-permute-start.13 = (bf16[224,256]{1,0:T(8,128)(2,1)S(1)}, bf16[224,256]{1,0:T(8,128)(2,1)S(1)}, u32[]{:S(2)}, u32[]{:S(2)}) collective-permute-start(bf16[224,256]{1,0:T(8,128)(2,1)S(1)} %get-tuple-element.66), channel_id=1, source_target_pairs={{0,8},{8,0},{16,24},{24,16},{1,9},{9,1},{17,25},{25,17},{2,10},{10... | collective-permute-start | bytes 344072 | tf_op jit(solution)/shard_map/ppermute | solution.py:76
  71.9 7.5 %collective-permute-start.18 = (bf16[224,256]{1,0:T(8,128)(2,1)S(1)}, bf16[224,256]{1,0:T(8,128)(2,1)S(1)}, u32[]{:S(2)}, u32[]{:S(2)}) collective-permute-start(bf16[224,256]{1,0:T(8,128)(2,1)S(1)} %multiply_convert_fusion), channel_id=1, source_target_pairs={{0,24},{8,16},{16,8},{24,0},{1,25},{9,17},{17,9},{25,1},{2,26},{10... | collective-permute-start | bytes 344072 | tf_op jit(solution)/shard_map/ppermute | solution.py:76
  75.0 8.5 %collective-permute-start.17 = (bf16[224,256]{1,0:T(8,128)(2,1)S(1)}, bf16[224,256]{1,0:T(8,128)(2,1)S(1)}, u32[]{:S(2)}, u32[]{:S(2)}) collective-permute-start(bf16[224,256]{1,0:T(8,128)(2,1)S(1)} %multiply_convert_fusion), channel_id=1, source_target_pairs={{0,16},{8,24},{16,0},{24,8},{1,17},{9,25},{17,1},{25,9},{2,18},{10... | collective-permute-start | bytes 344072 | tf_op jit(solution)/shard_map/ppermute | solution.py:76
  75.0 8.5 %collective-permute-start.16 = (bf16[224,256]{1,0:T(8,128)(2,1)S(1)}, bf16[224,256]{1,0:T(8,128)(2,1)S(1)}, u32[]{:S(2)}, u32[]{:S(2)}) collective-permute-start(bf16[224,256]{1,0:T(8,128)(2,1)S(1)} %multiply_convert_fusion), channel_id=1, source_target_pairs={{0,8},{8,0},{16,24},{24,16},{1,9},{9,1},{17,25},{25,17},{2,10},{10... | collective-permute-start | bytes 344072 | tf_op jit(solution)/shard_map/ppermute | solution.py:76
  (6 other events, 9.5 us)

commit v7 on v6

--- a/solution.py
+++ b/solution.py
@@ -8,7 +8,7 @@
 from jax.sharding import PartitionSpec as P
 
 EPSILON = 1e-06
-FIRST_TAPS = 11
+FIRST_TAPS = 12
 AXES = ("ta", "ha", "wa")
 BF16 = jnp.bfloat16
 F32 = jnp.float32
@@ -121,7 +121,9 @@
 
 
 def columns_kernel(count, slot, where_ref, lefts, rights, *refs):
-    swapped, targets = refs[:count], refs[count + 1 :]
+    swapped, mine = refs[:count], refs[count]
+    kept, *targets = refs[count + 2 :]
+    kept[...] = mine[...]
     _, frames, height, channels = lefts.shape
     even_h, even_w = where_ref[0] == 0, where_ref[1] == 0
     width = swapped[0].shape[2]
@@ -173,8 +175,10 @@
         send[at + t * inner : at + (t + 1) * inner] = inside_send
 
 
-def bundle_kernel(chips, slot, counts, where_ref, later, *refs):
+def bundle_kernel(chips, slot, counts, where_ref, later, mine_own, *refs):
     cot_edges, act_edges, mine, send = refs[sum(counts) :]
+    skip = mine.shape[0] - send.shape[0]
+    mine[:skip] = mine_own[...].reshape(skip, mine.shape[1])
     core, even_w = where_ref[0], where_ref[1] == 0
     more, inner, channels = later.shape
     frames, around, _ = cot_edges.shape
@@ -196,12 +200,12 @@
         target[...] = jnp.concatenate(parts, axis=1).astype(BF16)
     for t in range(more):
         inside, inside_send = halves(core, later[t], chips)
-        mine[t * inner : (t + 1) * inner] = inside
+        mine[skip + t * inner : skip + (t + 1) * inner] = inside
         send[t * inner : (t + 1) * inner] = inside_send
     at = more * inner
     for t in range(frames):
         outside, outside_send = halves(core, cot_edges[t], chips)
-        mine[at + t * around : at + (t + 1) * around] = outside
+        mine[skip + at + t * around : skip + at + (t + 1) * around] = outside
         send[at + t * around : at + (t + 1) * around] = outside_send
 
 
@@ -225,7 +229,7 @@
 def taps_kernel(height, width, all_taps, *refs):
     inner = height * width
     places, act_a, *rest = refs
-    mine, mine_more, other, other_more, *outs, terms_ref, spread_a, spread_b = rest
+    mine, other, other_more, *outs, terms_ref, spread_a, spread_b = rest
     count = len(outs)
     channels, cells = act_a.shape
     frames = cells // inner
@@ -233,20 +237,23 @@
     spreads = (spread_a, spread_b)
     step = (height + 2) * width
     blocks = cells // part
-    more = 2 * inner
-    around = (mine_more.shape[0] - more) // (frames + 2)
+    around = mine.shape[0] // (frames + 2) - inner
     lowest = 2 - max(tap[0] for tap in all_taps)
     for side, spread in enumerate(spreads):
         for at in range(lowest, frames + 2 - min(tap[0] for tap in all_taps)):
-            extra = (mine_more, other_more)[side]
-            if at >= frames:
-                center = extra[(at - frames) * inner : (at - frames + 1) * inner]
-            elif side == 0:
-                center = mine[at]
+            if side == 0:
+                center = mine[at * inner : (at + 1) * inner]
+                start = (frames + 2) * inner + at * around
+                edges = mine[start : start + around]
             else:
                 start = blocks * channels + at * inner
-                center = other[start : start + inner]
-            edges = extra[more + at * around : more + (at + 1) * around]
+                center = (
+                    other[start : start + inner]
+                    if at < frames
+                    else other_more[(at - frames) * inner : (at - frames + 1) * inner]
+                )
+                start = 2 * inner + at * around
+                edges = other_more[start : start + around]
             spread_frame(center, edges, height, width, spread, (at - lowest) * step)
     acts = jnp.concatenate(
         [act_a[...]] + [other[b * channels : (b + 1) * channels] for b in range(blocks)], axis=1
@@ -423,27 +430,31 @@
     other = swap_core(send)
     rows = [swap_pairs(for_even, "ha", 0), swap_pairs(for_odd, "ha", 1)]
     rows = [array for array in rows if array is not None]
-    by_swap = call(
+    mine, *by_swap = call(
         functools.partial(columns_kernel, len(rows), slot),
-        (shape_of(2, (frames + 2) * height + 2 * slot, channels),) * min(2, cols_of - 1),
+        (shape_of(frames, inner, half),)
+        + (shape_of(2, (frames + 2) * height + 2 * slot, channels),) * min(2, cols_of - 1),
         0,
         size // 2,
         scalars=1,
-        arrays=2 + len(rows),
+        arrays=3 + len(rows),
         left=1,
-    )(where, lefts, rights, *rows, other)
+    )(where, lefts, rights, *rows, mine, other)
     columns = [swap_pairs(array, "wa", odd) for odd, array in enumerate(by_swap)]
     later = later.reshape(2, inner, channels)
-    cot_edges, act_edges, mine_more, send_more = call(
+    cot_edges, act_edges, mine, send_more = call(
         functools.partial(bundle_kernel, chips, slot, (len(rows), len(columns))),
         (shape_of(frames + 2, around, channels),) * 2
-        + (shape_of(2 * inner + (frames + 2) * around, half),) * 2,
+        + (
+            shape_of((frames + 2) * (inner + around), half),
+            shape_of(2 * inner + (frames + 2) * around, half),
+        ),
         0,
         size,
         scalars=1,
-        arrays=1 + len(rows) + len(columns),
+        arrays=2 + len(rows) + len(columns),
         limit=12,
-    )(where, later, *rows, *columns)
+    )(where, later, mine, *rows, *columns)
     other_more = swap_core(send_more)
 
     count = chips * cols_of
@@ -466,9 +477,9 @@
             4 * size,
             (pltpu.VMEM((len(taps), half, channels), F32), spread, spread),
             scalars=1,
-            arrays=5,
+            arrays=4,
             limit=16,
-        )(places, act_t, mine, mine_more, other, other_more)
+        )(places, act_t, mine, other, other_more)
         moved = [to_chip(piece, *move) for piece, move in zip(pieces[1:], moves[1:])]
         terms.append([pieces[0]] + moved)
         after = pieces[0]

time: 85 us -> 84.9 us (level)
  local copies, waits for them, and re-layouts: 4.51 us -> 3.55 us
    unnamed x22 -> x18, local copies, waits for them, and re-layouts: 4.44 us -> 3.48 us
where the time goes in v7:
time: 84.9 us; the launch traced here: 84.7 us
  starting transfers between devices  28.8 us (34%)
  waiting for transfers between devices  28.6 us (34%)
  Pallas kernels  21.5 us (25%)
  local copies, waits for them, and re-layouts  3.55 us (4%)
  other arithmetic  1.41 us (2%)
    ppermute x6, waiting for transfers between devices, to_partner(): lax.ppermute(array, axis, [(i, partner(i, by, length)) for i in range(len...  14.3 us
    ppermute x6, starting transfers between devices, to_partner(): lax.ppermute(array, axis, [(i, partner(i, by, length)) for i in range(len...  10.8 us
    ppermute x5, waiting for transfers between devices, swap_pairs(): return lax.ppermute(array, axis, pairs) if pairs else None  10 us
    ppermute x6, starting transfers between devices, to_chip(): return lax.ppermute(array, ('ha', 'wa'), pairs)  8.03 us
    ppermute x5, starting transfers between devices, swap_pairs(): return lax.ppermute(array, axis, pairs) if pairs else None  6.65 us
    pallas_call x2, Pallas kernels, body(): call(functools.partial(taps_kernel, height, width, taps), tuple((shape_of...  5.85 us
    pallas_call x1, Pallas kernels, body(): call(functools.partial(backward_kernel, height, width), flat, 27 * produc...  5.08 us
    pallas_call x1, Pallas kernels, body(): call(functools.partial(forward_kernel, height, width), flat, 27 * product...  4.66 us
  transfers between devices with their start and end apart: 19, of which 9 were waited for; matrix products, arithmetic and copies ran while one was open for 0% of the time, Pallas kernels for 15%

profile of v7, /device:TPU:0, one launch (start us, length us, event | category | flops | bytes accessed | tf_op | source)
XLA Modules:
  0.0 84.7 jit_solution(4175337599863334086)
XLA Ops:
  4.5 3.1 %collective-permute-start = (bf16[2,16,16,256]{3,2,1,0:T(8,128)(2,1)S(1)}, bf16[2,16,16,256]{3,2,1,0:T(8,128)(2,1)S(1)}, u32[]{:S(2)}, u32[]{:S(2)}) collective-permute-start(bf16[2,16,16,256]{3,2,1,0:T(8,128)(2,1)S(1)} %get-tuple-element.40), channel_id=1, source_target_pairs={{0,8},{8,0},{16,24},{24,16},{1,9},{9,1},{17,25},{25,17},{2,10},{10... | collective-permute-start | bytes 786440 | tf_op jit(solution)/shard_map/ppermute | solution.py:55
  8.3 5.6 %collective-permute-done.refs_0_ = bf16[2,16,16,256]{3,2,1,0:T(8,128)(2,1)S(1)} collective-permute-done((bf16[2,16,16,256]{3,2,1,0:T(8,128)(2,1)S(1)}, bf16[2,16,16,256]{3,2,1,0:T(8,128)(2,1)S(1)}, u32[]{:S(2)}, u32[]{:S(2)}) %collective-permute-start) | collective-permute-done | bytes 262176 | tf_op jit(solution)/shard_map/ppermute | solution.py:55
  17.7 1.3 %collective-permute-done.2.refs_0_ = bf16[2,6,16,256]{3,2,1,0:T(8,128)(2,1)S(1)} collective-permute-done((bf16[2,6,16,256]{3,2,1,0:T(8,128)(2,1)S(1)}, bf16[2,6,16,256]{3,2,1,0:T(8,128)(2,1)S(1)}, u32[]{:S(2)}, u32[]{:S(2)}) %collective-permute-start.2) | collective-permute-done | bytes 98336 | tf_op jit(solution)/shard_map/ppermute | solution.py:55
  19.6 1.7 %collective-permute-start.5 = (bf16[2,112,256]{2,1,0:T(8,128)(2,1)S(1)}, bf16[2,112,256]{2,1,0:T(8,128)(2,1)S(1)}, u32[]{:S(2)}, u32[]{:S(2)}) collective-permute-start(bf16[2,112,256]{2,1,0:T(8,128)(2,1)S(1)} %get-tuple-element.52), channel_id=1, source_target_pairs={{0,1},{1,0},{2,3},{3,2},{4,5},{5,4},{6,7},{7,6},{8,9},{9,8},{10,11... | collective-permute-start | bytes 344072 | tf_op jit(solution)/shard_map/ppermute | solution.py:55
  21.4 3.1 %collective-permute-done.5.refs_2_ = bf16[2,112,256]{2,1,0:T(8,128)(2,1)S(1)} collective-permute-done((bf16[2,112,256]{2,1,0:T(8,128)(2,1)S(1)}, bf16[2,112,256]{2,1,0:T(8,128)(2,1)S(1)}, u32[]{:S(2)}, u32[]{:S(2)}) %collective-permute-start.5) | collective-permute-done | bytes 114720 | tf_op jit(solution)/shard_map/ppermute | solution.py:55
  24.5 1.5 %shard_map.71 = (bf16[6,96,256]{2,1,0:T(8,128)(2,1)S(1)}, bf16[6,96,256]{2,1,0:T(8,128)(2,1)S(1)}, bf16[2112,128]{1,0:T(8,128)(2,1)S(1)}, bf16[1088,128]{1,0:T(8,128)(2,1)}) custom-call(s32[3]{0:T(128)S(1)} %pad_add_fusion.where_ref, bf16[2,256,256]{2,1,0:T(8,128)(2,1)S(1)} %bitcast.35, bf16[4,256,128]{2,1,0:T(8,128)(2,1)S(1)} %get-tuple-element.51.mine_own, ...), custom_call_target="tpu_custom_call" | custom-call | bytes 524288 | tf_op jit(solution)/shard_map/pallas_call | solution.py:445
  26.0 3.2 %collective-permute-start.6 = (bf16[1088,128]{1,0:T(8,128)(2,1)}, bf16[1088,128]{1,0:T(8,128)(2,1)S(1)}, u32[]{:S(2)}, u32[]{:S(2)}) collective-permute-start(bf16[1088,128]{1,0:T(8,128)(2,1)} %get-tuple-element.55), channel_id=1, source_target_pairs={{0,2},{2,0},{4,6},{6,4},{1,3},{3,1},{5,7},{7,5},{8,10},{10,8},{12,... | collective-permute-start | bytes 835592 | tf_op jit(solution)/shard_map/ppermute | solution.py:47
  29.4 1.2 %collective-permute-done.6.refs_4_ = bf16[1088,128]{1,0:T(8,128)(2,1)S(1)} collective-permute-done((bf16[1088,128]{1,0:T(8,128)(2,1)}, bf16[1088,128]{1,0:T(8,128)(2,1)S(1)}, u32[]{:S(2)}, u32[]{:S(2)}) %collective-permute-start.6) | collective-permute-done | bytes 278560 | tf_op jit(solution)/shard_map/ppermute | solution.py:47
  30.6 2.7 %shard_map.75 = (f32[12,32,256]{2,1,0:T(8,128)S(1)}, bf16[12,32,256]{2,1,0:T(8,128)(2,1)S(1)}, bf16[12,32,256]{2,1,0:T(8,128)(2,1)S(1)}, bf16[12,32,256]{2,1,0:T(8,128)(2,1)S(1)}) custom-call(s32[4]{0:T(128)S(1)} %pad_add_fusion.1.refs_0_, bf16[256,1024]{1,0:T(8,128)(2,1)S(1)} %get-tuple-element.48.act_t.refs_1_, ...), custom_call_target="tpu_custom_call" | custom-call | flops 1610612736 | bytes 2097152 | tf_op jit(solution)/shard_map/pallas_call | solution.py:470
  33.3 1.8 %collective-permute-start.7 = (bf16[12,32,256]{2,1,0:T(8,128)(2,1)S(1)}, bf16[12,32,256]{2,1,0:T(8,128)(2,1)S(1)}, u32[]{:S(2)}, u32[]{:S(2)}) collective-permute-start(bf16[12,32,256]{2,1,0:T(8,128)(2,1)S(1)} %get-tuple-element.61), channel_id=1, source_target_pairs={{0,1},{1,0},{2,3},{3,2},{4,5},{5,4},{6,7},{7,6},{8,9},{9,8},{10,11... | collective-permute-start | bytes 589832 | tf_op jit(solution)/shard_map/ppermute | solution.py:67
  35.1 2.6 %collective-permute-start.8 = (bf16[12,32,256]{2,1,0:T(8,128)(2,1)S(1)}, bf16[12,32,256]{2,1,0:T(8,128)(2,1)S(1)}, u32[]{:S(2)}, u32[]{:S(2)}) collective-permute-start(bf16[12,32,256]{2,1,0:T(8,128)(2,1)S(1)} %get-tuple-element.62), channel_id=1, source_target_pairs={{0,4},{1,5},{2,6},{3,7},{4,0},{5,1},{6,2},{7,3},{8,12},{9,13},{10,... | collective-permute-start | bytes 589832 | tf_op jit(solution)/shard_map/ppermute | solution.py:67
  37.8 3.2 %shard_map.72 = (f32[15,32,256]{2,1,0:T(8,128)S(1)}, bf16[15,32,256]{2,1,0:T(8,128)(2,1)S(1)}, bf16[15,32,256]{2,1,0:T(8,128)(2,1)S(1)}, bf16[15,32,256]{2,1,0:T(8,128)(2,1)S(1)}) custom-call(s32[4]{0:T(128)S(1)} %pad_add_fusion.1.refs_0_, bf16[256,1024]{1,0:T(8,128)(2,1)S(1)} %get-tuple-element.48.act_t.refs_1_, ...), custom_call_target="tpu_custom_call" | custom-call | flops 2013265920 | bytes 2097152 | tf_op jit(solution)/shard_map/pallas_call | solution.py:470
  41.0 1.5 %collective-permute-start.10 = (bf16[15,32,256]{2,1,0:T(8,128)(2,1)S(1)}, bf16[15,32,256]{2,1,0:T(8,128)(2,1)S(1)}, u32[]{:S(2)}, u32[]{:S(2)}) collective-permute-start(bf16[15,32,256]{2,1,0:T(8,128)(2,1)S(1)} %get-tuple-element.64), channel_id=1, source_target_pairs={{0,1},{1,0},{2,3},{3,2},{4,5},{5,4},{6,7},{7,6},{8,9},{9,8},{10,11... | collective-permute-start | bytes 737288 | tf_op jit(solution)/shard_map/ppermute | solution.py:67
  42.5 2.0 %collective-permute-start.11 = (bf16[15,32,256]{2,1,0:T(8,128)(2,1)S(1)}, bf16[15,32,256]{2,1,0:T(8,128)(2,1)S(1)}, u32[]{:S(2)}, u32[]{:S(2)}) collective-permute-start(bf16[15,32,256]{2,1,0:T(8,128)(2,1)S(1)} %get-tuple-element.65), channel_id=1, source_target_pairs={{0,4},{1,5},{2,6},{3,7},{4,0},{5,1},{6,2},{7,3},{8,12},{9,13},{10,... | collective-permute-start | bytes 737288 | tf_op jit(solution)/shard_map/ppermute | solution.py:67
  44.5 5.1 %shard_map.74 = (bf16[1024,256]{1,0:T(8,128)(2,1)}, f32[8,128]{1,0:T(8,128)S(1)}) custom-call(bf16[1024,256]{1,0:T(8,128)(2,1)S(1)} %bitcast.32, f32[1,256]{1,0:T(1,128)S(1)} %bitcast.38, bf16[4,256,256]{2,1,0:T(8,128)(2,1)S(1)} %bitcast.31, bf16[2,256,256]{2,1,0:T(8,128)(2,1)S(1)} %bitcast.36, bf16[6,96,256]{2,1,0:T(8,128)(2,1)S(1)} %get-tuple-element.58.edges, ...), custom_call_target="tpu_custom_call" | custom-call | flops 3623878656 | bytes 5636096 | tf_op jit(solution)/shard_map/pallas_call | solution.py:492
  49.7 4.7 %shard_map.73 = (bf16[1024,256]{1,0:T(8,128)(2,1)}, f32[8,128]{1,0:T(8,128)S(1)}) custom-call(bf16[1024,256]{1,0:T(8,128)(2,1)S(1)} %bitcast.33, bf16[2,256,256]{2,1,0:T(8,128)(2,1)S(1)} %bitcast.39, bf16[4,256,256]{2,1,0:T(8,128)(2,1)S(1)} %bitcast.34, bf16[6,96,256]{2,1,0:T(8,128)(2,1)S(1)} %get-tuple-element.53.edges, ...), custom_call_target="tpu_custom_call" | custom-call | flops 3623878656 | bytes 5636096 | tf_op jit(solution)/shard_map/pallas_call | solution.py:502
  54.3 3.0 %collective-permute-done.12.refs_7_ = bf16[15,32,256]{2,1,0:T(8,128)(2,1)S(1)} collective-permute-done((bf16[15,32,256]{2,1,0:T(8,128)(2,1)S(1)}, bf16[15,32,256]{2,1,0:T(8,128)(2,1)S(1)}, u32[]{:S(2)}, u32[]{:S(2)}) %collective-permute-start.12) | collective-permute-done | bytes 245792 | tf_op jit(solution)/shard_map/ppermute | solution.py:67
  58.2 3.7 %collective-permute-start.15 = (bf16[224,256]{1,0:T(8,128)(2,1)S(1)}, bf16[224,256]{1,0:T(8,128)(2,1)S(1)}, u32[]{:S(2)}, u32[]{:S(2)}) collective-permute-start(bf16[224,256]{1,0:T(8,128)(2,1)S(1)} %get-tuple-element.72), channel_id=1, source_target_pairs={{0,24},{8,16},{16,8},{24,0},{1,25},{9,17},{17,9},{25,1},{2,26},{10... | collective-permute-start | bytes 344072 | tf_op jit(solution)/shard_map/ppermute | solution.py:76
  61.9 2.5 %collective-permute-start.14 = (bf16[224,256]{1,0:T(8,128)(2,1)S(1)}, bf16[224,256]{1,0:T(8,128)(2,1)S(1)}, u32[]{:S(2)}, u32[]{:S(2)}) collective-permute-start(bf16[224,256]{1,0:T(8,128)(2,1)S(1)} %get-tuple-element.71), channel_id=1, source_target_pairs={{0,16},{8,24},{16,0},{24,8},{1,17},{9,25},{17,1},{25,9},{2,18},{10... | collective-permute-start | bytes 344072 | tf_op jit(solution)/shard_map/ppermute | solution.py:76
  65.4 6.4 %collective-permute-done.14 = bf16[224,256]{1,0:T(8,128)(2,1)S(1)} collective-permute-done((bf16[224,256]{1,0:T(8,128)(2,1)S(1)}, bf16[224,256]{1,0:T(8,128)(2,1)S(1)}, u32[]{:S(2)}, u32[]{:S(2)}) %collective-permute-start.14) | collective-permute-done | bytes 114720 | tf_op jit(solution)/shard_map/ppermute | solution.py:76
  71.9 3.1 %collective-permute-start.18 = (bf16[224,256]{1,0:T(8,128)(2,1)S(1)}, bf16[224,256]{1,0:T(8,128)(2,1)S(1)}, u32[]{:S(2)}, u32[]{:S(2)}) collective-permute-start(bf16[224,256]{1,0:T(8,128)(2,1)S(1)} %multiply_convert_fusion), channel_id=1, source_target_pairs={{0,24},{8,16},{16,8},{24,0},{1,25},{9,17},{17,9},{25,1},{2,26},{10... | collective-permute-start | bytes 344072 | tf_op jit(solution)/shard_map/ppermute | solution.py:76
  75.0 1.3 %collective-permute-start.16 = (bf16[224,256]{1,0:T(8,128)(2,1)S(1)}, bf16[224,256]{1,0:T(8,128)(2,1)S(1)}, u32[]{:S(2)}, u32[]{:S(2)}) collective-permute-start(bf16[224,256]{1,0:T(8,128)(2,1)S(1)} %multiply_convert_fusion), channel_id=1, source_target_pairs={{0,8},{8,0},{16,24},{24,16},{1,9},{9,1},{17,25},{25,17},{2,10},{10... | collective-permute-start | bytes 344072 | tf_op jit(solution)/shard_map/ppermute | solution.py:76
  76.3 3.0 %collective-permute-done.18 = bf16[224,256]{1,0:T(8,128)(2,1)S(1)} collective-permute-done((bf16[224,256]{1,0:T(8,128)(2,1)S(1)}, bf16[224,256]{1,0:T(8,128)(2,1)S(1)}, u32[]{:S(2)}, u32[]{:S(2)}) %collective-permute-start.18) | collective-permute-done | bytes 114720 | tf_op jit(solution)/shard_map/ppermute | solution.py:76
  79.3 4.2 %collective-permute-done.17 = bf16[224,256]{1,0:T(8,128)(2,1)S(1)} collective-permute-done((bf16[224,256]{1,0:T(8,128)(2,1)S(1)}, bf16[224,256]{1,0:T(8,128)(2,1)S(1)}, u32[]{:S(2)}, u32[]{:S(2)}) %collective-permute-start.17) | collective-permute-done | bytes 114720 | tf_op jit(solution)/shard_map/ppermute | solution.py:76
  (51 shorter events, 12.4 us)
Async XLA Ops:
  4.5 9.4 %collective-permute-start = (bf16[2,16,16,256]{3,2,1,0:T(8,128)(2,1)S(1)}, bf16[2,16,16,256]{3,2,1,0:T(8,128)(2,1)S(1)}, u32[]{:S(2)}, u32[]{:S(2)}) collective-permute-start(bf16[2,16,16,256]{3,2,1,0:T(8,128)(2,1)S(1)} %get-tuple-element.40), channel_id=1, source_target_pairs={{0,8},{8,0},{16,24},{24,16},{1,9},{9,1},{17,25},{25,17},{2,10},{10... | collective-permute-start | bytes 786440 | tf_op jit(solution)/shard_map/ppermute | solution.py:55
  7.6 6.3 %collective-permute-start.1 = (bf16[2,16,16,256]{3,2,1,0:T(8,128)(2,1)S(1)}, bf16[2,16,16,256]{3,2,1,0:T(8,128)(2,1)S(1)}, u32[]{:S(2)}, u32[]{:S(2)}) collective-permute-start(bf16[2,16,16,256]{3,2,1,0:T(8,128)(2,1)S(1)} %get-tuple-element.41), channel_id=1, source_target_pairs={{8,16},{16,8},{9,17},{17,9},{10,18},{18,10},{11,19},{19,11},{12,20... | collective-permute-start | bytes 786440 | tf_op jit(solution)/shard_map/ppermute | solution.py:55
  16.5 2.5 %collective-permute-start.4 = (bf16[3072,128]{1,0:T(8,128)(2,1)S(1)}, bf16[3072,128]{1,0:T(8,128)(2,1)S(1)}, u32[]{:S(2)}, u32[]{:S(2)}) collective-permute-start(bf16[3072,128]{1,0:T(8,128)(2,1)S(1)} %get-tuple-element.50), channel_id=1, source_target_pairs={{0,2},{2,0},{4,6},{6,4},{1,3},{3,1},{5,7},{7,5},{8,10},{10,8},{12,... | collective-permute-start | bytes 2359304 | tf_op jit(solution)/shard_map/ppermute | solution.py:47
  16.6 2.4 %collective-permute-start.2 = (bf16[2,6,16,256]{3,2,1,0:T(8,128)(2,1)S(1)}, bf16[2,6,16,256]{3,2,1,0:T(8,128)(2,1)S(1)}, u32[]{:S(2)}, u32[]{:S(2)}) collective-permute-start(bf16[2,6,16,256]{3,2,1,0:T(8,128)(2,1)S(1)} %get-tuple-element.46.after), channel_id=1, source_target_pairs={{0,2},{2,0},{4,6},{6,4},{1,3},{3,1},{5,7},{7,5},{8,10},{10,8},{12,... | collective-permute-start | bytes 294920 | tf_op jit(solution)/shard_map/ppermute | solution.py:55
  17.1 1.9 %collective-permute-start.3 = (bf16[2,6,16,256]{3,2,1,0:T(8,128)(2,1)S(1)}, bf16[2,6,16,256]{3,2,1,0:T(8,128)(2,1)S(1)}, u32[]{:S(2)}, u32[]{:S(2)}) collective-permute-start(bf16[2,6,16,256]{3,2,1,0:T(8,128)(2,1)S(1)} %get-tuple-element.47), channel_id=1, source_target_pairs={{2,4},{4,2},{3,5},{5,3},{10,12},{12,10},{11,13},{13,11},{18,20},{2... | collective-permute-start | bytes 294920 | tf_op jit(solution)/shard_map/ppermute | solution.py:55
  19.6 4.9 %collective-permute-start.5 = (bf16[2,112,256]{2,1,0:T(8,128)(2,1)S(1)}, bf16[2,112,256]{2,1,0:T(8,128)(2,1)S(1)}, u32[]{:S(2)}, u32[]{:S(2)}) collective-permute-start(bf16[2,112,256]{2,1,0:T(8,128)(2,1)S(1)} %get-tuple-element.52), channel_id=1, source_target_pairs={{0,1},{1,0},{2,3},{3,2},{4,5},{5,4},{6,7},{7,6},{8,9},{9,8},{10,11... | collective-permute-start | bytes 344072 | tf_op jit(solution)/shard_map/ppermute | solution.py:55
  26.0 4.6 %collective-permute-start.6 = (bf16[1088,128]{1,0:T(8,128)(2,1)}, bf16[1088,128]{1,0:T(8,128)(2,1)S(1)}, u32[]{:S(2)}, u32[]{:S(2)}) collective-permute-start(bf16[1088,128]{1,0:T(8,128)(2,1)} %get-tuple-element.55), channel_id=1, source_target_pairs={{0,2},{2,0},{4,6},{6,4},{1,3},{3,1},{5,7},{7,5},{8,10},{10,8},{12,... | collective-permute-start | bytes 835592 | tf_op jit(solution)/shard_map/ppermute | solution.py:47
  33.3 16.3 %collective-permute-start.7 = (bf16[12,32,256]{2,1,0:T(8,128)(2,1)S(1)}, bf16[12,32,256]{2,1,0:T(8,128)(2,1)S(1)}, u32[]{:S(2)}, u32[]{:S(2)}) collective-permute-start(bf16[12,32,256]{2,1,0:T(8,128)(2,1)S(1)} %get-tuple-element.61), channel_id=1, source_target_pairs={{0,1},{1,0},{2,3},{3,2},{4,5},{5,4},{6,7},{7,6},{8,9},{9,8},{10,11... | collective-permute-start | bytes 589832 | tf_op jit(solution)/shard_map/ppermute | solution.py:67
  35.1 19.3 %collective-permute-start.8 = (bf16[12,32,256]{2,1,0:T(8,128)(2,1)S(1)}, bf16[12,32,256]{2,1,0:T(8,128)(2,1)S(1)}, u32[]{:S(2)}, u32[]{:S(2)}) collective-permute-start(bf16[12,32,256]{2,1,0:T(8,128)(2,1)S(1)} %get-tuple-element.62), channel_id=1, source_target_pairs={{0,4},{1,5},{2,6},{3,7},{4,0},{5,1},{6,2},{7,3},{8,12},{9,13},{10,... | collective-permute-start | bytes 589832 | tf_op jit(solution)/shard_map/ppermute | solution.py:67
  37.7 6.8 %copy-start.1 = (bf16[4,16,16,256]{3,2,1,0:T(8,128)(2,1)S(1)}, bf16[4,16,16,256]{3,2,1,0:T(8,128)(2,1)}, u32[]{:S(2)}) copy-start(bf16[4,16,16,256]{3,2,1,0:T(8,128)(2,1)} %cot_ref.1) | copy-start | bytes 1572868
  37.7 6.8 %copy-start.3 = (bf16[4,16,16,256]{3,2,1,0:T(8,128)(2,1)S(1)}, bf16[4,16,16,256]{3,2,1,0:T(8,128)(2,1)}, u32[]{:S(2)}) copy-start(bf16[4,16,16,256]{3,2,1,0:T(8,128)(2,1)} %x_ref.1) | copy-start | bytes 1572868
  37.7 6.8 %copy-start.5 = (f32[256]{0:T(256)S(1)}, f32[256]{0:T(256)}, u32[]{:S(2)}) copy-start(f32[256]{0:T(256)} %param.5) | copy-start | bytes 3076
  37.7 6.8 %copy-start.6 = (bf16[3,3,3,256,256]{4,3,2,1,0:T(8,128)(2,1)S(1)}, bf16[3,3,3,256,256]{4,3,2,1,0:T(8,128)(2,1)}, u32[]{:S(2)}) copy-start(bf16[3,3,3,256,256]{4,3,2,1,0:T(8,128)(2,1)} %weight.3) | copy-start | bytes 10616836
  37.7 16.6 %collective-permute-start.9 = (bf16[12,32,256]{2,1,0:T(8,128)(2,1)S(1)}, bf16[12,32,256]{2,1,0:T(8,128)(2,1)S(1)}, u32[]{:S(2)}, u32[]{:S(2)}) collective-permute-start(bf16[12,32,256]{2,1,0:T(8,128)(2,1)S(1)} %get-tuple-element.63), channel_id=1, source_target_pairs={{0,5},{1,4},{2,7},{3,6},{4,1},{5,0},{6,3},{7,2},{8,13},{9,12},{10,... | collective-permute-start | bytes 589832 | tf_op jit(solution)/shard_map/ppermute | solution.py:67
  41.0 13.3 %collective-permute-start.10 = (bf16[15,32,256]{2,1,0:T(8,128)(2,1)S(1)}, bf16[15,32,256]{2,1,0:T(8,128)(2,1)S(1)}, u32[]{:S(2)}, u32[]{:S(2)}) collective-permute-start(bf16[15,32,256]{2,1,0:T(8,128)(2,1)S(1)} %get-tuple-element.64), channel_id=1, source_target_pairs={{0,1},{1,0},{2,3},{3,2},{4,5},{5,4},{6,7},{7,6},{8,9},{9,8},{10,11... | collective-permute-start | bytes 737288 | tf_op jit(solution)/shard_map/ppermute | solution.py:67
  42.5 11.8 %collective-permute-start.11 = (bf16[15,32,256]{2,1,0:T(8,128)(2,1)S(1)}, bf16[15,32,256]{2,1,0:T(8,128)(2,1)S(1)}, u32[]{:S(2)}, u32[]{:S(2)}) collective-permute-start(bf16[15,32,256]{2,1,0:T(8,128)(2,1)S(1)} %get-tuple-element.65), channel_id=1, source_target_pairs={{0,4},{1,5},{2,6},{3,7},{4,0},{5,1},{6,2},{7,3},{8,12},{9,13},{10,... | collective-permute-start | bytes 737288 | tf_op jit(solution)/shard_map/ppermute | solution.py:67
  44.5 5.1 %copy-start.8 = (bf16[2,16,16,256]{3,2,1,0:T(8,128)(2,1)S(1)}, bf16[2,16,16,256]{3,2,1,0:T(8,128)(2,1)}, u32[]{:S(2)}) copy-start(bf16[2,16,16,256]{3,2,1,0:T(8,128)(2,1)} %copy-done.7) | copy-start | bytes 786436
  49.6 7.7 %collective-permute-start.12 = (bf16[15,32,256]{2,1,0:T(8,128)(2,1)S(1)}, bf16[15,32,256]{2,1,0:T(8,128)(2,1)S(1)}, u32[]{:S(2)}, u32[]{:S(2)}) collective-permute-start(bf16[15,32,256]{2,1,0:T(8,128)(2,1)S(1)} %get-tuple-element.66), channel_id=1, source_target_pairs={{0,5},{1,4},{2,7},{3,6},{4,1},{5,0},{6,3},{7,2},{8,13},{9,12},{10,... | collective-permute-start | bytes 737288 | tf_op jit(solution)/shard_map/ppermute | solution.py:67
  58.2 7.2 %collective-permute-start.15 = (bf16[224,256]{1,0:T(8,128)(2,1)S(1)}, bf16[224,256]{1,0:T(8,128)(2,1)S(1)}, u32[]{:S(2)}, u32[]{:S(2)}) collective-permute-start(bf16[224,256]{1,0:T(8,128)(2,1)S(1)} %get-tuple-element.72), channel_id=1, source_target_pairs={{0,24},{8,16},{16,8},{24,0},{1,25},{9,17},{17,9},{25,1},{2,26},{10... | collective-permute-start | bytes 344072 | tf_op jit(solution)/shard_map/ppermute | solution.py:76
  61.9 9.9 %collective-permute-start.14 = (bf16[224,256]{1,0:T(8,128)(2,1)S(1)}, bf16[224,256]{1,0:T(8,128)(2,1)S(1)}, u32[]{:S(2)}, u32[]{:S(2)}) collective-permute-start(bf16[224,256]{1,0:T(8,128)(2,1)S(1)} %get-tuple-element.71), channel_id=1, source_target_pairs={{0,16},{8,24},{16,0},{24,8},{1,17},{9,25},{17,1},{25,9},{2,18},{10... | collective-permute-start | bytes 344072 | tf_op jit(solution)/shard_map/ppermute | solution.py:76
  64.3 7.5 %collective-permute-start.13 = (bf16[224,256]{1,0:T(8,128)(2,1)S(1)}, bf16[224,256]{1,0:T(8,128)(2,1)S(1)}, u32[]{:S(2)}, u32[]{:S(2)}) collective-permute-start(bf16[224,256]{1,0:T(8,128)(2,1)S(1)} %get-tuple-element.70), channel_id=1, source_target_pairs={{0,8},{8,0},{16,24},{24,16},{1,9},{9,1},{17,25},{25,17},{2,10},{10... | collective-permute-start | bytes 344072 | tf_op jit(solution)/shard_map/ppermute | solution.py:76
  71.9 7.4 %collective-permute-start.18 = (bf16[224,256]{1,0:T(8,128)(2,1)S(1)}, bf16[224,256]{1,0:T(8,128)(2,1)S(1)}, u32[]{:S(2)}, u32[]{:S(2)}) collective-permute-start(bf16[224,256]{1,0:T(8,128)(2,1)S(1)} %multiply_convert_fusion), channel_id=1, source_target_pairs={{0,24},{8,16},{16,8},{24,0},{1,25},{9,17},{17,9},{25,1},{2,26},{10... | collective-permute-start | bytes 344072 | tf_op jit(solution)/shard_map/ppermute | solution.py:76
  75.0 8.5 %collective-permute-start.17 = (bf16[224,256]{1,0:T(8,128)(2,1)S(1)}, bf16[224,256]{1,0:T(8,128)(2,1)S(1)}, u32[]{:S(2)}, u32[]{:S(2)}) collective-permute-start(bf16[224,256]{1,0:T(8,128)(2,1)S(1)} %multiply_convert_fusion), channel_id=1, source_target_pairs={{0,16},{8,24},{16,0},{24,8},{1,17},{9,25},{17,1},{25,9},{2,18},{10... | collective-permute-start | bytes 344072 | tf_op jit(solution)/shard_map/ppermute | solution.py:76
  75.0 8.5 %collective-permute-start.16 = (bf16[224,256]{1,0:T(8,128)(2,1)S(1)}, bf16[224,256]{1,0:T(8,128)(2,1)S(1)}, u32[]{:S(2)}, u32[]{:S(2)}) collective-permute-start(bf16[224,256]{1,0:T(8,128)(2,1)S(1)} %multiply_convert_fusion), channel_id=1, source_target_pairs={{0,8},{8,0},{16,24},{24,16},{1,9},{9,1},{17,25},{25,17},{2,10},{10... | collective-permute-start | bytes 344072 | tf_op jit(solution)/shard_map/ppermute | solution.py:76
  (4 other events, 3.5 us)
